TPU v7x, 32 devices: a whole 2x2x4 slice. The times are simulated.
32 devices in a mesh: dp: 4 (over y, core), seq: 4 (over z), mp: 2 (over x).
Axes of the slice: x: 2, y: 2, z: 4, core: 2. Of those that a mesh axis runs over, the one named last changes fastest.
Arguments:
- tokens: bfloat16 [8192, 2048], P(('dp', 'seq')), may hold values from -6 to 6
- doc_lengths: int32 [4, 4], P('dp'), may hold values from 1 to 2048, as said below
- norm_gain: float32 [2048], replicated, may hold values from 0.1 to 1.9
- w_y: bfloat16 [2048, 2560], P(('dp', 'seq'), 'mp'), may hold values from -0.125 to 0.125
- w_x: bfloat16 [2048, 2560], P(('dp', 'seq'), 'mp'), may hold values from -0.125 to 0.125
- gate_a: bfloat16 [10, 256, 256], P('mp'), may hold values from -0.375 to 0.375
- gate_i: bfloat16 [10, 256, 256], P('mp'), may hold values from -0.375 to 0.375
- bias_a: float32 [2560], P('mp'), may hold values from -4 to 4
- bias_i: float32 [2560], P('mp'), may hold values from -4 to 4
- conv_w: float32 [4, 2560], P(None, 'mp'), may hold values from -3 to 3
- conv_b: float32 [2560], P('mp'), may hold values from -3 to 3
- decay_param: float32 [2560], P('mp'), may hold values from 3 to 13
- w_out: bfloat16 [2048, 2560], P(('dp', 'seq'), 'mp'), may hold values from -0.25 to 0.25
- mlp_gain: float32 [2048], replicated, may hold values from 0.1 to 1.9
- w_gate: bfloat16 [2048, 6144], P(('dp', 'seq'), 'mp'), may hold values from -0.125 to 0.125
- w_up: bfloat16 [2048, 6144], P(('dp', 'seq'), 'mp'), may hold values from -0.125 to 0.125
- w_down: bfloat16 [2048, 6144], P(('dp', 'seq'), 'mp'), may hold values from -0.15625 to 0.15625
- cotangent: bfloat16 [8192, 2048], P(('dp', 'seq')), may hold values from -6 to 6
Outputs:
- output: bfloat16 [8192, 2048], P(('dp', 'seq'))
- input_grad: float32 [8192, 2048], P(('dp', 'seq'))
- grad_norm_gain: float32 [2048], replicated
- grad_w_y: float32 [2048, 2560], P(('dp', 'seq'), 'mp')
- grad_w_x: float32 [2048, 2560], P(('dp', 'seq'), 'mp')
- grad_gate_a: float32 [10, 256, 256], P('mp')
- grad_gate_i: float32 [10, 256, 256], P('mp')
- grad_bias_a: float32 [2560], P('mp')
- grad_bias_i: float32 [2560], P('mp')
- grad_conv_w: float32 [4, 2560], P(None, 'mp')
- grad_conv_b: float32 [2560], P('mp')
- grad_decay_param: float32 [2560], P('mp')
- grad_w_out: float32 [2048, 2560], P(('dp', 'seq'), 'mp')
- grad_mlp_gain: float32 [2048], replicated
- grad_w_gate: float32 [2048, 6144], P(('dp', 'seq'), 'mp')
- grad_w_up: float32 [2048, 6144], P(('dp', 'seq'), 'mp')
- grad_w_down: float32 [2048, 6144], P(('dp', 'seq'), 'mp')
Inputs may be any that keep to these rules, and one draw needn't show every extreme that they name: `doc_lengths`: each row gives, in order, the lengths of the 4 documents packed into one sequence, and sums to 2048.
All inputs are finite; a program needn't handle non-finite values.
Results may differ from a plain program's by a relative error of at most 0.0088.
Values may be sent and summed in bfloat16 or wider, within the bound.
A program may use at most 384 MiB of HBM per device.

v0:
```python
import jax
import jax.numpy as jnp
from jax import lax
from jax.sharding import PartitionSpec as P

epsilon = 1e-06
decay_scale = 8.0


def from_behind(value, axis, steps):
    count = lax.axis_size(axis)
    initial, last = (max(0, -steps), min(count, count - steps))
    return lax.ppermute(value, axis, [(source, source + steps) for source in range(initial, last)])


def entering(value, axis, join, neutral, backward):
    count, mine = (lax.axis_size(axis), lax.axis_index(axis))
    pieces = jax.tree.map(lambda part: lax.all_gather(part, axis), value)
    if backward:
        pieces = jax.tree.map(lambda part: part[::-1], pieces)
        mine = count - 1 - mine
    total = jax.tree.map(
        lambda part, zero: jnp.full_like(part, 0) + jnp.asarray(zero, part.dtype), value, neutral
    )

    def turn(position, total):
        longer = join(total, jax.tree.map(lambda part: part[position], pieces))
        return jax.tree.map(lambda new, old: jnp.where(position < mine, new, old), longer, total)

    return lax.fori_loop(0, count - 1, turn, total)


def contract(left, right):
    return lax.dot_general(
        left, right, (((1,), (1,)), ((), ())), preferred_element_type=jnp.float32
    )


def contract_rows(left, right):
    return lax.dot_general(
        left, right, (((0,), (0,)), ((), ())), preferred_element_type=jnp.float32
    )


def normalize(values, gain):
    scale = lax.rsqrt(jnp.mean(values * values, axis=-1, keepdims=True) + epsilon)
    normed = values * scale
    return (normed, scale, (normed * gain).astype(jnp.bfloat16))


def norm_back(grad_out, normed, scale, gain):
    grad_normed = grad_out * gain
    grad_in = scale * (
        grad_normed - normed * jnp.mean(grad_normed * normed, axis=-1, keepdims=True)
    )
    return (grad_in, jnp.sum(grad_out * normed, axis=0))


def compose(first_part, second_part):
    return (first_part[0] * second_part[0], second_part[0] * first_part[1] + second_part[1])


def gate_decay(gate_r, gate_x, conv_out, decay_param, bias_a, bias_i, keep_state):
    rate = jax.nn.sigmoid(gate_r + bias_a)
    input_gate = jax.nn.sigmoid(gate_x + bias_i)
    log_decay = -decay_scale * rate * jax.nn.softplus(-decay_param)
    decays = jnp.exp(log_decay) * keep_state
    drives = conv_out * input_gate * jnp.sqrt(-jnp.expm1(2.0 * log_decay))
    return (decays, drives)


def project_pair(activations, first, second):
    return (
        jnp.dot(
            activations,
            lax.all_gather(first, ("dp", "seq"), axis=0, tiled=True),
            preferred_element_type=jnp.float32,
        ),
        jnp.dot(
            activations,
            lax.all_gather(second, ("dp", "seq"), axis=0, tiled=True),
            preferred_element_type=jnp.float32,
        ),
    )


def mp_total(partial_value):
    return lax.psum(partial_value, "mp")


def branch_out(mixed, weight):
    return mp_total(contract(mixed, lax.all_gather(weight, ("dp", "seq"), axis=0, tiled=True)))


def back_rows(grad_low, weight):
    return jnp.dot(
        grad_low,
        lax.all_gather(weight, ("dp", "seq"), axis=0, tiled=True),
        preferred_element_type=jnp.float32,
    )


def back_pair(first_grad, second_grad, first, second):
    return contract(
        first_grad, lax.all_gather(first, ("dp", "seq"), axis=0, tiled=True)
    ) + contract(second_grad, lax.all_gather(second, ("dp", "seq"), axis=0, tiled=True))


def mp_grads(part, gain_part):
    return lax.psum((part, gain_part), "mp")


def row_terms(pairs):
    return jnp.concatenate([contract_rows(left, right) for left, right in pairs], axis=1)


def reduce_rows(pairs):
    return lax.psum_scatter(row_terms(pairs), ("dp", "seq"), scatter_dimension=0, tiled=True)


def split_columns(whole, widths):
    pieces = []
    offset = 0
    for width_one in widths:
        pieces.append(whole[:, offset : offset + width_one])
        offset = offset + width_one
    return pieces


def on_device(
    tokens,
    doc_lengths,
    norm_gain,
    w_y,
    w_x,
    gate_a,
    gate_i,
    bias_a,
    bias_i,
    conv_w,
    conv_b,
    decay_param,
    w_out,
    mlp_gain,
    w_gate,
    w_up,
    w_down,
    cotangent,
):
    local_len = tokens.shape[0]
    conv_taps = conv_w.shape[0]
    heads_here = gate_a.shape[0]
    block_size = gate_a.shape[1]
    width_here = w_y.shape[1]
    hidden_here = w_gate.shape[1]
    position = lax.axis_index("seq") * local_len + jnp.arange(local_len, dtype=jnp.int32)
    lengths_row = doc_lengths[0]
    starts = jnp.cumsum(lengths_row) - lengths_row
    resets = jnp.any(position[:, None] == starts[None, :], axis=1)
    doc_start = jnp.max(jnp.where(starts[None, :] <= position[:, None], starts[None, :], 0), axis=1)
    keep_state = 1.0 - resets.astype(jnp.float32)[:, None]
    same_doc = [
        (position - offset >= doc_start).astype(jnp.float32)[:, None] for offset in range(conv_taps)
    ]
    resid = tokens.astype(jnp.float32)
    normed_one, scale_one, activations_one = normalize(resid, norm_gain)
    pre_y, pre_x = project_pair(activations_one, w_y, w_x)
    conv_in = pre_x.astype(jnp.bfloat16)
    prev_tail = from_behind(conv_in[local_len - conv_taps + 1 :], "seq", 1)
    extended = jnp.concatenate([prev_tail, conv_in], axis=0).astype(jnp.float32)
    windows = [
        lax.slice_in_dim(
            extended, conv_taps - 1 - offset, conv_taps - 1 - offset + local_len, axis=0
        )
        for offset in range(conv_taps)
    ]
    conv_out = conv_b
    for offset in range(conv_taps):
        conv_out = conv_out + conv_w[offset] * windows[offset] * same_doc[offset]
    conv_low = conv_out.astype(jnp.bfloat16).reshape(local_len, heads_here, block_size)
    gate_r = jnp.einsum(
        "thi,hij->thj", conv_low, gate_a, preferred_element_type=jnp.float32
    ).reshape(local_len, width_here)
    gate_x = jnp.einsum(
        "thi,hij->thj", conv_low, gate_i, preferred_element_type=jnp.float32
    ).reshape(local_len, width_here)
    decays, drives = gate_decay(gate_r, gate_x, conv_out, decay_param, bias_a, bias_i, keep_state)
    prefix_decay, local_state = lax.associative_scan(compose, (decays, drives))
    end_decay = prefix_decay[-1]
    end_state = local_state[-1]
    _, state_in = entering(
        (end_decay, end_state),
        "seq",
        compose,
        (jnp.ones_like(end_decay), jnp.zeros_like(end_state)),
        False,
    )
    states = local_state + prefix_decay * state_in
    gelu_y = jax.nn.gelu(pre_y)
    mixed_rec = (states * gelu_y).astype(jnp.bfloat16)
    rec_branch = branch_out(mixed_rec, w_out)
    middle = resid + rec_branch
    normed_two, scale_two, activations_two = normalize(middle, mlp_gain)
    pre_gate, pre_up = project_pair(activations_two, w_gate, w_up)
    mixed_mlp = (jax.nn.gelu(pre_gate) * pre_up).astype(jnp.bfloat16)
    final = middle + branch_out(mixed_mlp, w_down)
    output = final.astype(jnp.bfloat16)
    grad_final = cotangent.astype(jnp.float32)
    grad_mixed_mlp = back_rows(cotangent, w_down)
    _, gate_pull = jax.vjp(lambda gate_in, up_in: jax.nn.gelu(gate_in) * up_in, pre_gate, pre_up)
    grad_gate, grad_up = gate_pull(grad_mixed_mlp)
    grad_gate_low = grad_gate.astype(jnp.bfloat16)
    grad_up_low = grad_up.astype(jnp.bfloat16)
    grad_acts_two = back_pair(grad_gate_low, grad_up_low, w_gate, w_up)
    part_two, gain_two = norm_back(grad_acts_two, normed_two, scale_two, mlp_gain)
    sum_two, gain_two_total = mp_grads(part_two, gain_two)
    grad_middle = grad_final + sum_two
    mlp_pairs = (
        (activations_two, grad_gate_low),
        (activations_two, grad_up_low),
        (cotangent, mixed_mlp),
    )
    mlp_sums = reduce_rows(mlp_pairs)
    grad_middle_low = grad_middle.astype(jnp.bfloat16)
    grad_mixed_rec = back_rows(grad_middle_low, w_out)
    grad_state = grad_mixed_rec * gelu_y
    _, gelu_pull = jax.vjp(jax.nn.gelu, pre_y)
    grad_pre_y_low = gelu_pull(grad_mixed_rec * states)[0].astype(jnp.bfloat16)
    next_decay = jnp.concatenate([decays[1:], jnp.ones_like(decays[:1])], axis=0)
    suffix_decay, local_grad = lax.associative_scan(compose, (next_decay, grad_state), reverse=True)
    head_decay = decays[0] * suffix_decay[0]
    head_grad = decays[0] * local_grad[0]
    _, grad_in = entering(
        (head_decay, head_grad),
        "seq",
        compose,
        (jnp.ones_like(head_decay), jnp.zeros_like(head_grad)),
        True,
    )
    carry_grad = local_grad + suffix_decay * grad_in
    state_before = jnp.concatenate([state_in[None, :], states[:-1]], axis=0)

    def local_gates(gate_r_in, gate_x_in, conv_in_values, decay_in, bias_r_in, bias_x_in):
        return gate_decay(
            gate_r_in, gate_x_in, conv_in_values, decay_in, bias_r_in, bias_x_in, keep_state
        )

    _, decay_pull = jax.vjp(local_gates, gate_r, gate_x, conv_out, decay_param, bias_a, bias_i)
    grad_r, grad_x_gate, grad_conv_direct, grad_decay_param, grad_bias_a, grad_bias_i = decay_pull(
        (carry_grad * state_before, carry_grad)
    )
    grad_r_low = grad_r.astype(jnp.bfloat16).reshape(local_len, heads_here, block_size)
    grad_x_low = grad_x_gate.astype(jnp.bfloat16).reshape(local_len, heads_here, block_size)
    grad_gates_in = jnp.einsum(
        "thj,hij->thi", grad_r_low, gate_a, preferred_element_type=jnp.float32
    ) + jnp.einsum("thj,hij->thi", grad_x_low, gate_i, preferred_element_type=jnp.float32)
    grad_conv = grad_conv_direct + grad_gates_in.reshape(local_len, width_here)
    grad_gate_a = jnp.einsum(
        "thi,thj->hij", conv_low, grad_r_low, preferred_element_type=jnp.float32
    )
    grad_gate_i = jnp.einsum(
        "thi,thj->hij", conv_low, grad_x_low, preferred_element_type=jnp.float32
    )
    grad_ext = jnp.zeros((local_len + conv_taps - 1, width_here), jnp.float32)
    for offset in range(conv_taps):
        grad_ext = grad_ext + jnp.pad(
            conv_w[offset] * same_doc[offset] * grad_conv,
            ((conv_taps - 1 - offset, offset), (0, 0)),
        )
    from_next = from_behind(grad_ext[: conv_taps - 1], "seq", -1)
    grad_conv_in = grad_ext[conv_taps - 1 :] + jnp.pad(
        from_next, ((local_len - conv_taps + 1, 0), (0, 0))
    )
    grad_pre_x_low = grad_conv_in.astype(jnp.bfloat16)
    grad_conv_w = jnp.stack(
        [
            jnp.sum(grad_conv * same_doc[offset] * windows[offset], axis=0)
            for offset in range(conv_taps)
        ]
    )
    grad_conv_b = jnp.sum(grad_conv, axis=0)
    grad_acts_one = back_pair(grad_pre_y_low, grad_pre_x_low, w_y, w_x)
    part_one, gain_one = norm_back(grad_acts_one, normed_one, scale_one, norm_gain)
    sum_one, gain_one_total = mp_grads(part_one, gain_one)
    input_grad = grad_middle + sum_one
    rec_pairs = (
        (activations_one, grad_pre_y_low),
        (activations_one, grad_pre_x_low),
        (grad_middle_low, mixed_rec),
    )
    rec_sums = reduce_rows(rec_pairs)
    grad_w_y, grad_w_x, grad_w_out = split_columns(rec_sums, [width_here, width_here, width_here])
    grad_w_gate, grad_w_up, grad_w_down = split_columns(
        mlp_sums, [hidden_here, hidden_here, hidden_here]
    )
    totals = lax.psum(
        (
            grad_gate_a,
            grad_gate_i,
            grad_bias_a,
            grad_bias_i,
            grad_conv_w,
            grad_conv_b,
            grad_decay_param,
            gain_one_total,
            gain_two_total,
        ),
        ("dp", "seq"),
    )
    return (
        output,
        input_grad,
        totals[7],
        grad_w_y,
        grad_w_x,
        totals[0],
        totals[1],
        totals[2],
        totals[3],
        totals[4],
        totals[5],
        totals[6],
        grad_w_out,
        totals[8],
        grad_w_gate,
        grad_w_up,
        grad_w_down,
    )


def solution(mesh):
    return jax.shard_map(
        on_device,
        mesh=mesh,
        in_specs=(
            P(("dp", "seq"), None),
            P("dp", None),
            P(),
            P(("dp", "seq"), "mp"),
            P(("dp", "seq"), "mp"),
            P("mp", None, None),
            P("mp", None, None),
            P("mp"),
            P("mp"),
            P(None, "mp"),
            P("mp"),
            P("mp"),
            P(("dp", "seq"), "mp"),
            P(),
            P(("dp", "seq"), "mp"),
            P(("dp", "seq"), "mp"),
            P(("dp", "seq"), "mp"),
            P(("dp", "seq"), None),
        ),
        out_specs=(
            P(("dp", "seq"), None),
            P(("dp", "seq"), None),
            P(),
            P(("dp", "seq"), "mp"),
            P(("dp", "seq"), "mp"),
            P("mp", None, None),
            P("mp", None, None),
            P("mp"),
            P("mp"),
            P(None, "mp"),
            P("mp"),
            P("mp"),
            P(("dp", "seq"), "mp"),
            P(),
            P(("dp", "seq"), "mp"),
            P(("dp", "seq"), "mp"),
            P(("dp", "seq"), "mp"),
        ),
        check_vma=False,
    )
```

profile of v0, /device:TPU:0, one launch (start us, length us, event | category | flops | bytes accessed | tf_op | source)
XLA Modules:
  0.0 2732.0 jit_solution(12211440450678808521)
XLA Ops:
  14.0 55.1 %all-gather.11.cloned.1.call-done = bf16[2048,1280]{1,0:T(8,128)(2,1)} async-done(((bf16[128,1280]{1,0:T(8,128)(2,1)}), bf16[2048,1280]{1,0:T(8,128)(2,1)}) %all-gather.11.cloned.1.call-update) | async-done | bytes 5242896 | tf_op jit(solution)/shard_map/all_gather | solution.py:81
  381.2 13.5 all-gather
  407.1 13.1 all-gather.1
  420.5 12.5 multiply_convert_fusion.3
  442.8 104.6 %all-reduce.88.cloned.1.call-done = f32[512,2048]{1,0:T(8,128)} async-done(((f32[512,2048]{1,0:T(8,128)}), f32[512,2048]{1,0:T(8,128)}) %all-reduce.88.cloned.1.call-update) | async-done | bytes 4194320 | tf_op jit(solution)/shard_map/psum | solution.py:88
  554.6 96.0 %all-gather.19.cloned.1.call-done = bf16[2048,3072]{1,0:T(8,128)(2,1)} async-done(((bf16[128,3072]{1,0:T(8,128)(2,1)}), bf16[2048,3072]{1,0:T(8,128)(2,1)}) %all-gather.19.cloned.1.call-update) | async-done | bytes 12582928 | tf_op jit(solution)/shard_map/all_gather | solution.py:81
  662.7 89.3 %all-gather.17.cloned.1.call-done = bf16[2048,3072]{1,0:T(8,128)(2,1)} async-done(((bf16[128,3072]{1,0:T(8,128)(2,1)}), bf16[2048,3072]{1,0:T(8,128)(2,1)}) %all-gather.17.cloned.1.call-update) | async-done | bytes 12582928 | tf_op jit(solution)/shard_map/all_gather | solution.py:76
  764.0 89.6 %all-gather.21.cloned.1.call-done = bf16[2048,3072]{1,0:T(8,128)(2,1)} async-done(((bf16[128,3072]{1,0:T(8,128)(2,1)}), bf16[2048,3072]{1,0:T(8,128)(2,1)}) %all-gather.21.cloned.1.call-update) | async-done | bytes 12582928 | tf_op jit(solution)/shard_map/all_gather | solution.py:92
  853.5 18.6 multiply_convert_fusion
  872.2 12.2 fusion.110
  884.4 16.6 multiply_reduce_fusion
  963.7 12.8 fusion.109
  976.5 36.9 %all-reduce.90.cloned.1.call-done = f32[512,2048]{1,0:T(8,128)} async-done(((f32[512,2048]{1,0:T(8,128)}), f32[512,2048]{1,0:T(8,128)}) %all-reduce.90.cloned.1.call-update) | async-done | bytes 4194320 | tf_op jit(solution)/shard_map/psum | solution.py:110
  1296.6 13.1 rev.14
  1309.7 21.0 rev.15
  1330.7 13.2 all-gather.3
  1344.1 13.2 all-gather.2
  1429.7 22.0 pad_maximum_fusion.1
  1453.3 14.3 convolution_bitcast_fusion
  1491.3 50.8 %pad_maximum_fusion = f32[2048,9216]{1,0:T(8,128)} fusion(f32[2048,3072]{1,0:T(8,128)} %convolution_bitcast_fusion, f32[2048,3072]{1,0:T(8,128)} %fusion.115, f32[2048,3072]{1,0:T(8,128)} %fusion.114), kind=kLoop, calls=%fused_computation.6 | loop fusion | flops 37748736 | bytes 150994944 | tf_op jit(solution)/shard_map/concatenate | solution.py:114
  1555.6 63.3 %all-reduce.79 = (f32[2048]{0:T(1024)}, f32[1280]{0:T(1024)}, f32[1280]{0:T(1024)}, f32[4,1280]{1,0:T(4,128)}, f32[1280]{0:T(1024)}, /*index=5*/f32[1280]{0:T(1024)}, f32[2048]{0:T(1024)}) all-reduce(f32[2048]{0:T(1024)S(1)} %get-tuple-element.355, f32[1280]{0:T(1024)S(1)} %copy-done.75, ...), channel_id=1, replica_groups=mesh['dp'=4,'seq'=4,'mp'=2] {'dp','seq'}, use_global_device_ids=true, to_apply=%region_17.18 | all-reduce | flops 14336 | bytes 114688 | tf_op jit(solution)/shard_map/psum | solution.py:296
  1634.7 274.5 %reduce-scatter.3.cloned.1.call-done = f32[128,3840]{0,1:T(8,128)} async-done(((f32[2048,3840]{0,1:T(8,128)}), f32[128,3840]{0,1:T(8,128)}) %reduce-scatter.3.cloned.1.call-update) | async-done | bytes 1966096 | tf_op jit(solution)/shard_map/reduce_scatter | solution.py:118
  1914.0 702.6 %reduce-scatter.5.cloned.1.call-done = f32[128,9216]{1,0:T(8,128)} async-done(((f32[2048,9216]{1,0:T(8,128)}), f32[128,9216]{1,0:T(8,128)}) %reduce-scatter.5.cloned.1.call-update) | async-done | bytes 4718608 | tf_op jit(solution)/shard_map/reduce_scatter | solution.py:118
  2621.3 99.8 %all-reduce.92.cloned.1.call-done = (f32[5,256,256]{2,1,0:T(8,128)}, f32[5,256,256]{2,1,0:T(8,128)}) async-done(((f32[5,256,256]{2,1,0:T(8,128)}, f32[5,256,256]{2,1,0:T(8,128)}), (f32[5,256,256]{2,1,0:T(8,128)}, f32[5,256,256]{2,1,0:T(8,128)})) %all-reduce.92.cloned.1.call-update) | async-done | bytes 2621456 | tf_op jit(solution)/shard_map/psum | solution.py:296
  (665 shorter events, 857.7 us)
Async XLA Ops:
  7.2 79.4 %copy-start = (bf16[5,256,256]{2,1,0:T(8,128)(2,1)S(1)}, bf16[5,256,256]{2,1,0:T(8,128)(2,1)}, u32[]{:S(2)}) copy-start(bf16[5,256,256]{2,1,0:T(8,128)(2,1)} %param.27) | copy-start | bytes 1966084
  7.2 61.9 %copy-start.15 = (bf16[512,2048]{1,0:T(8,128)(2,1)S(1)}, bf16[512,2048]{1,0:T(8,128)(2,1)}, u32[]{:S(2)}) copy-start(bf16[512,2048]{1,0:T(8,128)(2,1)} %param.22) | copy-start | bytes 6291460
  7.2 61.9 %all-gather.11.cloned.1.call-start = ((), (), s32[]{:S(2)}) async-start(), calls=%async_computation.2 | async-start | bytes 5570560 | tf_op jit(solution)/shard_map/all_gather | solution.py:81
  8.0 412.5 %all-gather.13.cloned.1.call-start = ((), (), s32[]{:S(2)}) async-start(), calls=%async_computation.3 | async-start | bytes 5570560 | tf_op jit(solution)/shard_map/all_gather | solution.py:76
  8.7 424.3 %all-gather.15.cloned.1.call-start = ((), (), s32[]{:S(2)}) async-start(), calls=%async_computation.4 | async-start | bytes 5570560 | tf_op jit(solution)/shard_map/all_gather | solution.py:92
  9.5 537.9 %all-reduce.88.cloned.1.call-start = ((), (), s32[]{:S(2)}) async-start(), calls=%async_computation.5 | async-start | bytes 8388608 | tf_op jit(solution)/shard_map/psum | solution.py:88
  11.2 85.0 %copy-start.105 = (f32[512]{0:T(512)}, f32[512]{0:T(512)S(1)}, u32[]{:S(2)}) copy-start(f32[512]{0:T(512)S(1)} %convert_subtract_fusion) | copy-start | bytes 6148
  13.3 68.7 %copy-start.84 = (f32[512]{0:T(512)}, f32[512]{0:T(512)S(1)}, u32[]{:S(2)}) copy-start(f32[512]{0:T(512)S(1)} %get-tuple-element.473) | copy-start | bytes 6148
  13.3 68.7 %copy-start.86 = (f32[512]{0:T(512)}, f32[512]{0:T(512)S(1)}, u32[]{:S(2)}) copy-start(f32[512]{0:T(512)S(1)} %get-tuple-element.474) | copy-start | bytes 6148
  13.3 68.7 %copy-start.88 = (f32[512]{0:T(512)}, f32[512]{0:T(512)S(1)}, u32[]{:S(2)}) copy-start(f32[512]{0:T(512)S(1)} %get-tuple-element.475) | copy-start | bytes 6148
  13.3 68.7 %copy-start.90 = (f32[512]{0:T(512)}, f32[512]{0:T(512)S(1)}, u32[]{:S(2)}) copy-start(f32[512]{0:T(512)S(1)} %get-tuple-element.476) | copy-start | bytes 6148
  14.0 82.2 %copy-start.63 = (f32[1280]{0:T(1024)}, f32[1280]{0:T(1024)S(1)}, u32[]{:S(2)}) copy-start(f32[1280]{0:T(1024)S(1)} %get-tuple-element.472) | copy-start | bytes 15364
  14.0 65.0 %copy-start.97 = (f32[4,1280]{1,0:T(4,128)S(1)}, f32[4,1280]{1,0:T(4,128)}, u32[]{:S(2)}) copy-start(f32[4,1280]{1,0:T(4,128)} %param.31) | copy-start | bytes 61444
  75.6 4.8 collective-permute-start
  440.9 209.7 %all-gather.19.cloned.1.call-start = ((), (), s32[]{:S(2)}) async-start(), calls=%async_computation.7 | async-start | bytes 13369344 | tf_op jit(solution)/shard_map/all_gather | solution.py:81
  441.5 310.6 %all-gather.17.cloned.1.call-start = ((), (), s32[]{:S(2)}) async-start(), calls=%async_computation.6 | async-start | bytes 13369344 | tf_op jit(solution)/shard_map/all_gather | solution.py:76
  442.0 411.5 %all-gather.21.cloned.1.call-start = ((), (), s32[]{:S(2)}) async-start(), calls=%async_computation.8 | async-start | bytes 13369344 | tf_op jit(solution)/shard_map/all_gather | solution.py:92
  442.8 110.1 %copy-start.73 = (f32[2048]{0:T(1024)S(1)}, f32[2048]{0:T(1024)}, u32[]{:S(2)}) copy-start(f32[2048]{0:T(1024)} %param.35) | copy-start | bytes 24580
  442.8 570.7 %all-reduce.90.cloned.1.call-start = ((), (), s32[]{:S(2)}) async-start(), calls=%async_computation.9 | async-start | bytes 8388608 | tf_op jit(solution)/shard_map/psum | solution.py:110
  907.3 711.7 %all-reduce.94.cloned.1.call-start = ((), (), s32[]{:S(2)}) async-start(), calls=%async_computation.13 | async-start | bytes 16777216 | tf_op jit(solution)/shard_map/psum | solution.py:88
  1394.0 7.4 collective-permute-start.1
  1410.8 498.4 %reduce-scatter.3.cloned.1.call-start = ((), (), s32[]{:S(2)}) async-start(), calls=%async_computation.10 | async-start | bytes 33423360 | tf_op jit(solution)/shard_map/reduce_scatter | solution.py:118
  1451.7 1164.9 %reduce-scatter.5.cloned.1.call-start = ((), (), s32[]{:S(2)}) async-start(), calls=%async_computation.11 | async-start | bytes 80216064 | tf_op jit(solution)/shard_map/reduce_scatter | solution.py:118
  1542.2 1178.9 %all-reduce.92.cloned.1.call-start = ((), (), s32[]{:S(2)}) async-start(), calls=%async_computation.12 | async-start | bytes 5242880 | tf_op jit(solution)/shard_map/psum | solution.py:296
  (114 other events, 1035.5 us)
Sparse Core Ops, SparseCore 0:
  10.4 58.6 all-gather.10
  71.4 54.5 all-gather.12
  128.3 54.5 all-gather.14
  441.0 106.3 all-reduce.87
  549.8 100.7 all-gather.18
  653.0 98.9 all-gather.16
  754.6 98.9 all-gather.20
  907.4 106.0 all-reduce.89
  1410.9 199.0 all-reduce.93
  1614.0 295.1 reduce-scatter.2
  1913.4 703.1 reduce-scatter.4
  2621.2 99.9 all-reduce.91
where the time goes:
time: 2750 us; the launch traced here: 2730 us
  waiting for transfers between devices  1550 us (56%)
  local copies, waits for them, and re-layouts  565 us (21%)
  other arithmetic  270 us (10%)
  matrix products  198 us (7%)
  blocking collectives  124 us (5%)
    reduce_scatter x2, waiting for transfers between devices, reduce_rows(): lax.psum_scatter(row_terms(pairs), ('dp', 'seq'), scatter_dimension=0, ti...  977 us
    slice x65, local copies, waits for them, and re-layouts, on_device(): lax.associative_scan(compose, (next_decay, grad_state), reverse=True)  176 us
    all_gather x2, waiting for transfers between devices, project_pair(): lax.all_gather(second, ('dp', 'seq'), axis=0, tiled=True)  151 us
    slice x60, local copies, waits for them, and re-layouts, on_device(): prefix_decay, local_state = lax.associative_scan(compose, (decays, drives))  125 us
    psum x2, waiting for transfers between devices, mp_total(): return lax.psum(partial_value, 'mp')  105 us
    psum x1, waiting for transfers between devices, on_device(): lax.psum((grad_gate_a, grad_gate_i, grad_bias_a, grad_bias_i, grad_conv_w...  99.8 us
    pad x32, local copies, waits for them, and re-layouts, on_device(): prefix_decay, local_state = lax.associative_scan(compose, (decays, drives))  91.2 us
    all_gather x2, waiting for transfers between devices, branch_out(): lax.all_gather(weight, ('dp', 'seq'), axis=0, tiled=True)  89.6 us
  transfers between devices with their start and end apart: 14, of which 10 were waited for; matrix products, arithmetic and copies ran while one was open for 22% of the time, Pallas kernels for 0%

commit v1 on v0

v1 whole, which is shorter than its diff:
```python
import functools

import jax
import jax.numpy as jnp
from jax import lax
from jax.experimental import pallas as pl
from jax.experimental.pallas import tpu as pltpu
from jax.sharding import PartitionSpec as P

epsilon = 1e-06
decay_scale = 8.0
MESH = pl.DeviceIdType.MESH
VMEM_LIMIT = 60 * 2**20
SEGMENTS = 8
PAD = 8
CHUNKS = 4
bf16 = jnp.bfloat16
f32 = jnp.float32


def xor_permute(value, axis, bit):
    count = lax.axis_size(axis)
    return lax.ppermute(value, axis, [(source, source ^ bit) for source in range(count)])


def matmul(left, right):
    return jnp.dot(left, right, preferred_element_type=f32)


def contract(left, right):
    return lax.dot_general(left, right, (((1,), (1,)), ((), ())), preferred_element_type=f32)


def contract_rows(left, right):
    return lax.dot_general(left, right, (((0,), (0,)), ((), ())), preferred_element_type=f32)


def norm_scale(values):
    return lax.rsqrt(jnp.mean(values * values, axis=-1, keepdims=True) + epsilon)


def gelu_parts(y):
    c = 0.7978845608028654
    u = c * (y + 0.044715 * y * y * y)
    t = jnp.tanh(u)
    half = 0.5 * (1.0 + t)
    slope = half + 0.5 * y * (1.0 - t * t) * (c * (1.0 + 3.0 * 0.044715 * y * y))
    return y * half, slope


def one_minus_square(log_decay, decay):
    y = -2.0 * log_decay
    series = 1.0 - y * (1.0 / 8.0)
    for k in (7, 6, 5, 4, 3, 2):
        series = 1.0 - y * (1.0 / k) * series
    return jnp.where(y < 0.5, y * series, 1.0 - decay * decay)


def seq_barrier(nseq):
    dp, z, mp = (lax.axis_index(a) for a in ("dp", "seq", "mp"))
    barrier = pltpu.get_barrier_semaphore()
    for step in range(1, nseq):
        pl.semaphore_signal(
            barrier, inc=1, device_id=(dp, lax.rem(z + step, nseq), mp), device_id_type=MESH
        )
    pl.semaphore_wait(barrier, nseq - 1)


def to_seq(src, dst, send_sem, recv_sem, target):
    dp, mp = (lax.axis_index(a) for a in ("dp", "mp"))
    return pltpu.make_async_remote_copy(
        src_ref=src,
        dst_ref=dst,
        send_sem=send_sem,
        recv_sem=recv_sem,
        device_id=(dp, target, mp),
        device_id_type=MESH,
    )


LANES = 128


def put(ref, at, h, value):
    count = value.shape[1] // LANES
    for k in range(count):
        ref[h * count + k, at, :] = value[:, k * LANES : (k + 1) * LANES]


def take(ref, at, h, block):
    count = block // LANES
    return jnp.concatenate([ref[h * count + k, at, :] for k in range(count)], axis=1)


def side_by_side(parts):
    return jnp.concatenate(parts, axis=1)


def rec_forward_kernel(
    nseq, heads, block,
    px_ref, py_ref, marks_ref, ga_ref, gi_ref, vec_ref,
    mixed_ref, states_ref, pxe_ref, rate_ref, ig_ref, co_ref,
    a_s, b_s, msg, got, state_in, halo, halo_send, halo_recv, end_send, end_recv,
):
    rows, width = px_ref.shape
    seg = rows // SEGMENTS
    z = lax.axis_index("seq")
    seq_barrier(nseq)

    @pl.when(z < nseq - 1)
    def _():
        to_seq(px_ref.at[pl.ds(rows - PAD, PAD)], halo, halo_send, halo_recv, z + 1).start()

    def copy_rows(r, _):
        pxe_ref[pl.ds(PAD + r * seg, seg), :] = px_ref[pl.ds(r * seg, seg), :].astype(bf16).astype(f32)
        return 0

    lax.fori_loop(0, SEGMENTS, copy_rows, 0)

    @pl.when(z == 0)
    def _():
        halo[...] = jnp.zeros_like(halo)

    @pl.when(z > 0)
    def _():
        to_seq(px_ref.at[pl.ds(rows - PAD, PAD)], halo, halo_send, halo_recv, z).wait_recv()

    pxe_ref[pl.ds(0, PAD), :] = halo[...].astype(bf16).astype(f32)

    @pl.when(z < nseq - 1)
    def _():
        to_seq(px_ref.at[pl.ds(rows - PAD, PAD)], halo, halo_send, halo_recv, z).wait_send()

    def head(h, _):
        cols = pl.ds(pl.multiple_of(h * block, block), block)

        def part(r, _):
            at = pl.ds(pl.multiple_of(r * seg, seg), seg)
            window = pxe_ref[pl.ds(pl.multiple_of(r * seg, seg), seg + PAD), cols]
            conv_out = vec_ref[4:5, cols] + vec_ref[0:1, cols] * window[PAD:]
            for lag in (1, 2, 3):
                shifted = pltpu.roll(window, lag, 0)[PAD:]
                conv_out = conv_out + vec_ref[lag : lag + 1, cols] * shifted * marks_ref[lag, at, :]
            low = conv_out.astype(bf16)
            gate_r = matmul(low, ga_ref[h])
            gate_x = matmul(low, gi_ref[h])
            rate = jax.nn.sigmoid(gate_r + vec_ref[5:6, cols])
            ig = jax.nn.sigmoid(gate_x + vec_ref[6:7, cols])
            log_decay = -decay_scale * rate * vec_ref[7:8, cols]
            decay = jnp.exp(log_decay)
            mult = jnp.sqrt(one_minus_square(log_decay, decay))
            put(a_s, at, h, decay * marks_ref[0, at, :])
            put(b_s, at, h, conv_out * ig * mult)
            rate_ref[at, cols] = rate
            ig_ref[at, cols] = ig
            co_ref[at, cols] = conv_out
            return 0

        lax.fori_loop(0, SEGMENTS, part, 0)
        return 0

    lax.fori_loop(0, heads, head, 0)

    groups = width // LANES

    def turn(t, kept):
        at = pl.ds(t, SEGMENTS, stride=seg)
        result = []
        for g, (prefix, state) in enumerate(kept):
            decay = a_s[g, at, :]
            prefix = prefix * decay
            state = state * decay + b_s[g, at, :]
            a_s[g, at, :] = prefix
            b_s[g, at, :] = state
            result.append((prefix, state))
        return tuple(result)

    one, zero = jnp.ones((SEGMENTS, LANES), f32), jnp.zeros((SEGMENTS, LANES), f32)
    ends = lax.fori_loop(0, seg, turn, ((one, zero),) * groups)
    prefix, state = (side_by_side([end[k] for end in ends]) for k in (0, 1))
    total_a, total_b = prefix[0:1], state[0:1]
    for s in range(1, SEGMENTS):
        total_a, total_b = total_a * prefix[s : s + 1], total_b * prefix[s : s + 1] + state[s : s + 1]
    msg[0:1, :] = total_a
    msg[1:2, :] = total_b
    msg[2:PAD, :] = jnp.zeros((PAD - 2, width), f32)
    for step in range(1, nseq):

        @pl.when(z + step < nseq)
        def _():
            to_seq(msg, got.at[z], end_send.at[step - 1], end_recv.at[z], z + step).start()

    state_in[...] = jnp.zeros_like(state_in)
    for source in range(nseq - 1):

        @pl.when(source < z)
        def _():
            to_seq(msg, got.at[source], end_send.at[0], end_recv.at[source], z).wait_recv()
            state_in[...] = got[source, 0:1, :] * state_in[...] + got[source, 1:2, :]

    carry = state_in[...]
    states_ref[pl.ds(0, PAD), :] = jnp.broadcast_to(carry, (PAD, width))
    for s in range(SEGMENTS):
        halo[s : s + 1, :] = carry
        carry = prefix[s : s + 1] * carry + state[s : s + 1]

    def finish(i, _):
        s, h = i // heads, lax.rem(i, heads)
        cols = pl.ds(pl.multiple_of(h * block, block), block)
        at = pl.ds(pl.multiple_of(s * seg, seg), seg)
        states = take(b_s, at, h, block) + take(a_s, at, h, block) * halo[pl.ds(s, 1), cols]
        states_ref[pl.ds(pl.multiple_of(PAD + s * seg, PAD), seg), cols] = states
        mixed_ref[at, cols] = (states * gelu_parts(py_ref[at, cols])[0]).astype(bf16)
        return 0

    lax.fori_loop(0, SEGMENTS * heads, finish, 0)
    for step in range(1, nseq):

        @pl.when(z + step < nseq)
        def _():
            to_seq(msg, got.at[z], end_send.at[step - 1], end_recv.at[z], z).wait_send()


def rec_forward(nseq, px, py, marks, gate_a, gate_i, vectors):
    rows, width = px.shape
    heads, block = gate_a.shape[:2]
    vmem = pl.BlockSpec(memory_space=pltpu.VMEM)
    big = jax.ShapeDtypeStruct((rows, width), f32)
    ext = jax.ShapeDtypeStruct((rows + PAD, width), f32)
    small = pltpu.VMEM((PAD, width), f32)
    dma = pltpu.SemaphoreType.DMA
    return pl.pallas_call(
        functools.partial(rec_forward_kernel, nseq, heads, block),
        out_shape=(jax.ShapeDtypeStruct((rows, width), bf16), ext, ext, big, big, big),
        in_specs=[vmem] * 6,
        out_specs=[vmem] * 6,
        scratch_shapes=[
            pltpu.VMEM((width // LANES, rows, LANES), f32),
            pltpu.VMEM((width // LANES, rows, LANES), f32),
            small,
            pltpu.VMEM((nseq, PAD, width), f32),
            pltpu.VMEM((1, width), f32),
            small,
            dma, dma, dma((nseq - 1,)), dma((nseq,)),
        ],
        compiler_params=pltpu.CompilerParams(
            collective_id=1, has_side_effects=True, vmem_limit_bytes=VMEM_LIMIT
        ),
        name="rec_forward",
    )(px, py, marks, gate_a, gate_i, vectors)


def rec_backward_kernel(
    nseq, heads, block,
    gm_ref, py_ref, states_ref, pxe_ref, rate_ref, ig_ref, co_ref, marks_ref, ga_ref, gi_ref, vec_ref,
    gpy_ref, gpx_ref, gga_ref, ggi_ref, sums_ref,
    a_s, b_s, w_s, gc_s, gr_s, gx_s, msg, got, grad_in, carry_s, head_s, halo_send, halo_recv, end_send, end_recv,
):
    rows, width = gm_ref.shape
    seg = rows // SEGMENTS
    z = lax.axis_index("seq")
    seq_barrier(nseq)

    def first(i, _):
        s, h = i // heads, lax.rem(i, heads)
        cols = pl.ds(pl.multiple_of(h * block, block), block)
        at = pl.ds(pl.multiple_of(s * seg, seg), seg)
        gelu, slope = gelu_parts(py_ref[at, cols])
        gm = gm_ref[at, cols]
        states = states_ref[pl.ds(pl.multiple_of(PAD + s * seg, PAD), seg), cols]
        gpy_ref[at, cols] = (gm * states * slope).astype(bf16)
        put(b_s, at, h, gm * gelu)
        put(a_s, at, h, jnp.exp(-decay_scale * rate_ref[at, cols] * vec_ref[7:8, cols]) * marks_ref[0, at, :])
        return 0

    lax.fori_loop(0, SEGMENTS * heads, first, 0)

    groups = width // LANES

    def turn(i, kept):
        at = pl.ds(seg - 1 - i, SEGMENTS, stride=seg)
        result = []
        for g, (suffix, owed) in enumerate(kept):
            decay = a_s[g, at, :]
            carry = b_s[g, at, :] + owed
            b_s[g, at, :] = carry
            w_s[g, at, :] = suffix
            result.append((suffix * decay, carry * decay))
        return tuple(result)

    one, zero = jnp.ones((SEGMENTS, LANES), f32), jnp.zeros((SEGMENTS, LANES), f32)
    ends = lax.fori_loop(0, seg, turn, ((one, zero),) * groups)
    suffix, owed = (side_by_side([end[k] for end in ends]) for k in (0, 1))
    last = SEGMENTS - 1
    total_w, total_g = suffix[last:], owed[last:]
    for s in range(last - 1, -1, -1):
        total_w, total_g = total_w * suffix[s : s + 1], total_g * suffix[s : s + 1] + owed[s : s + 1]
    msg[0:1, :] = total_w
    msg[1:2, :] = total_g
    msg[2:PAD, :] = jnp.zeros((PAD - 2, width), f32)
    for step in range(1, nseq):

        @pl.when(z >= step)
        def _():
            to_seq(msg, got.at[z], end_send.at[step - 1], end_recv.at[z], z - step).start()

    grad_in[...] = jnp.zeros_like(grad_in)
    for source in range(nseq - 1, 0, -1):

        @pl.when(source > z)
        def _():
            to_seq(msg, got.at[source], end_send.at[0], end_recv.at[source], z).wait_recv()
            grad_in[...] = got[source, 0:1, :] * grad_in[...] + got[source, 1:2, :]

    carry = grad_in[...]
    for s in range(last, -1, -1):
        carry_s[s : s + 1, :] = carry
        carry = suffix[s : s + 1] * carry + owed[s : s + 1]

    def fold(value):
        return jnp.sum(value.reshape(seg // 8, 8, block), axis=0)

    def head(h, _):
        cols = pl.ds(pl.multiple_of(h * block, block), block)
        shrink = vec_ref[7:8, cols]

        def part(s, sums):
            at = pl.ds(pl.multiple_of(s * seg, seg), seg)
            ahead = pl.ds(pl.multiple_of(s * seg, seg), seg + PAD)
            carry = take(b_s, at, h, block) + take(w_s, at, h, block) * carry_s[pl.ds(s, 1), cols]
            before = pltpu.roll(states_ref[ahead, cols], 1, 0)[PAD:]
            rate, ig, conv_out = rate_ref[at, cols], ig_ref[at, cols], co_ref[at, cols]
            log_decay = -decay_scale * rate * shrink
            decay = jnp.exp(log_decay)
            mult = jnp.sqrt(one_minus_square(log_decay, decay))
            gated = carry * conv_out * ig
            grad_log = carry * before * decay * marks_ref[0, at, :] - gated * (decay * decay) / mult
            spread = grad_log * decay_scale * rate
            grad_r = -spread * shrink * (1.0 - rate)
            grad_x = gated * mult * (1.0 - ig)
            low_r, low_x = grad_r.astype(bf16), grad_x.astype(bf16)
            gr_s[at, :] = low_r
            gx_s[at, :] = low_x
            grad_conv = carry * ig * mult + contract(low_r, ga_ref[h]) + contract(low_x, gi_ref[h])
            gc_s[at, cols] = grad_conv
            window = pxe_ref[ahead, cols]
            terms = [grad_r, grad_x, spread, grad_conv, grad_conv * window[PAD:]]
            for lag in (1, 2, 3):
                terms.append(grad_conv * marks_ref[lag, at, :] * pltpu.roll(window, lag, 0)[PAD:])
            return tuple(total + fold(term) for total, term in zip(sums, terms))

        sums = lax.fori_loop(
            0, SEGMENTS, part, tuple(jnp.zeros((8, block), f32) for _ in range(8))
        )
        for k, total in enumerate(sums):
            sums_ref[k : k + 1, cols] = jnp.sum(total, axis=0, keepdims=True)
        low = co_ref[:, cols].astype(bf16)
        gga_ref[h] = contract_rows(low, gr_s[...])
        ggi_ref[h] = contract_rows(low, gx_s[...])
        return 0

    lax.fori_loop(0, heads, head, 0)
    head_s[...] = gc_s[pl.ds(0, PAD), :]

    @pl.when(z > 0)
    def _():
        to_seq(head_s, gc_s.at[pl.ds(rows, PAD)], halo_send, halo_recv, z - 1).start()

    @pl.when(z < nseq - 1)
    def _():
        to_seq(head_s, gc_s.at[pl.ds(rows, PAD)], halo_send, halo_recv, z).wait_recv()

    @pl.when(z == nseq - 1)
    def _():
        gc_s[pl.ds(rows, PAD), :] = jnp.zeros((PAD, width), f32)

    def final(i, _):
        s, h = i // heads, lax.rem(i, heads)
        cols = pl.ds(pl.multiple_of(h * block, block), block)
        at = pl.ds(pl.multiple_of(s * seg, seg), seg)
        ahead = pl.ds(pl.multiple_of(s * seg, seg), seg + PAD)
        owed = gc_s[ahead, cols]
        grad = vec_ref[0:1, cols] * owed[:seg]
        for lag in (1, 2, 3):
            shifted = pltpu.roll(owed * marks_ref[lag, ahead, :], seg + PAD - lag, 0)[:seg]
            grad = grad + vec_ref[lag : lag + 1, cols] * shifted
        gpx_ref[at, cols] = grad.astype(bf16)
        return 0

    lax.fori_loop(0, SEGMENTS * heads, final, 0)

    @pl.when(z > 0)
    def _():
        to_seq(head_s, gc_s.at[pl.ds(rows, PAD)], halo_send, halo_recv, z).wait_send()

    for step in range(1, nseq):

        @pl.when(z >= step)
        def _():
            to_seq(msg, got.at[z], end_send.at[step - 1], end_recv.at[z], z).wait_send()


def rec_backward(nseq, gm, py, states, pxe, rate, ig, co, marks, gate_a, gate_i, vectors):
    rows, width = gm.shape
    heads, block = gate_a.shape[:2]
    vmem = pl.BlockSpec(memory_space=pltpu.VMEM)
    low = jax.ShapeDtypeStruct((rows, width), bf16)
    gates = jax.ShapeDtypeStruct(gate_a.shape, f32)
    small = pltpu.VMEM((PAD, width), f32)
    dma = pltpu.SemaphoreType.DMA
    return pl.pallas_call(
        functools.partial(rec_backward_kernel, nseq, heads, block),
        out_shape=(low, low, gates, gates, jax.ShapeDtypeStruct((8, width), f32)),
        in_specs=[vmem] * 11,
        out_specs=[vmem] * 5,
        scratch_shapes=[
            pltpu.VMEM((width // LANES, rows, LANES), f32),
            pltpu.VMEM((width // LANES, rows, LANES), f32),
            pltpu.VMEM((width // LANES, rows, LANES), f32),
            pltpu.VMEM((rows + PAD, width), f32),
            pltpu.VMEM((rows, block), bf16),
            pltpu.VMEM((rows, block), bf16),
            small,
            pltpu.VMEM((nseq, PAD, width), f32),
            pltpu.VMEM((1, width), f32),
            small,
            small,
            dma, dma, dma((nseq - 1,)), dma((nseq,)),
        ],
        compiler_params=pltpu.CompilerParams(
            collective_id=2, has_side_effects=True, vmem_limit_bytes=VMEM_LIMIT
        ),
        name="rec_backward",
    )(gm, py, states, pxe, rate, ig, co, marks, gate_a, gate_i, vectors)


def on_device(
    ndp, nseq,
    tokens, doc_lengths, norm_gain, w_y, w_x, gate_a, gate_i, bias_a, bias_i, conv_w, conv_b,
    decay_param, w_out, mlp_gain, w_gate, w_up, w_down, cotangent,
):
    local_len, features = tokens.shape
    rows_here = w_y.shape[0]
    width_here = w_y.shape[1]
    hidden_here = w_gate.shape[1]
    block = gate_a.shape[1]
    bits = [1 << k for k in range(ndp.bit_length() - 1)]

    def inner(value):
        lead = value.shape[:-1]
        return jnp.swapaxes(value.reshape(*lead, ndp, nseq, rows_here), -3, -2).reshape(*lead, features)

    def outer(value):
        lead = value.shape[:-1]
        return jnp.swapaxes(value.reshape(*lead, nseq, ndp, rows_here), -3, -2).reshape(*lead, features)

    def gather(weight):
        return lax.all_gather(weight, ("seq", "dp"), axis=0, tiled=True)

    def spread(value):
        for bit in reversed(bits):
            value = jnp.concatenate([value, xor_permute(value, "dp", bit)], axis=0)
        return value

    def collect(value):
        for bit in bits:
            half = value.shape[0] // 2
            value = (value[:half] + xor_permute(value[half:], "dp", bit)).astype(bf16)
        return value.astype(f32) + xor_permute(value, "mp", 1).astype(f32)

    position = lax.axis_index("seq") * local_len + jnp.arange(local_len + PAD, dtype=jnp.int32)
    lengths_row = doc_lengths[0]
    starts = jnp.cumsum(lengths_row) - lengths_row
    resets = jnp.any(position[:, None] == starts[None, :], axis=1)
    doc_start = jnp.max(jnp.where(starts[None, :] <= position[:, None], starts[None, :], 0), axis=1)
    marks = jnp.stack(
        [1.0 - resets.astype(f32)] + [(position - lag >= doc_start).astype(f32) for lag in (1, 2, 3)]
    )
    marks = jnp.broadcast_to(marks[:, :, None], (4, local_len + PAD, block))
    vectors = jnp.concatenate(
        [conv_w, conv_b[None], bias_a[None], bias_i[None], jax.nn.softplus(-decay_param)[None]], axis=0
    )

    all_y, all_x = gather(w_y), gather(w_x)
    mlp_rows = lax.all_to_all(
        jnp.stack([w_gate, w_up, w_down]).reshape(3, rows_here, ndp, hidden_here // ndp),
        "dp", 2, 1, tiled=True,
    ).reshape(3, ndp * rows_here, hidden_here // ndp)
    all_out = gather(w_out)
    all_gate, all_up, all_down = (
        lax.all_gather(mlp_rows[k], "seq", axis=0, tiled=True) for k in range(3)
    )
    gain_one, gain_two = inner(norm_gain), inner(mlp_gain)
    resid = inner(tokens).astype(f32)
    scale_one = norm_scale(resid)
    acts_one = (resid * scale_one * gain_one).astype(bf16)
    pre_y, pre_x = matmul(acts_one, all_y), matmul(acts_one, all_x)
    mixed_rec, states, pxe, rate, ig, conv_out = rec_forward(
        nseq, pre_x, pre_y, marks, gate_a, gate_i, vectors
    )

    cot = inner(cotangent)
    per = local_len // CHUNKS
    pieces = []
    for k in range(CHUNKS):
        here = slice(k * per, (k + 1) * per)
        part = contract(mixed_rec[here], all_out).astype(bf16)
        middle = resid[here] + (part.astype(f32) + xor_permute(part, "mp", 1).astype(f32))
        scale_two = norm_scale(middle)
        acts = spread((middle * scale_two * gain_two).astype(bf16))
        cots = spread(cot[here])
        pre_gate, pre_up = matmul(acts, all_gate), matmul(acts, all_up)
        gelu, slope = gelu_parts(pre_gate)
        mixed = (gelu * pre_up).astype(bf16)
        grad_mixed = matmul(cots, all_down)
        grad_gate = (grad_mixed * pre_up * slope).astype(bf16)
        grad_up = (grad_mixed * gelu).astype(bf16)
        grad_acts = collect(
            (contract(grad_gate, all_gate) + contract(grad_up, all_up)).astype(bf16)
        )
        normed = middle * scale_two
        grad_normed = grad_acts * gain_two
        grad_middle = cot[here].astype(f32) + scale_two * (
            grad_normed - normed * jnp.mean(grad_normed * normed, axis=-1, keepdims=True)
        )
        gain_part = jnp.sum(grad_acts * normed, axis=0)
        final = middle + collect(contract(mixed, all_down).astype(bf16))
        pieces.append((acts, cots, mixed, grad_gate, grad_up, grad_middle, gain_part, final.astype(bf16)))
    acts, cots, mixed, grad_gate, grad_up, grad_middle, gain_parts, output = (
        [piece[j] for piece in pieces] for j in range(8)
    )
    join = functools.partial(jnp.concatenate, axis=0)
    acts, cots, mixed, grad_gate, grad_up = map(join, (acts, cots, mixed, grad_gate, grad_up))
    grad_middle = join(grad_middle)

    def reduce_mlp(left, right):
        total = lax.psum_scatter(
            contract_rows(left, right).astype(bf16), "seq", scatter_dimension=0, tiled=True
        )
        return total

    mlp_sums = jnp.stack(
        [reduce_mlp(acts, grad_gate), reduce_mlp(acts, grad_up), reduce_mlp(cots, mixed)]
    )
    mlp_sums = lax.all_to_all(mlp_sums, "dp", 1, 2, tiled=True).astype(f32)

    grad_middle_low = grad_middle.astype(bf16)
    grad_mixed_rec = matmul(grad_middle_low, all_out)
    grad_pre_y, grad_pre_x, grad_gate_a, grad_gate_i, sums = rec_backward(
        nseq, grad_mixed_rec, pre_y, states, pxe, rate, ig, conv_out, marks, gate_a, gate_i, vectors
    )
    part = (contract(grad_pre_y, all_y) + contract(grad_pre_x, all_x)).astype(bf16)
    grad_acts = part.astype(f32) + xor_permute(part, "mp", 1).astype(f32)
    normed = resid * scale_one
    grad_normed = grad_acts * gain_one
    input_grad = grad_middle + scale_one * (
        grad_normed - normed * jnp.mean(grad_normed * normed, axis=-1, keepdims=True)
    )

    def reduce_rec(left, right):
        return lax.psum_scatter(
            contract_rows(left, right).astype(bf16), ("seq", "dp"), scatter_dimension=0, tiled=True
        ).astype(f32)

    grad_w_out = reduce_rec(grad_middle_low, mixed_rec)
    grad_w_y = reduce_rec(acts_one, grad_pre_y)
    grad_w_x = reduce_rec(acts_one, grad_pre_x)
    totals = lax.psum(
        (
            grad_gate_a,
            grad_gate_i,
            sums,
            jnp.sum(grad_acts * normed, axis=0),
            functools.reduce(jnp.add, gain_parts),
        ),
        ("dp", "seq"),
    )
    sums = totals[2]
    return (
        outer(join(output)),
        outer(input_grad),
        outer(totals[3]),
        grad_w_y,
        grad_w_x,
        totals[0],
        totals[1],
        sums[0],
        sums[1],
        sums[4:8],
        sums[3],
        sums[2] * jax.nn.sigmoid(-decay_param),
        grad_w_out,
        outer(totals[4]),
        mlp_sums[0],
        mlp_sums[1],
        mlp_sums[2],
    )


def solution(mesh):
    rows, cols = P(("dp", "seq"), None), P(("dp", "seq"), "mp")
    return jax.shard_map(
        functools.partial(on_device, mesh.shape["dp"], mesh.shape["seq"]),
        mesh=mesh,
        in_specs=(
            rows, P("dp", None), P(), cols, cols, P("mp", None, None), P("mp", None, None), P("mp"), P("mp"),
            P(None, "mp"), P("mp"), P("mp"), cols, P(), cols, cols, cols, rows,
        ),
        out_specs=(
            rows, rows, P(), cols, cols, P("mp", None, None), P("mp", None, None), P("mp"), P("mp"),
            P(None, "mp"), P("mp"), P("mp"), cols, P(), cols, cols, cols,
        ),
        check_vma=False,
    )
```

time: 2750 us -> 1200 us (0.44)
  waiting for transfers between devices: 1550 us -> 617 us
  local copies, waits for them, and re-layouts: 565 us -> 122 us
  other arithmetic: 270 us -> 49.8 us
  Pallas kernels: 0 us -> 90.3 us
  matrix products: 198 us -> 157 us
  starting transfers between devices: 5.45 us -> 38.2 us
    reduce_scatter x2 -> x6, waiting for transfers between devices: 977 us -> 323 us  [the longest x3 187 us: reduce_mlp(): lax.psum_scatter(contract_rows(left, right).astype(bf16), 'seq', scatter_...]
    slice x130 -> x33, local copies, waits for them, and re-layouts: 308 us -> 32.5 us  [the longest x5 13.7 us: on_device(): resid[here] + (part.astype(f32) + xor_permute(part, 'mp', 1).astype(f32))]
    psum x4 -> x1, waiting for transfers between devices: 241 us -> 11.4 us  [on_device(): lax.psum((grad_gate_a, grad_gate_i, sums, jnp.sum(grad_acts * normed, axi...]
    all_gather x6, waiting for transfers between devices: 330 us -> 140 us  [the longest x3 121 us: on_device(): lax.all_gather(mlp_rows[k], 'seq', axis=0, tiled=True)]
    pad x64 -> x0, local copies, waits for them, and re-layouts: 176 us -> none  [the longest x32 91.2 us: on_device(): prefix_decay, local_state = lax.associative_scan(compose, (decays, drives))]
    ppermute x2 -> x45, waiting for transfers between devices: 1.25 us -> 140 us  [xor_permute(): lax.ppermute(value, axis, [(source, source ^ bit) for source in range(cou...]
    concatenate x32 -> x9, other arithmetic: 101 us -> 10.5 us  [the longest x8 10.3 us: spread(): value = jnp.concatenate([value, xor_permute(value, 'dp', bit)], axis=0)]
    pallas_call x0 -> x2, Pallas kernels: none -> 90.3 us  [the longest x1 49 us: rec_backward(): pl.pallas_call(functools.partial(rec_backward_kernel, nseq, heads, block)...]
  transfers between devices with their start and end apart: 14 -> 59, of which waited for: 10 -> 28; matrix products, arithmetic and copies ran while one was open for 22% -> 26% of each run, Pallas kernels for 0% -> 3%
where the time goes in v1:
time: 1200 us; the launch traced here: 1190 us
  waiting for transfers between devices  617 us (51%)
  matrix products  157 us (13%)
  local copies, waits for them, and re-layouts  122 us (10%)
  blocking collectives  103 us (9%)
  Pallas kernels  90.3 us (8%)
  other arithmetic  49.8 us (4%)
  starting transfers between devices  38.2 us (3%)
  between operations  15.9 us (1%)
    reduce_scatter x3, waiting for transfers between devices, reduce_mlp(): lax.psum_scatter(contract_rows(left, right).astype(bf16), 'seq', scatter_...  187 us
    ppermute x45, waiting for transfers between devices, xor_permute(): lax.ppermute(value, axis, [(source, source ^ bit) for source in range(cou...  140 us
    reduce_scatter x3, waiting for transfers between devices, reduce_rec(): lax.psum_scatter(contract_rows(left, right).astype(bf16), ('seq', 'dp'),...  136 us
    all_gather x3, waiting for transfers between devices, on_device(): lax.all_gather(mlp_rows[k], 'seq', axis=0, tiled=True)  121 us
    psum x1, blocking collectives, on_device(): lax.psum((grad_gate_a, grad_gate_i, sums, jnp.sum(grad_acts * normed, axi...  63.1 us
    dot_general x15, matrix products, matmul(): return jnp.dot(left, right, preferred_element_type=f32)  62 us
    dot_general x6, matrix products, contract_rows(): lax.dot_general(left, right, (((0,), (0,)), ((), ())), preferred_element_...  49.6 us
    pallas_call x1, Pallas kernels, rec_backward(): pl.pallas_call(functools.partial(rec_backward_kernel, nseq, heads, block)...  49 us
  transfers between devices with their start and end apart: 59, of which 28 were waited for; matrix products, arithmetic and copies ran while one was open for 26% of the time, Pallas kernels for 3%

profile of v1, /device:TPU:0, one launch (start us, length us, event | category | flops | bytes accessed | tf_op | source)
XLA Modules:
  0.0 1193.1 jit_solution(10829096624457350677)
XLA Ops:
  13.3 40.0 %all_to_all.24 = bf16[3,128,4,768]{1,3,0,2:T(8,128)(2,1)} all-to-all(bf16[3,128,4,768]{1,3,0,2:T(8,128)(2,1)S(1)} %copy.89), channel_id=1, replica_groups=mesh['dp'=4,'seq'=4,'mp'=2] {'dp'}, dimensions={2} | all-to-all | bytes 4718592 | tf_op jit(solution)/shard_map/all_to_all | solution.py:485
  132.0 10.4 all-gather.7.cloned.1.call-done
  151.0 41.3 %rec_forward.1 = (bf16[512,1280]{1,0:T(8,128)(2,1)}, f32[520,1280]{1,0:T(8,128)}, f32[520,1280]{1,0:T(8,128)}, f32[512,1280]{1,0:T(8,128)}, f32[512,1280]{1,0:T(8,128)}, /*index=5*/f32[512,1280]{1,0:T(8,128)}) custom-call(f32[512,1280]{1,0:T(8,128)} %fusion.121.px_ref, f32[512,1280]{1,0:T(8,128)} %fusion.122.py_ref, ...), custom_call_target="tpu_custom_call" | custom-call | tf_op jit(solution)/shard_map/rec_forward/pallas_call | solution.py:232
  192.3 7.9 all-gather.11.cloned.1.call-done
  222.4 8.4 collective-permute-done.6
  231.7 11.8 collective-permute-done.1
  246.4 9.0 collective-permute-done.18
  270.8 58.1 %all-gather.13.cloned.1.call-done = bf16[2048,768]{1,0:T(8,128)(2,1)} async-done(((bf16[512,768]{1,0:T(8,128)(2,1)}), bf16[2048,768]{1,0:T(8,128)(2,1)}) %all-gather.13.cloned.1.call-update) | async-done | bytes 3145744 | tf_op jit(solution)/shard_map/all_gather | solution.py:491
  334.5 58.1 %all-gather.17.cloned.1.call-done = bf16[2048,768]{1,0:T(8,128)(2,1)} async-done(((bf16[512,768]{1,0:T(8,128)(2,1)}), bf16[2048,768]{1,0:T(8,128)(2,1)}) %all-gather.17.cloned.1.call-update) | async-done | bytes 3145744 | tf_op jit(solution)/shard_map/all_gather | solution.py:491
  435.5 10.8 collective-permute-done.13
  475.1 10.8 collective-permute-done.19
  517.2 12.6 %collective-permute-done.42 = bf16[128,2048]{1,0:T(8,128)(2,1)S(1)} collective-permute-done((bf16[128,2048]{1,0:T(8,128)(2,1)S(1)}, bf16[128,2048]{1,0:T(8,128)(2,1)S(1)}, u32[]{:S(2)}, u32[]{:S(2)}) %collective-permute-start.42) | collective-permute-done | bytes 524320 | tf_op jit(solution)/shard_map/ppermute | solution.py:23
  544.6 32.3 %collective-permute-done.38 = bf16[128,2048]{1,0:T(8,128)(2,1)S(1)} collective-permute-done((bf16[128,2048]{1,0:T(8,128)(2,1)S(1)}, bf16[128,2048]{1,0:T(8,128)(2,1)S(1)}, u32[]{:S(2)}, u32[]{:S(2)}) %collective-permute-start.38) | collective-permute-done | bytes 524320 | tf_op jit(solution)/shard_map/ppermute | solution.py:23
  592.6 49.0 %rec_backward.1 = (bf16[512,1280]{1,0:T(8,128)(2,1)}, bf16[512,1280]{1,0:T(8,128)(2,1)}, f32[5,256,256]{2,1,0:T(8,128)}, f32[5,256,256]{2,1,0:T(8,128)}, f32[8,1280]{1,0:T(8,128)}) custom-call(f32[512,1280]{1,0:T(8,128)} %fusion.115.gm_ref, f32[512,1280]{1,0:T(8,128)} %fusion.122.py_ref, f32[520,1280]{1,0:T(8,128)} %get-tuple-element.29.states_ref, ...), custom_call_target="tpu_custom_call" | custom-call | tf_op jit(solution)/shard_map/rec_backward/pallas_call | solution.py:411
  641.7 10.9 convolution_convert_fusion.5
  654.0 11.1 convolution_convert_fusion.4
  675.1 8.5 convolution_convert_fusion.3
  728.5 11.4 all-reduce.4.cloned.1.call-done
  739.9 62.0 %reduce-scatter.13.cloned.1.call-done = bf16[512,768]{1,0:T(8,128)(2,1)} async-done(((bf16[2048,768]{1,0:T(8,128)(2,1)}), bf16[512,768]{1,0:T(8,128)(2,1)}) %reduce-scatter.13.cloned.1.call-update) | async-done | bytes 786448 | tf_op jit(solution)/shard_map/reduce_scatter | solution.py:537
  801.9 62.6 %reduce-scatter.15.cloned.1.call-done = bf16[512,768]{1,0:T(8,128)(2,1)} async-done(((bf16[2048,768]{1,0:T(8,128)(2,1)}), bf16[512,768]{1,0:T(8,128)(2,1)}) %reduce-scatter.15.cloned.1.call-update) | async-done | bytes 786448 | tf_op jit(solution)/shard_map/reduce_scatter | solution.py:537
  864.5 62.5 %reduce-scatter.17.cloned.1.call-done = bf16[512,768]{1,0:T(8,128)(2,1)} async-done(((bf16[2048,768]{1,0:T(8,128)(2,1)}), bf16[512,768]{1,0:T(8,128)(2,1)}) %reduce-scatter.17.cloned.1.call-update) | async-done | bytes 786448 | tf_op jit(solution)/shard_map/reduce_scatter | solution.py:537
  941.6 63.1 %all-reduce = (f32[2048]{0:T(1024)}, f32[8,1280]{1,0:T(8,128)S(1)}, f32[2048]{0:T(1024)}) all-reduce(f32[2048]{0:T(1024)S(1)} %bitcast.144, f32[8,1280]{1,0:T(8,128)S(1)} %copy-done.44, f32[2048]{0:T(1024)S(1)} %bitcast.143), channel_id=1, replica_groups=mesh['dp'=4,'seq'=4,'mp'=2] {'dp','seq'}, use_global_device_ids=true, to_apply=%region_14.15 | all-reduce | flops 14336 | bytes 114688 | tf_op jit(solution)/shard_map/psum | solution.py:568
  1044.3 56.8 %reduce-scatter.7.cloned.1.call-done = bf16[128,1280]{1,0:T(8,128)(2,1)} async-done(((bf16[2048,1280]{1,0:T(8,128)(2,1)}), bf16[128,1280]{1,0:T(8,128)(2,1)}) %reduce-scatter.7.cloned.1.call-update) | async-done | bytes 327696 | tf_op jit(solution)/shard_map/reduce_scatter | solution.py:561
  1103.0 79.5 %reduce-scatter.9.cloned.1.call-done = bf16[128,1280]{1,0:T(8,128)(2,1)} async-done(((bf16[2048,1280]{1,0:T(8,128)(2,1)}), bf16[128,1280]{1,0:T(8,128)(2,1)}) %reduce-scatter.9.cloned.1.call-update) | async-done | bytes 327696 | tf_op jit(solution)/shard_map/reduce_scatter | solution.py:561
  (471 shorter events, 388.3 us)
Async XLA Ops:
  7.2 117.0 %all-gather.9.cloned.1.call-start = ((), (), s32[]{:S(2)}) async-start(), calls=%async_computation.9 | async-start | bytes 5570560 | tf_op jit(solution)/shard_map/all_gather | solution.py:458
  7.9 134.5 %all-gather.7.cloned.1.call-start = ((), (), s32[]{:S(2)}) async-start(), calls=%async_computation.8 | async-start | bytes 5570560 | tf_op jit(solution)/shard_map/all_gather | solution.py:458
  8.7 191.5 %all-gather.11.cloned.1.call-start = ((), (), s32[]{:S(2)}) async-start(), calls=%async_computation.10 | async-start | bytes 5570560 | tf_op jit(solution)/shard_map/all_gather | solution.py:458
  9.4 256.0 %all-gather.15.cloned.1.call-start = ((), (), s32[]{:S(2)}) async-start(), calls=%async_computation.12 | async-start | bytes 3932160 | tf_op jit(solution)/shard_map/all_gather | solution.py:491
  57.7 271.3 %all-gather.13.cloned.1.call-start = ((), (), s32[]{:S(2)}) async-start(), calls=%async_computation.11 | async-start | bytes 3932160 | tf_op jit(solution)/shard_map/all_gather | solution.py:491
  58.3 334.3 %all-gather.17.cloned.1.call-start = ((), (), s32[]{:S(2)}) async-start(), calls=%async_computation.13 | async-start | bytes 3932160 | tf_op jit(solution)/shard_map/all_gather | solution.py:491
  66.7 43.1 %collective-permute-start.39 = (bf16[128,2048]{1,0:T(8,128)(2,1)S(1)}, bf16[128,2048]{1,0:T(8,128)(2,1)}, u32[]{:S(2)}, u32[]{:S(2)}) collective-permute-start(bf16[128,2048]{1,0:T(8,128)(2,1)S(1)} %slice.249), channel_id=1, source_target_pairs={{0,16},{8,24},{16,0},{24,8},{1,17},{9,25},{17,1},{25,9},{2,18},{10... | collective-permute-start | bytes 1572872 | tf_op jit(solution)/shard_map/ppermute | solution.py:23
  73.2 48.4 %collective-permute-start.29 = (bf16[128,2048]{1,0:T(8,128)(2,1)}, bf16[128,2048]{1,0:T(8,128)(2,1)}, u32[]{:S(2)}, u32[]{:S(2)}) collective-permute-start(bf16[128,2048]{1,0:T(8,128)(2,1)} %slice.237), channel_id=1, source_target_pairs={{0,16},{8,24},{16,0},{24,8},{1,17},{9,25},{17,1},{25,9},{2,18},{10... | collective-permute-start | bytes 1572872 | tf_op jit(solution)/shard_map/ppermute | solution.py:23
  109.7 348.8 %collective-permute-start.35 = (bf16[256,2048]{1,0:T(8,128)(2,1)}, bf16[256,2048]{1,0:T(8,128)(2,1)}, u32[]{:S(2)}, u32[]{:S(2)}) collective-permute-start(bf16[256,2048]{1,0:T(8,128)(2,1)} %pad_maximum_fusion.14), channel_id=1, source_target_pairs={{0,8},{8,0},{16,24},{24,16},{1,9},{9,1},{17,25},{25,17},{2,10},{10... | collective-permute-start | bytes 3145736 | tf_op jit(solution)/shard_map/ppermute | solution.py:23
  111.9 383.2 %collective-permute-start.40 = (bf16[256,2048]{1,0:T(8,128)(2,1)}, bf16[256,2048]{1,0:T(8,128)(2,1)}, u32[]{:S(2)}, u32[]{:S(2)}) collective-permute-start(bf16[256,2048]{1,0:T(8,128)(2,1)} %pad_maximum_fusion.15), channel_id=1, source_target_pairs={{0,8},{8,0},{16,24},{24,16},{1,9},{9,1},{17,25},{25,17},{2,10},{10... | collective-permute-start | bytes 3145736 | tf_op jit(solution)/shard_map/ppermute | solution.py:23
  114.5 219.9 %collective-permute-start.25 = (bf16[256,2048]{1,0:T(8,128)(2,1)}, bf16[256,2048]{1,0:T(8,128)(2,1)}, u32[]{:S(2)}, u32[]{:S(2)}) collective-permute-start(bf16[256,2048]{1,0:T(8,128)(2,1)} %pad_maximum_fusion.12), channel_id=1, source_target_pairs={{0,8},{8,0},{16,24},{24,16},{1,9},{9,1},{17,25},{25,17},{2,10},{10... | collective-permute-start | bytes 3145736 | tf_op jit(solution)/shard_map/ppermute | solution.py:23
  123.8 616.1 %all-reduce.4.cloned.1.call-start = ((), (), s32[]{:S(2)}) async-start(), calls=%async_computation.20 | async-start | bytes 5242880 | tf_op jit(solution)/shard_map/psum | solution.py:568
  259.9 145.6 %collective-permute-start.7 = (bf16[128,2048]{1,0:T(8,128)(2,1)}, bf16[128,2048]{1,0:T(8,128)(2,1)}, u32[]{:S(2)}, u32[]{:S(2)}) collective-permute-start(bf16[128,2048]{1,0:T(8,128)(2,1)} %get-tuple-element.63), channel_id=1, source_target_pairs={{0,16},{8,24},{16,0},{24,8},{1,17},{9,25},{17,1},{25,9},{2,18},{10... | collective-permute-start | bytes 1572872 | tf_op jit(solution)/shard_map/ppermute | solution.py:23
  446.3 96.7 %collective-permute-start.5 = (bf16[128,2048]{1,0:T(8,128)(2,1)S(1)}, bf16[128,2048]{1,0:T(8,128)(2,1)S(1)}, u32[]{:S(2)}, u32[]{:S(2)}) collective-permute-start(bf16[128,2048]{1,0:T(8,128)(2,1)S(1)} %slice_add_fusion.15), channel_id=1, source_target_pairs={{0,1},{1,0},{2,3},{3,2},{4,5},{5,4},{6,7},{7,6},{8,9},{9,8},{10,11... | collective-permute-start | bytes 1572872 | tf_op jit(solution)/shard_map/ppermute | solution.py:23
  485.8 54.3 %collective-permute-start.28 = (bf16[128,2048]{1,0:T(8,128)(2,1)S(1)}, bf16[128,2048]{1,0:T(8,128)(2,1)S(1)}, u32[]{:S(2)}, u32[]{:S(2)}) collective-permute-start(bf16[128,2048]{1,0:T(8,128)(2,1)S(1)} %slice_add_fusion.11), channel_id=1, source_target_pairs={{0,1},{1,0},{2,3},{3,2},{4,5},{5,4},{6,7},{7,6},{8,9},{9,8},{10,11... | collective-permute-start | bytes 1572872 | tf_op jit(solution)/shard_map/ppermute | solution.py:23
  543.0 42.6 %collective-permute-start.23 = (bf16[128,2048]{1,0:T(8,128)(2,1)S(1)}, bf16[128,2048]{1,0:T(8,128)(2,1)S(1)}, u32[]{:S(2)}, u32[]{:S(2)}) collective-permute-start(bf16[128,2048]{1,0:T(8,128)(2,1)S(1)} %slice_add_fusion.12), channel_id=1, source_target_pairs={{0,1},{1,0},{2,3},{3,2},{4,5},{5,4},{6,7},{7,6},{8,9},{9,8},{10,11... | collective-permute-start | bytes 1572872 | tf_op jit(solution)/shard_map/ppermute | solution.py:23
  641.6 160.3 %reduce-scatter.13.cloned.1.call-start = ((), (), s32[]{:S(2)}) async-start(), calls=%async_computation.17 | async-start | bytes 3932160 | tf_op jit(solution)/shard_map/reduce_scatter | solution.py:537
  652.6 211.9 %reduce-scatter.15.cloned.1.call-start = ((), (), s32[]{:S(2)}) async-start(), calls=%async_computation.18 | async-start | bytes 3932160 | tf_op jit(solution)/shard_map/reduce_scatter | solution.py:537
  665.1 261.9 %reduce-scatter.17.cloned.1.call-start = ((), (), s32[]{:S(2)}) async-start(), calls=%async_computation.19 | async-start | bytes 3932160 | tf_op jit(solution)/shard_map/reduce_scatter | solution.py:537
  683.7 358.7 %reduce-scatter.11.cloned.1.call-start = ((), (), s32[]{:S(2)}) async-start(), calls=%async_computation.16 | async-start | bytes 5570560 | tf_op jit(solution)/shard_map/reduce_scatter | solution.py:561
  692.1 409.1 %reduce-scatter.7.cloned.1.call-start = ((), (), s32[]{:S(2)}) async-start(), calls=%async_computation.14 | async-start | bytes 5570560 | tf_op jit(solution)/shard_map/reduce_scatter | solution.py:561
  700.1 482.4 %reduce-scatter.9.cloned.1.call-start = ((), (), s32[]{:S(2)}) async-start(), calls=%async_computation.15 | async-start | bytes 5570560 | tf_op jit(solution)/shard_map/reduce_scatter | solution.py:561
  719.5 216.9 %collective-permute-start.44 = (bf16[512,2048]{1,0:T(8,128)(2,1)}, bf16[512,2048]{1,0:T(8,128)(2,1)}, u32[]{:S(2)}, u32[]{:S(2)}) collective-permute-start(bf16[512,2048]{1,0:T(8,128)(2,1)} %add_convert_fusion), channel_id=1, source_target_pairs={{0,1},{1,0},{2,3},{3,2},{4,5},{5,4},{6,7},{7,6},{8,9},{9,8},{10,11... | collective-permute-start | bytes 6291464 | tf_op jit(solution)/shard_map/ppermute | solution.py:23
  932.5 98.0 %all-to-all-start.1 = ((bf16[3,512,768]{2,0,1:T(4,128)(2,1)}), bf16[3,512,768]{2,0,1:T(4,128)(2,1)S(1)}, u32[]{:S(2)}, u32[]{:S(2)}) async-start(bf16[3,512,768]{2,0,1:T(4,128)(2,1)} %copy.96), calls=%async_computation.7 | async-start | bytes 6291456 | tf_op jit(solution)/shard_map/all_to_all | solution.py:545
  (118 other events, 1710.2 us)
Sparse Core Ops, SparseCore 0:
  10.3 65.8 all-gather.8
  78.5 63.8 all-gather.6
  144.7 55.4 all-gather.10
  201.6 63.7 all-gather.14
  266.8 62.1 all-gather.12
  330.4 62.1 all-gather.16
  641.8 98.0 all-reduce.3
  742.2 59.6 reduce-scatter.12
  804.2 60.2 reduce-scatter.14
  866.7 60.2 reduce-scatter.16
  930.9 89.0 reduce-scatter.10
  1023.7 77.3 reduce-scatter.6
  1105.0 77.3 reduce-scatter.8

commit v2 on v1

v2 whole, which is shorter than its diff:
```python
import functools

import jax
import jax.numpy as jnp
from jax import lax
from jax.experimental import pallas as pl
from jax.experimental.pallas import tpu as pltpu
from jax.sharding import PartitionSpec as P

epsilon = 1e-06
decay_scale = 8.0
MESH = pl.DeviceIdType.MESH
VMEM_LIMIT = 60 * 2**20
SEGMENTS = 8
PAD = 8
bf16 = jnp.bfloat16
f32 = jnp.float32


def xor_permute(value, axis, bit):
    count = lax.axis_size(axis)
    return lax.ppermute(value, axis, [(source, source ^ bit) for source in range(count)])


def matmul(left, right):
    return jnp.dot(left, right, preferred_element_type=f32)


def contract(left, right):
    return lax.dot_general(left, right, (((1,), (1,)), ((), ())), preferred_element_type=f32)


def contract_rows(left, right):
    return lax.dot_general(left, right, (((0,), (0,)), ((), ())), preferred_element_type=f32)


def norm_scale(values):
    return lax.rsqrt(jnp.mean(values * values, axis=-1, keepdims=True) + epsilon)


def gelu_parts(y):
    c = 0.7978845608028654
    u = c * (y + 0.044715 * y * y * y)
    t = jnp.tanh(u)
    half = 0.5 * (1.0 + t)
    slope = half + 0.5 * y * (1.0 - t * t) * (c * (1.0 + 3.0 * 0.044715 * y * y))
    return y * half, slope


def one_minus_square(log_decay, decay):
    y = -2.0 * log_decay
    series = 1.0 - y * (1.0 / 5.0)
    for k in (4, 3, 2):
        series = 1.0 - y * (1.0 / k) * series
    return jnp.where(y < 0.1, y * series, 1.0 - decay * decay)


def seq_barrier(nseq):
    dp, z, mp = (lax.axis_index(a) for a in ("dp", "seq", "mp"))
    barrier = pltpu.get_barrier_semaphore()
    for step in range(1, nseq):
        pl.semaphore_signal(
            barrier, inc=1, device_id=(dp, lax.rem(z + step, nseq), mp), device_id_type=MESH
        )
    pl.semaphore_wait(barrier, nseq - 1)


def to_seq(src, dst, send_sem, recv_sem, target):
    dp, mp = (lax.axis_index(a) for a in ("dp", "mp"))
    return pltpu.make_async_remote_copy(
        src_ref=src,
        dst_ref=dst,
        send_sem=send_sem,
        recv_sem=recv_sem,
        device_id=(dp, target, mp),
        device_id_type=MESH,
    )


LANES = 128


def spread_lanes(value, width):
    return jnp.concatenate([value] * (width // value.shape[1]), axis=1)


def rec_forward_kernel(
    nseq, heads, block,
    acts_ref, wx_ref, wy_ref, marks_ref, ga_ref, gi_ref, vec_ref,
    mixed_ref, states_out, pxe_out, py_out, rate_out, ig_out, co_out,
    wy_s, states_s, pxe_s, py_s, rate_s, ig_s, co_s,
    a_s, b_s, tail_s, msg, got, state_in, halo, load_sem, store_sems, halo_send, halo_recv, end_send, end_recv,
):
    rows, width = mixed_ref.shape
    seg = rows // SEGMENTS
    z = lax.axis_index("seq")
    load = pltpu.make_async_copy(wy_ref, wy_s, load_sem)
    load.start()
    seq_barrier(nseq)

    def store(k, source, target):
        return pltpu.make_async_copy(source, target, store_sems.at[k])

    pairs = (
        (py_s, py_out), (pxe_s, pxe_out), (rate_s, rate_out), (ig_s, ig_out), (co_s, co_out), (states_s, states_out),
    )

    def block_cols(h):
        return pl.ds(pl.multiple_of(h * block, block), block)

    def project_x(h, _):
        product = matmul(acts_ref[...], wx_ref[:, block_cols(h)])
        pxe_s[pl.ds(PAD, rows), block_cols(h)] = product.astype(bf16).astype(f32)
        return 0

    lax.fori_loop(0, heads, project_x, 0)
    tail_s[...] = pxe_s[pl.ds(rows, PAD), :]

    def halo_copy(target):
        return to_seq(tail_s, halo, halo_send, halo_recv, target)

    @pl.when(z < nseq - 1)
    def _():
        halo_copy(z + 1).start()

    load.wait()

    def project_y(h, _):
        py_s[:, block_cols(h)] = matmul(acts_ref[...], wy_s[:, block_cols(h)])
        return 0

    lax.fori_loop(0, heads, project_y, 0)
    store(0, *pairs[0]).start()

    @pl.when(z == 0)
    def _():
        halo[...] = jnp.zeros_like(halo)

    @pl.when(z > 0)
    def _():
        halo_copy(z).wait_recv()

    pxe_s[pl.ds(0, PAD), :] = halo[...]
    store(1, *pairs[1]).start()

    def head(h, _):
        cols = block_cols(h)

        def part(r, _):
            at = pl.ds(pl.multiple_of(r * seg, seg), seg)
            window = pxe_s[pl.ds(pl.multiple_of(r * seg, seg), seg + PAD), cols]
            conv_out = vec_ref[4:5, cols] + vec_ref[0:1, cols] * window[PAD:]
            for lag in (1, 2, 3):
                shifted = pltpu.roll(window, lag, 0)[PAD:]
                conv_out = conv_out + vec_ref[lag : lag + 1, cols] * shifted * spread_lanes(marks_ref[lag, at, :], block)
            low = conv_out.astype(bf16)
            gate_r = matmul(low, ga_ref[h])
            gate_x = matmul(low, gi_ref[h])
            rate = jax.nn.sigmoid(gate_r + vec_ref[5:6, cols])
            ig = jax.nn.sigmoid(gate_x + vec_ref[6:7, cols])
            log_decay = -decay_scale * rate * vec_ref[7:8, cols]
            decay = jnp.exp(log_decay)
            mult = jnp.sqrt(one_minus_square(log_decay, decay))
            a_s[at, cols] = decay * spread_lanes(marks_ref[0, at, :], block)
            b_s[at, cols] = conv_out * ig * mult
            rate_s[at, cols] = rate
            ig_s[at, cols] = ig
            co_s[at, cols] = conv_out
            return 0

        lax.fori_loop(0, SEGMENTS, part, 0)
        return 0

    lax.fori_loop(0, heads, head, 0)
    for k in (2, 3, 4):
        store(k, *pairs[k]).start()
    row = lax.broadcasted_iota(jnp.int32, (8, width), 0)

    def turn(t, kept):
        prefix, state = kept
        at = pl.ds(pl.multiple_of(t * 8, 8), 8)
        decay, drive = a_s[at, :], b_s[at, :]
        for k in (1, 2, 4):
            inside = row >= k
            drive = decay * jnp.where(inside, pltpu.roll(drive, k, 0), 0.0) + drive
            decay = decay * jnp.where(inside, pltpu.roll(decay, k, 0), 1.0)
        drive = decay * state + drive
        decay = decay * prefix
        a_s[at, :] = decay
        b_s[at, :] = drive
        return decay[7:8], drive[7:8]

    one, zero = jnp.ones((1, width), f32), jnp.zeros((1, width), f32)
    prefix, state = lax.fori_loop(0, rows // 8, turn, (one, zero))
    msg[0:1, :] = prefix
    msg[1:2, :] = state
    msg[2:PAD, :] = jnp.zeros((PAD - 2, width), f32)
    for step in range(1, nseq):

        @pl.when(z + step < nseq)
        def _():
            to_seq(msg, got.at[z], end_send.at[step - 1], end_recv.at[z], z + step).start()

    state_in[...] = jnp.zeros_like(state_in)
    for source in range(nseq - 1):

        @pl.when(source < z)
        def _():
            to_seq(msg, got.at[source], end_send.at[0], end_recv.at[source], z).wait_recv()
            state_in[...] = got[source, 0:1, :] * state_in[...] + got[source, 1:2, :]

    states_s[pl.ds(0, PAD), :] = jnp.broadcast_to(state_in[...], (PAD, width))

    def finish(i, _):
        s, h = i // heads, lax.rem(i, heads)
        cols = block_cols(h)
        at = pl.ds(pl.multiple_of(s * seg, seg), seg)
        states = b_s[at, cols] + a_s[at, cols] * state_in[:, cols]
        states_s[pl.ds(pl.multiple_of(PAD + s * seg, PAD), seg), cols] = states
        mixed_ref[at, cols] = (states * gelu_parts(py_s[at, cols])[0]).astype(bf16)
        return 0

    lax.fori_loop(0, SEGMENTS * heads, finish, 0)
    store(5, *pairs[5]).start()

    @pl.when(z < nseq - 1)
    def _():
        halo_copy(z).wait_send()

    for step in range(1, nseq):

        @pl.when(z + step < nseq)
        def _():
            to_seq(msg, got.at[z], end_send.at[step - 1], end_recv.at[z], z).wait_send()

    for k, pair in enumerate(pairs):
        store(k, *pair).wait()


def rec_forward(nseq, acts, all_x, all_y, marks, gate_a, gate_i, vectors):
    rows, width = acts.shape[0], all_x.shape[1]
    heads, block = gate_a.shape[:2]
    vmem, anywhere = pl.BlockSpec(memory_space=pltpu.VMEM), pl.BlockSpec(memory_space=pl.ANY)
    big, ext = (rows, width), (rows + PAD, width)
    kept = (ext, ext, big, big, big, big)
    small = pltpu.VMEM((PAD, width), f32)
    dma = pltpu.SemaphoreType.DMA
    return pl.pallas_call(
        functools.partial(rec_forward_kernel, nseq, heads, block),
        out_shape=[jax.ShapeDtypeStruct(big, bf16)] + [jax.ShapeDtypeStruct(shape, f32) for shape in kept],
        in_specs=[vmem, vmem, anywhere] + [vmem] * 4,
        out_specs=[vmem] + [anywhere] * 6,
        scratch_shapes=[
            pltpu.VMEM(all_y.shape, bf16),
            *[pltpu.VMEM(shape, f32) for shape in kept],
            pltpu.VMEM(big, f32),
            pltpu.VMEM(big, f32),
            small,
            small,
            pltpu.VMEM((nseq, PAD, width), f32),
            pltpu.VMEM((1, width), f32),
            small,
            dma, dma((6,)), dma, dma, dma((nseq - 1,)), dma((nseq,)),
        ],
        compiler_params=pltpu.CompilerParams(
            collective_id=1, has_side_effects=True, vmem_limit_bytes=VMEM_LIMIT
        ),
        cost_estimate=cost(35),
        name="rec_forward",
    )(acts, all_x, all_y, marks, gate_a, gate_i, vectors)


def rec_backward_kernel(
    nseq, heads, block,
    low_ref, out_ref, marks_ref, ga_ref, gi_ref, vec_ref, py_ref, states_ref, rate_ref, pxe_ref, ig_ref, co_ref,
    gpy_ref, gpx_ref, gga_ref, ggi_ref, sums_ref,
    py_s, states_s, rate_s, pxe_s, ig_s, co_s, w_s, b_s, g_s, gm_s, gc_s, gr_s, gx_s,
    msg, got, grad_in, head_s, load_sems, halo_send, halo_recv, end_send, end_recv,
):
    rows, width = gpy_ref.shape
    seg = rows // SEGMENTS
    z = lax.axis_index("seq")
    loads = [
        pltpu.make_async_copy(source, target, load_sems.at[k])
        for k, (source, target) in enumerate(
            ((py_ref, py_s), (states_ref, states_s), (rate_ref, rate_s), (pxe_ref, pxe_s), (ig_ref, ig_s), (co_ref, co_s))
        )
    ]
    for load in loads:
        load.start()
    seq_barrier(nseq)
    for load in loads[:3]:
        load.wait()

    def block_cols(h):
        return pl.ds(pl.multiple_of(h * block, block), block)

    def first(h, _):
        cols = block_cols(h)
        gm_s[...] = matmul(low_ref[...], out_ref[:, cols])

        def part(s, _):
            at = pl.ds(pl.multiple_of(s * seg, seg), seg)
            gelu, slope = gelu_parts(py_s[at, cols])
            gm = gm_s[at, :]
            states = states_s[pl.ds(pl.multiple_of(PAD + s * seg, PAD), seg), cols]
            gpy_ref[at, cols] = (gm * states * slope).astype(bf16)
            decay = jnp.exp(-decay_scale * rate_s[at, cols] * vec_ref[7:8, cols])
            decay = decay * spread_lanes(marks_ref[0, at, :], block)
            grad = gm * gelu
            b_s[at, cols] = grad
            w_s[at, cols] = decay
            g_s[at, cols] = grad * decay
            return 0

        lax.fori_loop(0, SEGMENTS, part, 0)
        return 0

    lax.fori_loop(0, heads, first, 0)
    row = lax.broadcasted_iota(jnp.int32, (8, width), 0)

    def turn(i, kept):
        suffix, owed = kept
        at = pl.ds(pl.multiple_of(rows - 8 - i * 8, 8), 8)
        decay, grad = w_s[at, :], g_s[at, :]
        for k in (1, 2, 4):
            inside = row < 8 - k
            grad = decay * jnp.where(inside, pltpu.roll(grad, 8 - k, 0), 0.0) + grad
            decay = decay * jnp.where(inside, pltpu.roll(decay, 8 - k, 0), 1.0)
        grad = decay * owed + grad
        decay = decay * suffix
        w_s[at, :] = decay
        g_s[at, :] = grad
        return decay[0:1], grad[0:1]

    one, zero = jnp.ones((1, width), f32), jnp.zeros((1, width), f32)
    suffix, owed = lax.fori_loop(0, rows // 8, turn, (one, zero))
    w_s[pl.ds(rows, PAD), :] = jnp.ones((PAD, width), f32)
    g_s[pl.ds(rows, PAD), :] = jnp.zeros((PAD, width), f32)
    msg[0:1, :] = suffix
    msg[1:2, :] = owed
    msg[2:PAD, :] = jnp.zeros((PAD - 2, width), f32)
    for step in range(1, nseq):

        @pl.when(z >= step)
        def _():
            to_seq(msg, got.at[z], end_send.at[step - 1], end_recv.at[z], z - step).start()

    for load in loads[3:]:
        load.wait()
    grad_in[...] = jnp.zeros_like(grad_in)
    for source in range(nseq - 1, 0, -1):

        @pl.when(source > z)
        def _():
            to_seq(msg, got.at[source], end_send.at[0], end_recv.at[source], z).wait_recv()
            grad_in[...] = got[source, 0:1, :] * grad_in[...] + got[source, 1:2, :]

    def fold(value):
        return jnp.sum(value.reshape(seg // 8, 8, block), axis=0)

    def head(h, _):
        cols = block_cols(h)
        shrink = vec_ref[7:8, cols]

        def part(s, sums):
            at = pl.ds(pl.multiple_of(s * seg, seg), seg)
            ahead = pl.ds(pl.multiple_of(s * seg, seg), seg + PAD)
            owed = g_s[ahead, cols] + w_s[ahead, cols] * grad_in[:, cols]
            carry = b_s[at, cols] + pltpu.roll(owed, seg + PAD - 1, 0)[:seg]
            before = pltpu.roll(states_s[ahead, cols], 1, 0)[PAD:]
            rate, ig, conv_out = rate_s[at, cols], ig_s[at, cols], co_s[at, cols]
            log_decay = -decay_scale * rate * shrink
            decay = jnp.exp(log_decay)
            square = one_minus_square(log_decay, decay)
            inverse = lax.rsqrt(square)
            gated = carry * ig
            direct = gated * (square * inverse)
            gated = gated * conv_out
            keep = spread_lanes(marks_ref[0, at, :], block)
            grad_log = carry * before * decay * keep - gated * (decay * decay) * inverse
            spread = grad_log * decay_scale * rate
            grad_r = -spread * shrink * (1.0 - rate)
            grad_x = direct * conv_out * (1.0 - ig)
            low_r, low_x = grad_r.astype(bf16), grad_x.astype(bf16)
            gr_s[at, :] = low_r
            gx_s[at, :] = low_x
            grad_conv = direct + contract(low_r, ga_ref[h]) + contract(low_x, gi_ref[h])
            gc_s[at, cols] = grad_conv
            window = pxe_s[ahead, cols]
            terms = [grad_r, grad_x, spread, grad_conv, grad_conv * window[PAD:]]
            for lag in (1, 2, 3):
                terms.append(grad_conv * spread_lanes(marks_ref[lag, at, :], block) * pltpu.roll(window, lag, 0)[PAD:])
            return tuple(total + fold(term) for total, term in zip(sums, terms))

        sums = lax.fori_loop(
            0, SEGMENTS, part, tuple(jnp.zeros((8, block), f32) for _ in range(8))
        )
        for k, total in enumerate(sums):
            sums_ref[k : k + 1, cols] = jnp.sum(total, axis=0, keepdims=True)
        low = co_s[:, cols].astype(bf16)
        gga_ref[h] = contract_rows(low, gr_s[...])
        ggi_ref[h] = contract_rows(low, gx_s[...])
        return 0

    lax.fori_loop(0, heads, head, 0)
    head_s[...] = gc_s[pl.ds(0, PAD), :]

    @pl.when(z > 0)
    def _():
        to_seq(head_s, gc_s.at[pl.ds(rows, PAD)], halo_send, halo_recv, z - 1).start()

    @pl.when(z < nseq - 1)
    def _():
        to_seq(head_s, gc_s.at[pl.ds(rows, PAD)], halo_send, halo_recv, z).wait_recv()

    @pl.when(z == nseq - 1)
    def _():
        gc_s[pl.ds(rows, PAD), :] = jnp.zeros((PAD, width), f32)

    def final(i, _):
        s, h = i // heads, lax.rem(i, heads)
        cols = block_cols(h)
        at = pl.ds(pl.multiple_of(s * seg, seg), seg)
        ahead = pl.ds(pl.multiple_of(s * seg, seg), seg + PAD)
        owed = gc_s[ahead, cols]
        grad = vec_ref[0:1, cols] * owed[:seg]
        for lag in (1, 2, 3):
            shifted = owed * spread_lanes(marks_ref[lag, ahead, :], block)
            shifted = pltpu.roll(shifted, seg + PAD - lag, 0)[:seg]
            grad = grad + vec_ref[lag : lag + 1, cols] * shifted
        gpx_ref[at, cols] = grad.astype(bf16)
        return 0

    lax.fori_loop(0, SEGMENTS * heads, final, 0)

    @pl.when(z > 0)
    def _():
        to_seq(head_s, gc_s.at[pl.ds(rows, PAD)], halo_send, halo_recv, z).wait_send()

    for step in range(1, nseq):

        @pl.when(z >= step)
        def _():
            to_seq(msg, got.at[z], end_send.at[step - 1], end_recv.at[z], z).wait_send()


def rec_backward(nseq, low, all_out, marks, gate_a, gate_i, vectors, kept):
    rows, width = low.shape[0], all_out.shape[1]
    heads, block = gate_a.shape[:2]
    vmem, anywhere = pl.BlockSpec(memory_space=pltpu.VMEM), pl.BlockSpec(memory_space=pl.ANY)
    grads = jax.ShapeDtypeStruct((rows, width), bf16)
    gates = jax.ShapeDtypeStruct(gate_a.shape, f32)
    small = pltpu.VMEM((PAD, width), f32)
    ext = pltpu.VMEM((rows + PAD, width), f32)
    dma = pltpu.SemaphoreType.DMA
    return pl.pallas_call(
        functools.partial(rec_backward_kernel, nseq, heads, block),
        out_shape=(grads, grads, gates, gates, jax.ShapeDtypeStruct((8, width), f32)),
        in_specs=[vmem] * 6 + [anywhere] * len(kept),
        out_specs=[vmem] * 5,
        scratch_shapes=[
            *[pltpu.VMEM(k.shape, k.dtype) for k in kept],
            ext,
            pltpu.VMEM((rows, width), f32),
            ext,
            pltpu.VMEM((rows, block), f32),
            ext,
            pltpu.VMEM((rows, block), bf16),
            pltpu.VMEM((rows, block), bf16),
            small,
            pltpu.VMEM((nseq, PAD, width), f32),
            pltpu.VMEM((1, width), f32),
            small,
            dma((len(kept),)), dma, dma, dma((nseq - 1,)), dma((nseq,)),
        ],
        compiler_params=pltpu.CompilerParams(
            collective_id=2, has_side_effects=True, vmem_limit_bytes=VMEM_LIMIT
        ),
        cost_estimate=cost(45),
        name="rec_backward",
    )(low, all_out, marks, gate_a, gate_i, vectors, *kept)


def flip(index, mask):
    bit = 1
    while bit <= mask:
        if mask & bit:
            index = index + bit - 2 * bit * lax.rem(index // bit, 2)
        bit *= 2
    return index


def neighbour_barrier(ndp, nseq):
    dp, z, mp = (lax.axis_index(a) for a in ("dp", "seq", "mp"))
    barrier = pltpu.get_barrier_semaphore()

    def greet(target):
        pl.semaphore_signal(barrier, inc=1, device_id=target, device_id_type=MESH)

    for mask in range(1, ndp):
        greet((flip(dp, mask), z, mp))

    @pl.when(z > 0)
    def _():
        greet((dp, z - 1, mp))

    @pl.when(z < nseq - 1)
    def _():
        greet((dp, z + 1, mp))

    neighbours = lax.div(z + nseq - 1, nseq) + lax.div(2 * nseq - 2 - z, nseq)
    pl.semaphore_wait(barrier, ndp - 1 + neighbours)


class Copies:
    def __init__(self):
        self.sent = []

    def start(self, here, make):
        if here is None:
            make().start()
        else:

            @pl.when(here)
            def _():
                make().start()

        self.sent.append((here, make))

    def finish(self):
        for here, make in self.sent:
            if here is None:
                make().wait_send()
            else:

                @pl.when(here)
                def _():
                    make().wait_send()


def gather_kernel(ndp, nseq, side_first, split, *refs):
    count = len(side_first)
    shards, wide = refs[:count], refs[count : count + split]
    wholes, pieces = refs[count + split : 2 * count + split], refs[2 * count + split : 2 * (count + split)]
    local_sem, send, recv, piece_send, piece_recv = refs[2 * (count + split) :]
    dp, z, mp = (lax.axis_index(a) for a in ("dp", "seq", "mp"))
    rows = shards[0].shape[0]
    piece_cols = pieces[0].shape[1] if split else 0
    bits = [1 << k for k in range(1, ndp.bit_length() - 1)][::-1]
    copies = Copies()

    def valid(step):
        if step == 0:
            return None
        return z + step < nseq if step > 0 else z + step >= 0

    def copy(i, step, mask, there, mask_there, target):
        at = pl.ds(pl.multiple_of((flip(dp, mask) * nseq + z + step) * rows, rows), rows)
        index = (i, there + nseq - 1, mask_there)
        return pltpu.make_async_remote_copy(
            src_ref=shards[i] if step == 0 and mask == 0 and target is not None else wholes[i].at[at],
            dst_ref=wholes[i].at[at],
            send_sem=send.at[index],
            recv_sem=recv.at[index],
            device_id=(dp, z, mp) if target is None else target,
            device_id_type=MESH,
        )

    def along(i, step, mask):
        for way in (1, -1):
            if step * way > 0:
                continue
            near = z < nseq - 1 if way > 0 else z > 0
            here = near if step == 0 else near & valid(step)
            copies.start(
                here,
                functools.partial(copy, i, step, mask, step - way, mask, (dp, z + way, mp)),
            )

    def across(i, step, mask, bit):
        copies.start(
            valid(step),
            functools.partial(copy, i, step, mask, step, mask | bit, (flip(dp, bit), z, mp)),
        )

    def go_on(i, step, mask):
        if mask & 1:
            return
        lowest = mask & -mask if mask else ndp
        if side_first[i]:
            if step == 0:
                for bit in bits:
                    if bit < lowest:
                        across(i, step, mask, bit)
            along(i, step, mask)
        else:
            if mask == 0:
                along(i, step, mask)
            for bit in bits:
                if bit < lowest:
                    across(i, step, mask, bit)
        across(i, step, mask, 1)

    def arrive(i, step, mask):
        def wait():
            copy(i, step, mask, step, mask, None).wait_recv()

        if step == 0:
            wait()
        else:
            pl.when(valid(step))(wait)
        go_on(i, step, mask)

    def piece_copy(k, mask):
        cols = pl.ds(pl.multiple_of(flip(dp, mask) * piece_cols, LANES), piece_cols)
        src = wide[k].at[:, cols] if len(wide[k].shape) == 2 else wide[k].at[flip(dp, mask)]
        dst = pieces[k].at[pl.ds(pl.multiple_of(dp * rows, rows), rows)]
        if mask == 0:
            return pltpu.make_async_copy(src, dst, local_sem.at[count + k])
        return pltpu.make_async_remote_copy(
            src_ref=src, dst_ref=dst, send_sem=piece_send.at[k, mask], recv_sem=piece_recv.at[k, mask],
            device_id=(flip(dp, mask), z, mp), device_id_type=MESH,
        )

    def piece_arrived(k, mask):
        at = pl.ds(pl.multiple_of(flip(dp, mask) * rows, rows), rows)
        pltpu.make_async_remote_copy(
            src_ref=pieces[k].at[at], dst_ref=pieces[k].at[at], send_sem=piece_send.at[k, mask],
            recv_sem=piece_recv.at[k, mask], device_id=(dp, z, mp), device_id_type=MESH,
        ).wait_recv()

    neighbour_barrier(ndp, nseq)
    for i in range(count):
        here = pl.ds(pl.multiple_of((dp * nseq + z) * rows, rows), rows)
        pltpu.make_async_copy(shards[i], wholes[i].at[here], local_sem.at[i]).start()
    order = sorted(range(count), key=lambda i: not side_first[i])
    for i in order:
        go_on(i, 0, 0)
    masks = [0]
    for bit in bits:
        masks += [m | bit for m in masks]
    sides = masks[1:]
    first, last = [i for i in order if side_first[i]], [i for i in order if not side_first[i]]
    for i in first:
        for mask in sides:
            arrive(i, 0, mask)
    pieces_left = list(range(split))
    for step in range(1, nseq):
        if pieces_left:
            k = pieces_left.pop(0)
            for mask in range(ndp):
                piece_copy(k, mask).start()
        for i in order:
            arrive(i, -step, 0)
            arrive(i, step, 0)
        for i in last:
            for mask in sides:
                arrive(i, 1 - step, mask)
                if step > 1:
                    arrive(i, step - 1, mask)
        for i in first:
            for mask in sides:
                arrive(i, -step, mask)
                arrive(i, step, mask)
    for k in pieces_left:
        for mask in range(ndp):
            piece_copy(k, mask).start()
    for i in last:
        for mask in sides:
            arrive(i, 1 - nseq, mask)
            arrive(i, nseq - 1, mask)
    for i in range(count):
        for mask in masks:
            for step in range(1 - nseq, nseq):
                arrive(i, step, mask | 1)
    for k in range(split):
        for mask in range(1, ndp):
            piece_arrived(k, mask)
    for i in range(count):
        here = pl.ds(pl.multiple_of((dp * nseq + z) * rows, rows), rows)
        pltpu.make_async_copy(shards[i], wholes[i].at[here], local_sem.at[i]).wait()
    for k in range(split):
        piece_copy(k, 0).wait()
        for mask in range(1, ndp):
            piece_copy(k, mask).wait_send()
    copies.finish()


def gather_weights(ndp, nseq, shards, side_first, wide, number):
    rows = shards[0].shape[0]
    count, split = len(shards), len(wide)
    piece = wide[0].shape[1] // ndp if split else LANES
    if piece % LANES:
        wide = [jnp.swapaxes(w.reshape(rows, ndp, piece), 0, 1) for w in wide]
    dma = pltpu.SemaphoreType.DMA
    anywhere = pl.BlockSpec(memory_space=pl.ANY)
    return pl.pallas_call(
        functools.partial(gather_kernel, ndp, nseq, side_first, split),
        out_shape=[jax.ShapeDtypeStruct((ndp * nseq * rows, s.shape[1]), s.dtype) for s in shards]
        + [jax.ShapeDtypeStruct((ndp * rows, piece), w.dtype) for w in wide],
        in_specs=[anywhere] * (count + split),
        out_specs=[anywhere] * (count + split),
        scratch_shapes=[
            dma((count + split,)), dma((count, 2 * nseq - 1, ndp)), dma((count, 2 * nseq - 1, ndp)),
            dma((max(split, 1), ndp)), dma((max(split, 1), ndp)),
        ],
        compiler_params=pltpu.CompilerParams(collective_id=number, has_side_effects=True),
        name="gather_weights",
    )(*shards, *wide)


def reduce_kernel(ndp, nseq, kinds, *refs):
    lefts = max(kind[0] for kind in kinds if kind[0] is not None) + 1
    left_refs, refs = refs[:lefts], refs[lefts:]
    count = len(kinds)
    rights, outs = refs[:count], refs[count : 2 * count]
    buffers, refs = refs[2 * count : 9 * count], refs[9 * count :]
    core_out, core_in, side_out, side_in, flow_out, up_in, down_in = (
        buffers[k * count : (k + 1) * count] for k in range(7)
    )
    acc, core_sems, side_sems, flow_sems, up_sems, down_sems = refs
    dp, z, mp = (lax.axis_index(a) for a in ("dp", "seq", "mp"))
    evens = list(range(0, ndp, 2))
    bits = [1 << k for k in range(1, ndp.bit_length() - 1)][::-1]
    order = [s for k in range(nseq - 1, 0, -1) for s in (k, -k)] + [0]
    copies = Copies()
    me = (dp, z, mp)

    def valid(step):
        if step == 0:
            return None
        return z + step < nseq if step > 0 else z + step >= 0

    def under(here, body):
        if here is None:
            body()
        else:
            pl.when(here)(body)

    def remote(src, dst, send_sem, recv_sem, target):
        return pltpu.make_async_remote_copy(
            src_ref=src, dst_ref=dst, send_sem=send_sem, recv_sem=recv_sem,
            device_id=target, device_id_type=MESH,
        )

    def core(i, step, mask):
        at = (z + step, mask // 2)
        return remote(
            core_out[i].at[at], core_in[i].at[at], core_sems.at[(0, i, *at)], core_sems.at[(1, i, *at)],
            (flip(dp, 1), z, mp),
        )

    def side(i, step, mask, bit):
        at = (z + step, mask // 2 - 1)
        return remote(
            side_out[i].at[at], side_in[i].at[at], side_sems.at[(0, i, *at)], side_sems.at[(1, i, *at)],
            (flip(dp, bit), z, mp),
        )

    def flow(i, step, way):
        into, sems = (up_in, up_sems) if way > 0 else (down_in, down_sems)
        return remote(
            flow_out[i].at[z + step], into[i].at[z + step], flow_sems.at[i, z + step], sems.at[i, z + step],
            (dp, z + way, mp),
        )

    def product(i, step, mask):
        rows = kinds[i][2]
        start = pl.multiple_of((flip(dp, mask) * nseq + z + step) * rows, rows)
        left = kinds[i][0]
        if left is None:
            return rights[i][pl.ds(start, rows), :]
        return jnp.dot(left_refs[left][pl.ds(start, rows), :], rights[i][...], preferred_element_type=f32)

    def block(ref, i, step, *more):
        return ref[i][(z + step, *more)].astype(f32)

    def store(ref, value, i, step, *more):
        ref[i][(z + step, *more)] = value.astype(bf16)

    neighbour_barrier(ndp, nseq)
    for i in range(count):
        for step in order:

            def to_core():
                for mask in evens:
                    store(core_out, product(i, step, mask | 1), i, step, mask // 2)

            under(valid(step), to_core)
            for mask in evens:
                copies.start(valid(step), functools.partial(core, i, step, mask))
    for i in range(count):
        for step in order:
            for mask in evens[:0:-1]:
                bit = 1 << (mask.bit_length() - 1)

                def to_side():
                    core(i, step, mask).wait_recv()
                    total = product(i, step, mask) + block(core_in, i, step, mask // 2)
                    for more in bits:
                        if more > bit:
                            side(i, step, mask | more, more).wait_recv()
                            total = total + block(side_in, i, step, (mask | more) // 2 - 1)
                    store(side_out, total, i, step, mask // 2 - 1)

                under(valid(step), to_side)
                copies.start(valid(step), functools.partial(side, i, step, mask, bit))
    for i in range(count):
        spot = (pl.ds(0, kinds[i][2]), pl.ds(0, kinds[i][1]))
        for step in order:

            def to_flow():
                core(i, step, 0).wait_recv()
                acc[spot] = product(i, step, 0) + block(core_in, i, step, 0)
                for more in bits:
                    side(i, step, more, more).wait_recv()
                    acc[spot] += block(side_in, i, step, more // 2 - 1)

                def add(into, way):
                    flow(i, step, way).wait_recv()
                    acc[spot] += block(into, i, step)

                if step >= 0:
                    pl.when(z > 0)(lambda: add(up_in, 1))
                if step <= 0:
                    pl.when(z < nseq - 1)(lambda: add(down_in, -1))
                if step:
                    store(flow_out, acc[spot], i, step)
                else:
                    outs[i][...] = acc[spot]

            under(valid(step), to_flow)
            if step:
                copies.start(valid(step), functools.partial(flow, i, step, 1 if step > 0 else -1))
    copies.finish()


def reduce_weights(ndp, nseq, lefts, rights, number):
    blocks = ndp * nseq
    kinds = [(k, r.shape[1], (r if k is None else lefts[k].T).shape[0] // blocks) for k, r in rights]
    count, evens = len(rights), ndp // 2
    vmem = pl.BlockSpec(memory_space=pltpu.VMEM)
    dma = pltpu.SemaphoreType.DMA
    low = functools.partial(pltpu.VMEM, dtype=bf16)

    def buffers(*lead):
        return [low((nseq, *lead, rows, width)) for _, width, rows in kinds]

    return pl.pallas_call(
        functools.partial(reduce_kernel, ndp, nseq, kinds),
        out_shape=[jax.ShapeDtypeStruct((rows, width), f32) for _, width, rows in kinds],
        in_specs=[vmem] * (len(lefts) + count),
        out_specs=[vmem] * count,
        scratch_shapes=[
            *buffers(evens), *buffers(evens), *buffers(evens - 1), *buffers(evens - 1),
            *buffers(), *buffers(), *buffers(),
            pltpu.VMEM((max(kind[2] for kind in kinds), max(kind[1] for kind in kinds)), f32),
            dma((2, count, nseq, evens)), dma((2, count, nseq, evens)),
            dma((count, nseq)), dma((count, nseq)), dma((count, nseq)),
        ],
        compiler_params=pltpu.CompilerParams(
            collective_id=number, has_side_effects=True, vmem_limit_bytes=VMEM_LIMIT
        ),
        cost_estimate=cost(100),
        name="reduce_weights",
    )(*[left.T for left in lefts], *[r for _, r in rights])


PART = 64


def cost(us):
    return pl.CostEstimate(flops=int(us * 1e9), bytes_accessed=int(us * 1e5), transcendentals=0)


def peers_barrier(ndp):
    dp, z, mp = (lax.axis_index(a) for a in ("dp", "seq", "mp"))
    barrier = pltpu.get_barrier_semaphore()
    for mask in range(1, ndp):
        pl.semaphore_signal(barrier, inc=1, device_id=(flip(dp, mask), z, mp), device_id_type=MESH)
    pl.semaphore_signal(barrier, inc=1, device_id=(dp, z, 1 - mp), device_id_type=MESH)
    pl.semaphore_wait(barrier, ndp)


def doubling(ndp):
    bits = [1 << k for k in range(1, ndp.bit_length() - 1)][::-1]
    masks = [0]
    for bit in bits:
        masks += [mask | bit for mask in masks]
    return bits, masks


def enter_kernel(
    ndp, mixed_ref, out_ref, tokens_ref, gain_ref, *refs
):
    bits, masks = doubling(ndp)
    cots, refs = refs[: len(masks)], refs[len(masks) :]
    middle_ref, acts_ref, all_cots = refs[:3]
    mine, theirs, normed, mine_sem, theirs_sem, own_sem, send, recv, cot_own, cot_send, cot_recv = refs[3:]
    rows = mixed_ref.shape[0]
    parts = rows // PART
    dp, z, mp = (lax.axis_index(a) for a in ("dp", "seq", "mp"))
    peers_barrier(ndp)

    def at(c):
        return pl.ds(pl.multiple_of(c * PART, PART), PART)

    def exchange(c):
        return pltpu.make_async_remote_copy(
            src_ref=mine.at[at(c)], dst_ref=theirs.at[at(c)], send_sem=mine_sem.at[c], recv_sem=theirs_sem.at[c],
            device_id=(dp, z, 1 - mp), device_id_type=MESH,
        )

    def hand(c, mask, bit):
        return pltpu.make_async_remote_copy(
            src_ref=acts_ref.at[mask, at(c)] if mask else normed.at[at(c)],
            dst_ref=acts_ref.at[mask | bit, at(c)],
            send_sem=send.at[mask | bit, c],
            recv_sem=recv.at[mask | bit, c],
            device_id=(flip(dp, bit), z, mp),
            device_id_type=MESH,
        )

    def own(c):
        return pltpu.make_async_copy(normed.at[at(c)], acts_ref.at[0, at(c)], own_sem.at[c])

    def cot_copy(k):
        return pltpu.make_async_copy(cots[k], all_cots.at[masks[k]], cot_own.at[k])

    def cot_hand(k):
        return pltpu.make_async_remote_copy(
            src_ref=cots[k], dst_ref=all_cots.at[masks[k] | 1], send_sem=cot_send.at[k], recv_sem=cot_recv.at[k],
            device_id=(flip(dp, 1), z, mp), device_id_type=MESH,
        )

    def project(k, _):
        several = pl.ds(pl.multiple_of(k * 4 * PART, 4 * PART), 4 * PART)
        mine[several, :] = contract(mixed_ref[several, :], out_ref[...]).astype(bf16)
        for c in range(4):
            exchange(4 * k + c).start()
        return 0

    lax.fori_loop(0, parts // 4, project, 0)
    for k in range(len(masks)):
        cot_copy(k).start()
        cot_hand(k).start()

    def norm(c, _):
        exchange(c).wait_recv()
        both = mine[at(c), :].astype(f32) + theirs[at(c), :].astype(f32)
        middle = tokens_ref[at(c), :].astype(f32) + both
        middle_ref[at(c), :] = middle
        scale = lax.rsqrt(jnp.mean(middle * middle, axis=-1, keepdims=True) + epsilon)
        normed[at(c), :] = (middle * scale * gain_ref[...]).astype(bf16)
        own(c).start()
        for bit in bits + [1]:
            hand(c, 0, bit).start()
        return 0

    lax.fori_loop(0, parts, norm, 0)
    for mask in masks[1:]:

        def pass_on(c, _):
            hand(c, mask & (mask - 1), mask & -mask).wait_recv()
            for bit in bits + [1]:
                if bit < mask & -mask:
                    hand(c, mask, bit).start()
            return 0

        lax.fori_loop(0, parts, pass_on, 0)

    def finish(c, _):
        own(c).wait()
        exchange(c).wait_send()
        for mask in masks:
            hand(c, mask, 1).wait_recv()
            for bit in bits + [1]:
                if mask == 0 or bit < mask & -mask:
                    hand(c, mask, bit).wait_send()
        return 0

    lax.fori_loop(0, parts, finish, 0)
    for k in range(len(masks)):
        cot_copy(k).wait()
        cot_hand(k).wait()


def enter_mlp(ndp, mixed, all_out, tokens, gain, cots):
    rows, features = tokens.shape
    parts, count = rows // PART, len(cots)
    vmem, anywhere = pl.BlockSpec(memory_space=pltpu.VMEM), pl.BlockSpec(memory_space=pl.ANY)
    dma = pltpu.SemaphoreType.DMA
    everyone = jax.ShapeDtypeStruct((ndp, rows, features), bf16)
    low = pltpu.VMEM((rows, features), bf16)
    return pl.pallas_call(
        functools.partial(enter_kernel, ndp),
        out_shape=(jax.ShapeDtypeStruct((rows, features), f32), everyone, everyone),
        in_specs=[vmem] * (4 + count),
        out_specs=(vmem, anywhere, anywhere),
        scratch_shapes=[
            low, low, low, dma((parts,)), dma((parts,)), dma((parts,)), dma((ndp, parts)), dma((ndp, parts)),
            dma((count,)), dma((count,)), dma((count,)),
        ],
        compiler_params=pltpu.CompilerParams(
            collective_id=6, has_side_effects=True, vmem_limit_bytes=VMEM_LIMIT
        ),
        cost_estimate=cost(65),
        name="enter_mlp",
    )(mixed, all_out, tokens, gain, *cots)


def leave_kernel(
    ndp, cots_ref, to_gate_ref, to_up_ref, mixed_ref, gate_up_ref, down_ref, middle_ref, gain_ref,
    grads_ref, out_ref, grad_ref, low_ref, gain_out_ref,
    cot_s, to_gate_s, to_up_s, mixed_s, grads_s, out_s, grad_s, load_sem, grads_sem, out_sem, grad_sem,
    keep, core_out, core_in, side_out, side_in, mine, theirs, out_keep, out_core, out_core_in,
    core_sems, side_sems, mp_sems, out_sems,
):
    rows, features = middle_ref.shape
    piece = down_ref.shape[1]
    parts = rows // PART
    bits, masks = doubling(ndp)
    dp, z, mp = (lax.axis_index(a) for a in ("dp", "seq", "mp"))
    peers_barrier(ndp)

    def at(c):
        return pl.ds(pl.multiple_of(c * PART, PART), PART)

    def loads(c):
        slot = lax.rem(c, 2)
        pairs = ((cots_ref, cot_s), (to_gate_ref, to_gate_s), (to_up_ref, to_up_s), (mixed_ref, mixed_s))
        return [
            pltpu.make_async_copy(ref.at[:, at(c)], buffer.at[slot], load_sem.at[k, slot])
            for k, (ref, buffer) in enumerate(pairs)
        ]

    def store_grads(c):
        slot = lax.rem(c, 2)
        return pltpu.make_async_copy(grads_s.at[slot], grads_ref.at[:, at(c)], grads_sem.at[slot])

    def store_out(c):
        slot = lax.rem(c, 2)
        return pltpu.make_async_copy(out_s.at[slot], out_ref.at[:, at(c)], out_sem.at[slot])

    def store_grad(c):
        slot = lax.rem(c, 2)
        return pltpu.make_async_copy(grad_s.at[slot], grad_ref.at[at(c)], grad_sem.at[slot])

    def remote(src, dst, sems, index, target):
        return pltpu.make_async_remote_copy(
            src_ref=src, dst_ref=dst, send_sem=sems.at[(0, *index)], recv_sem=sems.at[(1, *index)],
            device_id=target, device_id_type=MESH,
        )

    def to_core(c):
        return remote(core_out.at[lax.rem(c, 2)], core_in.at[c], core_sems, (c,), (flip(dp, 1), z, mp))

    def out_to_core(c):
        return remote(out_core.at[lax.rem(c, 2)], out_core_in.at[c], out_sems, (c,), (flip(dp, 1), z, mp))

    def to_side(c, mask):
        bit = 1 << (mask.bit_length() - 1)
        k = mask // 2 - 1
        return remote(side_out.at[c, k], side_in.at[c, k], side_sems, (c, k), (flip(dp, bit), z, mp))

    def to_mp(c):
        return remote(mine.at[c], theirs.at[c], mp_sems, (c,), (dp, z, 1 - mp))

    for copy in loads(0):
        copy.start()
    gain_out_ref[...] = jnp.zeros_like(gain_out_ref)

    def compute(c):
        slot = lax.rem(c, 2)
        for copy in loads(c):
            copy.wait()

        @pl.when(c + 1 < parts)
        def _():
            for copy in loads(c + 1):
                copy.start()

        @pl.when(c >= 2)
        def _():
            store_grads(c - 2).wait()
            to_core(c - 2).wait_send()
            out_to_core(c - 2).wait_send()

        low_ref[at(c), :] = cot_s[slot, 0]
        grad_mixed = matmul(cot_s[slot].reshape(ndp * PART, features), down_ref[...]).reshape(ndp, PART, piece)
        grads_s[slot, :, :, :piece] = (grad_mixed * to_gate_s[slot].astype(f32)).astype(bf16)
        grads_s[slot, :, :, piece:] = (grad_mixed * to_up_s[slot].astype(f32)).astype(bf16)
        store_grads(c).start()
        total = contract(grads_s[slot].reshape(ndp * PART, 2 * piece), gate_up_ref[...])
        total = total.reshape(ndp, PART, features)
        for mask in range(0, ndp, 2):
            keep[lax.rem(c, 4), mask // 2] = total[mask]
            core_out[slot, mask // 2] = total[mask | 1].astype(bf16)
        to_core(c).start()
        total = contract(mixed_s[slot].reshape(ndp * PART, piece), down_ref[...])
        total = total.reshape(ndp, PART, features)
        for mask in range(0, ndp, 2):
            out_keep[slot, mask // 2] = total[mask]
            out_core[slot, mask // 2] = total[mask | 1].astype(bf16)
        out_to_core(c).start()

    def after_core(c):
        to_core(c).wait_recv()
        slot = lax.rem(c, 4)
        keep[slot, 0] += core_in[c, 0].astype(f32)
        for mask in range(ndp - 2, 0, -2):
            total = keep[slot, mask // 2] + core_in[c, mask // 2].astype(f32)
            bit = 1 << (mask.bit_length() - 1)
            for more in bits:
                if more > bit:
                    to_side(c, mask | more).wait_recv()
                    total = total + side_in[c, (mask | more) // 2 - 1].astype(f32)
            side_out[c, mask // 2 - 1] = total.astype(bf16)
            to_side(c, mask).start()

        @pl.when(c >= 2)
        def _():
            store_out(c - 2).wait()

        slot = lax.rem(c, 2)
        out_to_core(c).wait_recv()
        for k in range(ndp // 2):
            out_s[slot, k] = (out_keep[slot, k] + out_core_in[c, k].astype(f32)).astype(bf16)
        store_out(c).start()

    def after_side(c):
        total = keep[lax.rem(c, 4), 0]
        for bit in bits:
            to_side(c, bit).wait_recv()
            total = total + side_in[c, bit // 2 - 1].astype(f32)
        mine[c] = total.astype(bf16)
        to_mp(c).start()

    def after_mp(c):
        to_mp(c).wait_recv()

        @pl.when(c >= 2)
        def _():
            store_grad(c - 2).wait()

        grad = mine[c].astype(f32) + theirs[c].astype(f32)
        middle = middle_ref[at(c), :]
        scale = lax.rsqrt(jnp.mean(middle * middle, axis=-1, keepdims=True) + epsilon)
        normed = middle * scale
        grad_normed = grad * gain_ref[...]
        grad_middle = low_ref[at(c), :].astype(f32) + scale * (
            grad_normed - normed * jnp.mean(grad_normed * normed, axis=-1, keepdims=True)
        )
        grad_s[lax.rem(c, 2)] = grad_middle
        store_grad(c).start()
        low_ref[at(c), :] = grad_middle.astype(bf16)
        gain_out_ref[...] += jnp.sum((grad * normed).reshape(PART // 8, 8, features), axis=0)

    def turn(t, _):
        for lag, stage in ((0, compute), (1, after_core), (2, after_side), (4, after_mp)):
            pl.when((t >= lag) & (t < parts + lag))(functools.partial(stage, t - lag))
        return 0

    lax.fori_loop(0, parts + 4, turn, 0)
    for c in (parts - 2, parts - 1):
        store_grads(c).wait()
        store_out(c).wait()
        store_grad(c).wait()
        to_core(c).wait_send()
        out_to_core(c).wait_send()

    def finish(c, _):
        to_mp(c).wait_send()
        for mask in range(2, ndp, 2):
            to_side(c, mask).wait_send()
        return 0

    lax.fori_loop(0, parts, finish, 0)


def leave_mlp(ndp, cots, to_gate, to_up, mixed, gate_up, down, middle, gain):
    rows, features = middle.shape
    piece = down.shape[1]
    parts, evens = rows // PART, ndp // 2
    vmem, anywhere = pl.BlockSpec(memory_space=pltpu.VMEM), pl.BlockSpec(memory_space=pl.ANY)
    dma = pltpu.SemaphoreType.DMA
    low = functools.partial(pltpu.VMEM, dtype=bf16)
    thin = (parts, PART, features)
    return pl.pallas_call(
        functools.partial(leave_kernel, ndp),
        out_shape=(
            jax.ShapeDtypeStruct((ndp, rows, 2 * piece), bf16),
            jax.ShapeDtypeStruct((evens, rows, features), bf16),
            jax.ShapeDtypeStruct((rows, features), f32),
            jax.ShapeDtypeStruct((rows, features), bf16),
            jax.ShapeDtypeStruct((8, features), f32),
        ),
        in_specs=[anywhere] * 4 + [vmem] * 4,
        out_specs=(anywhere, anywhere, anywhere, vmem, vmem),
        scratch_shapes=[
            low((2, ndp, PART, features)),
            pltpu.VMEM((2, ndp, PART, piece), to_gate.dtype),
            pltpu.VMEM((2, ndp, PART, piece), to_up.dtype),
            low((2, ndp, PART, piece)),
            low((2, ndp, PART, 2 * piece)),
            low((2, evens, PART, features)),
            pltpu.VMEM((2, PART, features), f32),
            dma((4, 2)), dma((2,)), dma((2,)), dma((2,)),
            pltpu.VMEM((4, evens, PART, features), f32),
            low((2, evens, PART, features)), low((parts, evens, PART, features)),
            low((parts, evens - 1, PART, features)), low((parts, evens - 1, PART, features)),
            low(thin), low(thin),
            pltpu.VMEM((2, evens, PART, features), f32),
            low((2, evens, PART, features)), low((parts, evens, PART, features)),
            dma((2, parts)), dma((2, parts, evens - 1)), dma((2, parts)), dma((2, parts)),
        ],
        compiler_params=pltpu.CompilerParams(
            collective_id=7, has_side_effects=True, vmem_limit_bytes=VMEM_LIMIT
        ),
        cost_estimate=cost(75),
        name="leave_mlp",
    )(cots, to_gate, to_up, mixed, gate_up, down, middle, gain)


def everyone(ndp, values):
    masks = doubling(ndp)[1]
    by_mask = {}
    for mask, value in zip(masks, values):
        by_mask[mask], by_mask[mask | 1] = value, xor_permute(value, "dp", 1)
    return jnp.stack([by_mask[mask] for mask in range(ndp)])


def side_sum(ndp, value):
    return (value[0::2].astype(f32) + xor_permute(value[1::2], "dp", 1).astype(f32)).astype(bf16)


def halving(ndp, value, after=None):
    for bit in doubling(ndp)[0]:
        half = value.shape[0] // 2
        other = xor_permute(value[half:], "dp", bit)
        if after is not None:
            other, _ = lax.optimization_barrier((other, after))
        value = (value[:half].astype(f32) + other.astype(f32)).astype(bf16)
    return value[0]


def enter_mlp_plain(ndp, mixed, all_out, tokens, gain, cots):
    part = contract(mixed, all_out).astype(bf16)
    middle = tokens.astype(f32) + (part.astype(f32) + xor_permute(part, "mp", 1).astype(f32))
    normed = [(middle * norm_scale(middle) * gain).astype(bf16)]
    for bit in doubling(ndp)[0]:
        normed += [xor_permute(value, "dp", bit) for value in normed]
    return middle, everyone(ndp, normed), everyone(ndp, cots)


def leave_mlp_plain(ndp, cots, to_gate, to_up, mixed, gate_up, down, middle, gain):
    rows, features = middle.shape
    piece = down.shape[1]
    grad_mixed = matmul(cots.reshape(-1, features), down).reshape(ndp, rows, piece)
    grads = jnp.concatenate([grad_mixed * to_gate, grad_mixed * to_up], axis=-1).astype(bf16)
    total = contract(grads.reshape(-1, 2 * piece), gate_up).astype(bf16).reshape(ndp, rows, features)
    total = halving(ndp, side_sum(ndp, total))
    grad = total.astype(f32) + xor_permute(total, "mp", 1).astype(f32)
    scale = norm_scale(middle)
    normed, grad_normed = middle * scale, grad * gain
    grad_middle = cots[0].astype(f32) + scale * (
        grad_normed - normed * jnp.mean(grad_normed * normed, axis=-1, keepdims=True)
    )
    out = contract(mixed.reshape(-1, piece), down).astype(bf16).reshape(ndp, rows, features)
    gain_out = jnp.sum((grad * normed).reshape(rows // 8, 8, features), axis=0)
    return grads, side_sum(ndp, out), grad_middle, grad_middle.astype(bf16), gain_out


def on_device(
    ndp, nseq,
    tokens, doc_lengths, norm_gain, w_y, w_x, gate_a, gate_i, bias_a, bias_i, conv_w, conv_b,
    decay_param, w_out, mlp_gain, w_gate, w_up, w_down, cotangent,
):
    local_len, features = tokens.shape
    rows_here = w_y.shape[0]
    hidden_here = w_gate.shape[1]
    block = gate_a.shape[1]
    piece = hidden_here // ndp
    bits = [1 << k for k in range(ndp.bit_length() - 1)]

    def spread(value):
        values = [value]
        for bit in doubling(ndp)[0]:
            values += [xor_permute(v, "dp", bit) for v in values]
        return values

    def flat(value):
        return value.reshape(-1, value.shape[-1])

    def gather_mlp(value):
        value = value.reshape(ndp, rows_here, -1)
        return lax.all_gather(value, "seq", axis=1, tiled=True).reshape(features, -1)

    all_y, all_x, all_out, gate_rows, up_rows, down_rows = gather_weights(
        ndp, nseq, [w_y, w_x, w_out], [False, True, False], [w_gate, w_up, w_down], 3
    )
    gate_up = gather_mlp(jnp.concatenate([gate_rows, up_rows], axis=1))
    all_down = gather_mlp(down_rows)

    position = lax.axis_index("seq") * local_len + jnp.arange(local_len + PAD, dtype=jnp.int32)
    lengths_row = doc_lengths[0]
    starts = jnp.cumsum(lengths_row) - lengths_row
    resets = jnp.any(position[:, None] == starts[None, :], axis=1)
    doc_start = jnp.max(jnp.where(starts[None, :] <= position[:, None], starts[None, :], 0), axis=1)
    marks = jnp.stack(
        [1.0 - resets.astype(f32)] + [(position - lag >= doc_start).astype(f32) for lag in (1, 2, 3)]
    )
    marks = jnp.broadcast_to(marks[:, :, None], (4, local_len + PAD, LANES))
    vectors = jnp.concatenate(
        [conv_w, conv_b[None], bias_a[None], bias_i[None], jax.nn.softplus(-decay_param)[None]], axis=0
    )

    resid = tokens.astype(f32)
    scale_one = norm_scale(resid)
    acts_one = (resid * scale_one * norm_gain).astype(bf16)
    cots_ready, _ = lax.optimization_barrier((cotangent, all_y))
    mixed_rec, states, pxe, pre_y, rate, ig, conv_out = rec_forward(
        nseq, acts_one, all_x, all_y, marks, gate_a, gate_i, vectors
    )
    all_cots = spread(cots_ready)

    small_group = ndp <= 4
    middle, acts, cots = (enter_mlp if small_group else enter_mlp_plain)(
        ndp, mixed_rec, all_out, tokens, mlp_gain[None], all_cots
    )
    acts_flat, cots_flat = flat(acts), flat(cots)
    pre = matmul(acts_flat, gate_up)
    pre_gate, pre_up = pre[:, :piece], pre[:, piece:]
    gelu, slope = gelu_parts(pre_gate)
    mixed = (gelu * pre_up).astype(bf16)
    to_gate, to_up = (pre_up * slope).reshape(ndp, local_len, piece), gelu.reshape(ndp, local_len, piece)

    def rows_total(left, right):
        return contract_rows(left, right).astype(bf16).reshape(ndp, nseq * rows_here, -1)

    def reduce_mlp(total):
        return lax.psum_scatter(total, "seq", scatter_dimension=1, tiled=True)

    sum_down = reduce_mlp(rows_total(cots_flat, mixed))
    grads, out_sides, grad_middle, grad_middle_low, gain_two = (leave_mlp if small_group else leave_mlp_plain)(
        ndp, cots, to_gate, to_up, mixed.reshape(ndp, local_len, piece), gate_up, all_down, middle, mlp_gain[None]
    )
    total_gate_up, grad_middle_low = lax.optimization_barrier((rows_total(acts_flat, flat(grads)), grad_middle_low))
    sum_gate_up = reduce_mlp(total_gate_up)

    grad_pre_y, grad_pre_x, grad_gate_a, grad_gate_i, sums = rec_backward(
        nseq, grad_middle_low, all_out, marks, gate_a, gate_i, vectors, (pre_y, states, rate, pxe, ig, conv_out)
    )
    part = (contract(grad_pre_y, all_y) + contract(grad_pre_x, all_x)).astype(bf16)
    other = xor_permute(part, "mp", 1)
    out_part = halving(ndp, out_sides, grad_pre_y)
    other_out = xor_permute(out_part, "mp", 1)
    normed = resid * scale_one
    small = [
        grad_gate_a, grad_gate_i, sums, jnp.sum(part.astype(f32) * normed, axis=0), jnp.sum(gain_two, axis=0),
    ]
    sizes = [value.size // block for value in small]
    total_rows = -(-sum(sizes) // (16 * ndp * nseq)) * 16 * ndp * nseq
    small_rows = jnp.concatenate(
        [value.reshape(-1, block) for value in small] + [jnp.zeros((total_rows - sum(sizes), block), f32)], axis=0
    )
    small_sum, grad_w_y, grad_w_x, grad_w_out = reduce_weights(
        ndp, nseq, [acts_one, grad_middle_low],
        [(None, small_rows), (0, grad_pre_y), (0, grad_pre_x), (1, mixed_rec)], 4,
    )
    small_sum, sum_gate_up, other, other_out = lax.optimization_barrier((small_sum, sum_gate_up, other, other_out))
    (small_all,) = gather_weights(ndp, nseq, [small_sum.astype(bf16)], [False], [], 5)
    totals, begin = [], 0
    for value, size in zip(small, sizes):
        totals.append(small_all[begin : begin + size].astype(f32).reshape(value.shape))
        begin += size
    grad_gate_a, grad_gate_i, sums, gain_one, gain_two = totals
    gain_one = gain_one + xor_permute(gain_one, "mp", 1)

    grad_acts = part.astype(f32) + other.astype(f32)
    grad_normed = grad_acts * norm_gain
    input_grad = grad_middle + scale_one * (
        grad_normed - normed * jnp.mean(grad_normed * normed, axis=-1, keepdims=True)
    )

    output = (middle + (out_part.astype(f32) + other_out.astype(f32))).astype(bf16)

    def regroup(value):
        return lax.all_to_all(value, "dp", 0, 2, tiled=True)[0].astype(f32)

    grad_w_down = regroup(sum_down)
    grad_w_gate, grad_w_up = regroup(sum_gate_up[:, :, :piece]), regroup(sum_gate_up[:, :, piece:])
    return (
        output,
        input_grad,
        gain_one,
        grad_w_y,
        grad_w_x,
        grad_gate_a,
        grad_gate_i,
        sums[0],
        sums[1],
        sums[4:8],
        sums[3],
        sums[2] * jax.nn.sigmoid(-decay_param),
        grad_w_out,
        gain_two,
        grad_w_gate,
        grad_w_up,
        grad_w_down,
    )


def solution(mesh):
    rows, cols = P(("dp", "seq"), None), P(("dp", "seq"), "mp")
    return jax.shard_map(
        functools.partial(on_device, mesh.shape["dp"], mesh.shape["seq"]),
        mesh=mesh,
        in_specs=(
            rows, P("dp", None), P(), cols, cols, P("mp", None, None), P("mp", None, None), P("mp"), P("mp"),
            P(None, "mp"), P("mp"), P("mp"), cols, P(), cols, cols, cols, rows,
        ),
        out_specs=(
            rows, rows, P(), cols, cols, P("mp", None, None), P("mp", None, None), P("mp"), P("mp"),
            P(None, "mp"), P("mp"), P("mp"), cols, P(), cols, cols, cols,
        ),
        check_vma=False,
    )
```

time: 1200 us -> 670 us (0.56)
  waiting for transfers between devices: 617 us -> 33.5 us
  Pallas kernels: 90.3 us -> 453 us
  blocking collectives: 103 us -> 0 us
  matrix products: 157 us -> 61.8 us
  local copies, waits for them, and re-layouts: 122 us -> 48.1 us
  starting transfers between devices: 38.2 us -> 16.9 us
  other arithmetic: 49.8 us -> 36.5 us
    pallas_call x0 -> x5, Pallas kernels: none -> 371 us  [the longest x2 116 us: gather_weights(): pl.pallas_call(functools.partial(gather_kernel, ndp, nseq, side_first, sp...]
    reduce_scatter x6 -> x2, waiting for transfers between devices: 323 us -> 0.01 us  [reduce_mlp(): return lax.psum_scatter(total, 'seq', scatter_dimension=1, tiled=True)]
    ppermute x45 -> x5, waiting for transfers between devices: 140 us -> 0.01 us  [xor_permute(): lax.ppermute(value, axis, [(source, source ^ bit) for source in range(cou...]
    all_gather x6 -> x2, waiting for transfers between devices: 140 us -> 33.2 us  [gather_mlp(): lax.all_gather(value, 'seq', axis=1, tiled=True).reshape(features, -1)]
    psum x1 -> x0, blocking collectives: 63.1 us -> none  [on_device(): lax.psum((grad_gate_a, grad_gate_i, sums, jnp.sum(grad_acts * normed, axi...]
    dot_general x15 -> x1, matrix products: 62 us -> 17.4 us  [matmul(): return jnp.dot(left, right, preferred_element_type=f32)]
    all_to_all x1 -> x0, blocking collectives: 40 us -> none  [on_device(): lax.all_to_all(jnp.stack([w_gate, w_up, w_down]).reshape(3, rows_here, nd...]
    dot_general x18 -> x2, matrix products: 45.4 us -> 16.7 us  [contract(): lax.dot_general(left, right, (((1,), (1,)), ((), ())), preferred_element_...]
  transfers between devices with their start and end apart: 59 -> 12, of which waited for: 28 -> 2; matrix products, arithmetic and copies ran while one was open for 26% -> 20% of each run, Pallas kernels for 3% -> 51%
where the time goes in v2:
time: 670 us; the launch traced here: 665 us
  Pallas kernels  453 us (68%)
  matrix products  61.8 us (9%)
  local copies, waits for them, and re-layouts  48.1 us (7%)
  other arithmetic  36.5 us (5%)
  waiting for transfers between devices  33.5 us (5%)
  starting transfers between devices  16.9 us (3%)
  between operations  14.5 us (2%)
    pallas_call x2, Pallas kernels, gather_weights(): pl.pallas_call(functools.partial(gather_kernel, ndp, nseq, side_first, sp...  116 us
    pallas_call x1, Pallas kernels, reduce_weights(): pl.pallas_call(functools.partial(reduce_kernel, ndp, nseq, kinds), out_sh...  113 us
    pallas_call x1, Pallas kernels, leave_mlp(): pl.pallas_call(functools.partial(leave_kernel, ndp), out_shape=(jax.Shape...  76.2 us
    pallas_call x1, Pallas kernels, enter_mlp(): pl.pallas_call(functools.partial(enter_kernel, ndp), out_shape=(jax.Shape...  66.7 us
    pallas_call x1, Pallas kernels, rec_backward(): pl.pallas_call(functools.partial(rec_backward_kernel, nseq, heads, block)...  46.8 us
    pallas_call x1, Pallas kernels, rec_forward(): pl.pallas_call(functools.partial(rec_forward_kernel, nseq, heads, block),...  35.2 us
    all_gather x2, waiting for transfers between devices, gather_mlp(): lax.all_gather(value, 'seq', axis=1, tiled=True).reshape(features, -1)  33.2 us
    dot_general x2, matrix products, contract_rows(): lax.dot_general(left, right, (((0,), (0,)), ((), ())), preferred_element_...  27.7 us
  transfers between devices with their start and end apart: 12, of which 2 were waited for; matrix products, arithmetic and copies ran while one was open for 20% of the time, Pallas kernels for 51%

profile of v2, /device:TPU:0, one launch (start us, length us, event | category | flops | bytes accessed | tf_op | source)
XLA Modules:
  0.0 664.6 jit_solution(8888383711737658357)
XLA Ops:
  7.2 97.2 %gather_weights.2 = (bf16[2048,1280]{1,0:T(8,128)(2,1)}, bf16[2048,1280]{1,0:T(8,128)(2,1)}, bf16[2048,1280]{1,0:T(8,128)(2,1)}, bf16[512,768]{1,0:T(8,128)(2,1)...) custom-call(bf16[128,1280]{1,0:T(8,128)(2,1)} %refs_0_.1, bf16[128,1280]{1,0:T(8,128)(2,1)} %refs_1_.1, ...), custom_call_target="tpu_custom_call" | custom-call | tf_op jit(solution)/shard_map/gather_weights/pallas_call | solution.py:698
  115.9 4.1 copy.47.acts_ref
  122.1 35.2 %rec_forward.1 = (bf16[512,1280]{1,0:T(8,128)(2,1)}, f32[520,1280]{1,0:T(8,128)}, f32[520,1280]{1,0:T(8,128)}, f32[512,1280]{1,0:T(8,128)}, f32[512,1280]{1,0:T(...) custom-call(bf16[512,2048]{1,0:T(8,128)(2,1)} %copy.47.acts_ref, bf16[2048,1280]{1,0:T(8,128)(2,1)} %get-tuple-element.55.wx_ref, ...), custom_call_target="tpu_custom_call" | custom-call | flops 35000000512 | bytes 3500000 | tf_op jit(solution)/shard_map/rec_forward/pallas_call | solution.py:248
  157.3 66.7 %enter_mlp.1 = (f32[512,2048]{1,0:T(8,128)}, bf16[4,512,2048]{2,1,0:T(8,128)(2,1)}, bf16[4,512,2048]{2,1,0:T(8,128)(2,1)}) custom-call(bf16[512,1280]{1,0:T(8,128)(2,1)} %get-tuple-element.57.mixed_ref.refs_5_, bf16[2048,1280]{1,0:T(8,128)(2,1)} %get-tuple-element.58.out_ref, bf16[512,2048]{1,0:T(8,128)(2,1)} %tokens_ref.1, f32[1,2048]{1,0:T(1,128)} %bitcast.91, ...), custom_call_target="tpu_custom_call" | custom-call | flops 65000001536 | bytes 6500000 | tf_op jit(solution)/shard_map/enter_mlp/pallas_call | solution.py:996
  224.0 17.4 %fusion.23 = f32[2048,1536]{1,0:T(8,128)S(1)} fusion(bf16[2048,2048]{1,0:T(8,128)(2,1)} %bitcast.93, bf16[2048,1536]{1,0:T(8,128)(2,1)} %bitcast.88), kind=kOutput, calls=%fused_computation.63 | convolution fusion | flops 12884901888 | bytes 27262976 | tf_op jit(solution)/shard_map/dot_general | solution.py:26
  241.4 7.3 %multiply_convert_fusion = (bf16[2048,768]{1,0:T(8,128)(2,1)S(1)}, f32[2048,768]{1,0:T(8,128)}, f32[2048,768]{1,0:T(8,128)}) fusion(f32[2048,1536]{1,0:T(8,128)S(1)} %fusion.23), kind=kLoop, calls=%fused_computation.10 | loop fusion | flops 33030144 | bytes 28311552 | tf_op jit(solution)/shard_map/convert_element_type | solution.py:1336
  248.7 8.5 %convolution_convert_fusion = bf16[2048,768]{1,0:T(8,128)(2,1)} fusion(bf16[2048,2048]{1,0:T(8,128)(2,1)S(1)} %bitcast.94, bf16[2048,768]{1,0:T(8,128)(2,1)S(1)} %get-tuple-element.127), kind=kOutput, calls=%fused_computation.31 | convolution fusion | flops 6444023808 | bytes 14680064 | tf_op jit(solution)/shard_map/dot_general | solution.py:34
  257.8 33.2 %all-gather.5.cloned.1.call-done = bf16[4,512,768]{2,1,0:T(8,128)(2,1)} async-done(((bf16[4,128,768]{2,1,0:T(8,128)(2,1)}), bf16[4,512,768]{2,1,0:T(8,128)(2,1)}) %all-gather.5.cloned.1.call-update) | async-done | bytes 3145744 | tf_op jit(solution)/shard_map/all_gather | solution.py:1298
  291.0 76.2 %leave_mlp.1 = (bf16[4,512,1536]{2,1,0:T(8,128)(2,1)}, bf16[2,512,2048]{2,1,0:T(8,128)(2,1)}, f32[512,2048]{1,0:T(8,128)}, bf16[512,2048]{1,0:T(8,128)(2,1)}, f32[8,2048]{1,0:T(8,128)}) custom-call(bf16[4,512,2048]{2,1,0:T(8,128)(2,1)} %get-tuple-element.61.cots_ref, f32[4,512,768]{2,1,0:T(8,128)} %bitcast.68, f32[4,512,768]{2,1,0:T(8,128)} %bitcast.67, ...), custom_call_target="tpu_custom_call" | custom-call | flops 74999996416 | bytes 7500000 | tf_op jit(solution)/shard_map/leave_mlp/pallas_call | solution.py:1190
  367.2 19.2 %bitcast_convert_fusion = bf16[2048,1536]{1,0:T(8,128)(2,1)} fusion(bf16[4,512,2048]{2,1,0:T(8,128)(2,1)} %get-tuple-element.62, bf16[4,512,1536]{2,1,0:T(8,128)(2,1)} %get-tuple-element.67), kind=kOutput, calls=%fused_computation | convolution fusion | flops 12888047616 | bytes 20971520 | tf_op jit(solution)/shard_map/dot_general | solution.py:34
  390.6 46.8 %rec_backward.1 = (bf16[512,1280]{1,0:T(8,128)(2,1)}, bf16[512,1280]{1,0:T(8,128)(2,1)}, f32[5,256,256]{2,1,0:T(8,128)}, f32[5,256,256]{2,1,0:T(8,128)}, f32[8,1280]{1,0:T(8,128)}) custom-call(bf16[512,2048]{1,0:T(8,128)(2,1)} %get-tuple-element.69.low_ref, bf16[2048,1280]{1,0:T(8,128)(2,1)} %get-tuple-element.58.out_ref, ...), custom_call_target="tpu_custom_call" | custom-call | flops 44999999488 | bytes 4500000 | tf_op jit(solution)/shard_map/rec_backward/pallas_call | solution.py:457
  437.4 7.8 %fusion.24 = f32[512,2048]{0,1:T(8,128)} fusion(bf16[512,1280]{1,0:T(8,128)(2,1)} %get-tuple-element.76.refs_3_, bf16[2048,1280]{1,0:T(8,128)(2,1)} %get-tuple-element.56.wy_ref), kind=kOutput, calls=%fused_computation.64 | convolution fusion | flops 2684354560 | bytes 10747904 | tf_op jit(solution)/shard_map/dot_general | solution.py:30
  445.3 4.1 copy.49
  449.4 8.9 %fusion.17 = (f32[2048]{0:T(1024)S(1)}, bf16[512,2048]{0,1:T(8,128)(2,1)}) fusion(bf16[512,2048]{0,1:T(8,128)(2,1)S(1)} %copy-done.1, f32[512]{0:T(512)S(1)} %copy-done.17, f32[512,2048]{0,1:T(8,128)} %fusion.24, bf16[512,1280]{1,0:T(8,128)(2,1)} %get-tuple-element.81.refs_4_, bf16[2048,1280]{1,0:T(8,128)(2,1)} %get-tuple-element.55.wx_ref), kind=kOutput, calls=%fused_computation.26 | convolution fusion | flops 2691692544 | bytes 14952448 | tf_op jit(solution)/shard_map/dot_general | solution.py:30
  466.8 3.7 fusion.19
  471.3 3.5 all-to-all-start.2
  474.8 112.5 %reduce_weights.1 = (f32[176,256]{1,0:T(8,128)}, f32[128,1280]{1,0:T(8,128)}, f32[128,1280]{1,0:T(8,128)}, f32[128,1280]{1,0:T(8,128)}) custom-call(bf16[2048,512]{1,0:T(8,128)(2,1)} %fusion.35.refs_0_, bf16[2048,512]{1,0:T(8,128)(2,1)} %bitcast.78, f32[2816,256]{1,0:T(8,128)} %broadcast_dynamic-update-slice_fusion.refs_2_, ...), custom_call_target="tpu_custom_call" | custom-call | flops 99999997952 | bytes 10000000 | tf_op jit(solution)/shard_map/reduce_weights/pallas_call | solution.py:850
  587.4 5.3 copy.52
  596.0 18.8 %gather_weights.3 = bf16[2816,256]{1,0:T(8,128)(2,1)} custom-call(bf16[176,256]{1,0:T(8,128)(2,1)} %convert_element_type.147.refs_0_), custom_call_target="tpu_custom_call" | custom-call | tf_op jit(solution)/shard_map/gather_weights/pallas_call | solution.py:698
  619.5 3.5 all-to-all-start
  623.1 6.0 add_convert_fusion
  629.1 4.0 fusion.15
  634.7 3.5 all-to-all-start.1
  638.8 5.3 copy.56
  (141 shorter events, 51.3 us)
Async XLA Ops:
  7.2 101.1 %copy-start.24 = (s32[1,4]{1,0:T(1,128)S(1)}, s32[1,4]{1,0:T(1,128)}, u32[]{:S(2)}) copy-start(s32[1,4]{1,0:T(1,128)} %param.19) | copy-start | bytes 52
  7.2 216.8 %all-gather.3.cloned.1.call-start = ((), (), s32[]{:S(2)}) async-start(), calls=%async_computation.5 | async-start | bytes 7864320 | tf_op jit(solution)/shard_map/all_gather | solution.py:1298
  107.1 183.9 %all-gather.5.cloned.1.call-start = ((), (), s32[]{:S(2)}) async-start(), calls=%async_computation.6 | async-start | bytes 3932160 | tf_op jit(solution)/shard_map/all_gather | solution.py:1298
  107.2 50.1 %collective-permute-start = (bf16[512,2048]{1,0:T(8,128)(2,1)}, bf16[512,2048]{1,0:T(8,128)(2,1)}, u32[]{:S(2)}, u32[]{:S(2)}) collective-permute-start(bf16[512,2048]{1,0:T(8,128)(2,1)} %refs_0_.2), channel_id=1, source_target_pairs={{0,16},{8,24},{16,0},{24,8},{1,17},{9,25},{17,1},{25,9},{2,18},{10... | collective-permute-start | bytes 6291464 | tf_op jit(solution)/shard_map/ppermute | solution.py:22
  108.3 363.1 %reduce-scatter.5.cloned.1.call-start = ((), (), s32[]{:S(2)}) async-start(), calls=%async_computation.8 | async-start | bytes 3932160 | tf_op jit(solution)/shard_map/reduce_scatter | solution.py:1343
  114.0 6.1 copy-start.23
  114.0 6.1 copy-start.20
  241.4 7.4 %copy-start.25 = (bf16[4,512,2048]{2,1,0:T(8,128)(2,1)S(1)}, bf16[4,512,2048]{2,1,0:T(8,128)(2,1)}, u32[]{:S(2)}) copy-start(bf16[4,512,2048]{2,1,0:T(8,128)(2,1)} %get-tuple-element.61.cots_ref) | copy-start | bytes 25165828
  248.7 8.5 %copy-start.6 = (bf16[2048,768]{1,0:T(8,128)(2,1)}, bf16[2048,768]{1,0:T(8,128)(2,1)S(1)}, u32[]{:S(2)}) copy-start(bf16[2048,768]{1,0:T(8,128)(2,1)S(1)} %get-tuple-element.127) | copy-start | bytes 9437188
  257.2 338.1 %reduce-scatter.3.cloned.1.call-start = ((), (), s32[]{:S(2)}) async-start(), calls=%async_computation.7 | async-start | bytes 7864320 | tf_op jit(solution)/shard_map/reduce_scatter | solution.py:1343
  389.5 77.2 %collective-permute-start.1 = (bf16[1,512,2048]{2,1,0:T(8,128)(2,1)}, bf16[1,512,2048]{2,1,0:T(8,128)(2,1)}, u32[]{:S(2)}, u32[]{:S(2)}) collective-permute-start(bf16[1,512,2048]{2,1,0:T(8,128)(2,1)} %slice.58), channel_id=1, source_target_pairs={{0,16},{8,24},{16,0},{24,8},{1,17},{9,25},{17,1},{25,9},{2,18},{10... | collective-permute-start | bytes 6291464 | tf_op jit(solution)/shard_map/ppermute | solution.py:22
  449.4 9.7 %copy-start.15 = (f32[8,2048]{1,0:T(8,128)S(1)}, f32[8,2048]{1,0:T(8,128)}, u32[]{:S(2)}) copy-start(f32[8,2048]{1,0:T(8,128)} %get-tuple-element.82) | copy-start | bytes 196612
  449.4 13.8 %copy-start.8 = (f32[5,256,256]{2,1,0:T(8,128)S(1)}, f32[5,256,256]{2,1,0:T(8,128)}, u32[]{:S(2)}) copy-start(f32[5,256,256]{2,1,0:T(8,128)} %get-tuple-element.79) | copy-start | bytes 3932164
  459.1 7.7 %copy-start.5 = (bf16[2,512,2048]{2,1,0:T(8,128)(2,1)S(1)}, bf16[2,512,2048]{2,1,0:T(8,128)(2,1)}, u32[]{:S(2)}) copy-start(bf16[2,512,2048]{2,1,0:T(8,128)(2,1)} %get-tuple-element.66) | copy-start | bytes 12582916
  459.1 136.2 %collective-permute-start.2 = (bf16[512,2048]{0,1:T(8,128)(2,1)}, bf16[512,2048]{0,1:T(8,128)(2,1)}, u32[]{:S(2)}, u32[]{:S(2)}) collective-permute-start(bf16[512,2048]{0,1:T(8,128)(2,1)} %get-tuple-element.144), channel_id=1, source_target_pairs={{0,1},{1,0},{2,3},{3,2},{4,5},{5,4},{6,7},{7,6},{8,9},{9,8},{10,11... | collective-permute-start | bytes 6291464 | tf_op jit(solution)/shard_map/ppermute | solution.py:22
  470.5 124.8 %collective-permute-start.3 = (bf16[512,2048]{1,0:T(8,128)(2,1)}, bf16[512,2048]{1,0:T(8,128)(2,1)}, u32[]{:S(2)}, u32[]{:S(2)}) collective-permute-start(bf16[512,2048]{1,0:T(8,128)(2,1)} %fusion.19), channel_id=1, source_target_pairs={{0,1},{1,0},{2,3},{3,2},{4,5},{5,4},{6,7},{7,6},{8,9},{9,8},{10,11... | collective-permute-start | bytes 6291464 | tf_op jit(solution)/shard_map/ppermute | solution.py:22
  471.3 121.4 %all-to-all-start.2 = ((bf16[4,128,768]{2,1,0:T(8,128)(2,1)}), bf16[4,128,768]{2,1,0:T(8,128)(2,1)S(1)}, u32[]{:S(2)}, u32[]{:S(2)}) async-start(bf16[4,128,768]{2,1,0:T(8,128)(2,1)} %reduce-scatter.5.cloned.1.call-done), calls=%async_computation.4 | async-start | bytes 1572864 | tf_op jit(solution)/shard_map/all_to_all | solution.py:1390
  592.9 21.9 %copy-start.14 = (f32[2048]{0:T(1024)S(1)}, f32[2048]{0:T(1024)}, u32[]{:S(2)}) copy-start(f32[2048]{0:T(1024)} %param.20) | copy-start | bytes 24580
  619.5 15.1 %all-to-all-start = ((bf16[4,128,768]{2,1,0:T(8,128)(2,1)}), bf16[4,128,768]{2,1,0:T(8,128)(2,1)S(1)}, u32[]{:S(2)}, u32[]{:S(2)}) async-start(bf16[4,128,768]{2,1,0:T(8,128)(2,1)} %get-tuple-element.131), calls=%async_computation.1 | async-start | bytes 1572864 | tf_op jit(solution)/shard_map/all_to_all | solution.py:1390
  623.0 6.1 copy-start.4
  623.0 6.1 copy-start.2
  623.1 6.1 copy-start.3
  633.2 16.4 %collective-permute-start.4 = (f32[2048]{0:T(1024)S(1)}, f32[2048]{0:T(1024)S(1)}, u32[]{:S(2)}, u32[]{:S(2)}) collective-permute-start(f32[2048]{0:T(1024)S(1)} %bitcast.85), channel_id=1, source_target_pairs={{0,1},{1,0},{2,3},{3,2},{4,5},{5,4},{6,7},{7,6},{8,9},{9,8},{10,11... | collective-permute-start | bytes 24584 | tf_op jit(solution)/shard_map/ppermute | solution.py:22
  634.7 18.1 %all-to-all-start.1 = ((bf16[4,128,768]{2,1,0:T(8,128)(2,1)}), bf16[4,128,768]{2,1,0:T(8,128)(2,1)S(1)}, u32[]{:S(2)}, u32[]{:S(2)}) async-start(bf16[4,128,768]{2,1,0:T(8,128)(2,1)} %get-tuple-element.130), calls=%async_computation.2 | async-start | bytes 1572864 | tf_op jit(solution)/shard_map/all_to_all | solution.py:1390
  (14 other events, 60.5 us)
Sparse Core Ops, SparseCore 0:
  107.2 116.2 all-gather.2
  225.1 65.8 all-gather.4
  293.3 58.9 reduce-scatter.4
  390.7 115.2 reduce-scatter.2

commit v3 on v2

--- a/solution.py
+++ b/solution.py
@@ -55,14 +55,16 @@
     return jnp.where(y < 0.1, y * series, 1.0 - decay * decay)
 
 
-def seq_barrier(nseq):
+def seq_barrier(nseq, ndp=1):
     dp, z, mp = (lax.axis_index(a) for a in ("dp", "seq", "mp"))
     barrier = pltpu.get_barrier_semaphore()
     for step in range(1, nseq):
         pl.semaphore_signal(
             barrier, inc=1, device_id=(dp, lax.rem(z + step, nseq), mp), device_id_type=MESH
         )
-    pl.semaphore_wait(barrier, nseq - 1)
+    for mask in range(1, ndp):
+        pl.semaphore_signal(barrier, inc=1, device_id=(flip(dp, mask), z, mp), device_id_type=MESH)
+    pl.semaphore_wait(barrier, nseq + ndp - 2)
 
 
 def to_seq(src, dst, send_sem, recv_sem, target):
@@ -265,17 +267,18 @@
         compiler_params=pltpu.CompilerParams(
             collective_id=1, has_side_effects=True, vmem_limit_bytes=VMEM_LIMIT
         ),
-        cost_estimate=cost(35),
+        cost_estimate=cost(3),
         name="rec_forward",
     )(acts, all_x, all_y, marks, gate_a, gate_i, vectors)
 
 
 def rec_backward_kernel(
-    nseq, heads, block,
-    low_ref, out_ref, marks_ref, ga_ref, gi_ref, vec_ref, py_ref, states_ref, rate_ref, pxe_ref, ig_ref, co_ref,
-    gpy_ref, gpx_ref, gga_ref, ggi_ref, sums_ref,
+    ndp, nseq, heads, block,
+    low_ref, mixed_ref, out_ref, marks_ref, ga_ref, gi_ref, vec_ref, py_ref, states_ref, rate_ref, pxe_ref, ig_ref, co_ref,
+    gpy_ref, gpx_ref, gga_ref, ggi_ref, sums_ref, ready_ref,
     py_s, states_s, rate_s, pxe_s, ig_s, co_s, w_s, b_s, g_s, gm_s, gc_s, gr_s, gx_s,
     msg, got, grad_in, head_s, load_sems, halo_send, halo_recv, end_send, end_recv,
+    low_t, core_out, core_in, side_out, side_in, keep, core_sems, side_sems,
 ):
     rows, width = gpy_ref.shape
     seg = rows // SEGMENTS
@@ -288,7 +291,25 @@
     ]
     for load in loads:
         load.start()
-    seq_barrier(nseq)
+
+    def transpose(k, _):
+        at = pl.ds(pl.multiple_of(k * LANES, LANES), LANES)
+        low_t[:, at] = low_ref[at, :].astype(f32).T.astype(bf16)
+        return 0
+
+    lax.fori_loop(0, rows // LANES, transpose, 0)
+    seq_barrier(nseq, ndp)
+    dp = lax.axis_index("dp")
+    row_block = ready_ref.shape[1]
+
+    def product(mask):
+        return matmul(dp_rows(low_t, row_block * nseq, mask), mixed_ref[...])
+
+    copies = Copies()
+    weight = DpSum(
+        ndp, nseq, product, keep, None, (core_out, core_in, side_out, side_in), (core_sems, side_sems), copies
+    )
+    weight.begin()
     for load in loads[:3]:
         load.wait()
 
@@ -317,6 +338,7 @@
         return 0
 
     lax.fori_loop(0, heads, first, 0)
+    weight.to_side()
     row = lax.broadcasted_iota(jnp.int32, (8, width), 0)
 
     def turn(i, kept):
@@ -433,6 +455,13 @@
         return 0
 
     lax.fori_loop(0, SEGMENTS * heads, final, 0)
+    for step in far_first(nseq):
+
+        def ready():
+            ready_ref[z + step] = weight.with_core(step, 0).astype(bf16)
+
+        under(in_line(nseq, step), ready)
+    copies.finish()
 
     @pl.when(z > 0)
     def _():
@@ -445,8 +474,10 @@
             to_seq(msg, got.at[z], end_send.at[step - 1], end_recv.at[z], z).wait_send()
 
 
-def rec_backward(nseq, low, all_out, marks, gate_a, gate_i, vectors, kept):
+def rec_backward(ndp, nseq, low, mixed, all_out, marks, gate_a, gate_i, vectors, kept):
     rows, width = low.shape[0], all_out.shape[1]
+    row_block = all_out.shape[0] // (ndp * nseq)
+    buffers, sems = dp_sum_shapes(ndp, nseq, row_block, width, True)
     heads, block = gate_a.shape[:2]
     vmem, anywhere = pl.BlockSpec(memory_space=pltpu.VMEM), pl.BlockSpec(memory_space=pl.ANY)
     grads = jax.ShapeDtypeStruct((rows, width), bf16)
@@ -455,10 +486,13 @@
     ext = pltpu.VMEM((rows + PAD, width), f32)
     dma = pltpu.SemaphoreType.DMA
     return pl.pallas_call(
-        functools.partial(rec_backward_kernel, nseq, heads, block),
-        out_shape=(grads, grads, gates, gates, jax.ShapeDtypeStruct((8, width), f32)),
-        in_specs=[vmem] * 6 + [anywhere] * len(kept),
-        out_specs=[vmem] * 5,
+        functools.partial(rec_backward_kernel, ndp, nseq, heads, block),
+        out_shape=(
+            grads, grads, gates, gates, jax.ShapeDtypeStruct((8, width), f32),
+            jax.ShapeDtypeStruct((nseq, row_block, width), bf16),
+        ),
+        in_specs=[vmem] * 7 + [anywhere] * len(kept),
+        out_specs=[vmem] * 6,
         scratch_shapes=[
             *[pltpu.VMEM(k.shape, k.dtype) for k in kept],
             ext,
@@ -473,13 +507,14 @@
             pltpu.VMEM((1, width), f32),
             small,
             dma((len(kept),)), dma, dma, dma((nseq - 1,)), dma((nseq,)),
+            pltpu.VMEM(low.shape[::-1], bf16), *buffers, *sems,
         ],
         compiler_params=pltpu.CompilerParams(
             collective_id=2, has_side_effects=True, vmem_limit_bytes=VMEM_LIMIT
         ),
-        cost_estimate=cost(45),
+        cost_estimate=cost(20),
         name="rec_backward",
-    )(low, all_out, marks, gate_a, gate_i, vectors, *kept)
+    )(low, mixed, all_out, marks, gate_a, gate_i, vectors, *kept)
 
 
 def flip(index, mask):
@@ -518,353 +553,540 @@
         self.sent = []
 
     def start(self, here, make):
-        if here is None:
-            make().start()
-        else:
-
-            @pl.when(here)
-            def _():
-                make().start()
-
+        under(here, lambda: make().start())
         self.sent.append((here, make))
 
     def finish(self):
         for here, make in self.sent:
-            if here is None:
-                make().wait_send()
-            else:
-
-                @pl.when(here)
-                def _():
-                    make().wait_send()
-
-
-def gather_kernel(ndp, nseq, side_first, split, *refs):
-    count = len(side_first)
-    shards, wide = refs[:count], refs[count : count + split]
-    wholes, pieces = refs[count + split : 2 * count + split], refs[2 * count + split : 2 * (count + split)]
-    local_sem, send, recv, piece_send, piece_recv = refs[2 * (count + split) :]
-    dp, z, mp = (lax.axis_index(a) for a in ("dp", "seq", "mp"))
-    rows = shards[0].shape[0]
-    piece_cols = pieces[0].shape[1] if split else 0
-    bits = [1 << k for k in range(1, ndp.bit_length() - 1)][::-1]
-    copies = Copies()
-
-    def valid(step):
-        if step == 0:
-            return None
-        return z + step < nseq if step > 0 else z + step >= 0
-
-    def copy(i, step, mask, there, mask_there, target):
-        at = pl.ds(pl.multiple_of((flip(dp, mask) * nseq + z + step) * rows, rows), rows)
-        index = (i, there + nseq - 1, mask_there)
+            under(here, lambda: make().wait_send())
+
+
+def under(here, body):
+    if here is None:
+        body()
+    else:
+        pl.when(here)(body)
+
+
+def in_line(nseq, step):
+    z = lax.axis_index("seq")
+    if step == 0:
+        return None
+    return z + step < nseq if step > 0 else z + step >= 0
+
+
+class Gather:
+    def __init__(self, ndp, nseq, side_first, shards, wholes, send, recv):
+        self.ndp, self.nseq, self.side_first = ndp, nseq, side_first
+        self.shards, self.wholes, self.send, self.recv = shards, wholes, send, recv
+        self.bits, self.masks = doubling(ndp)
+        self.copies = Copies()
+        self.dp, self.z, self.mp = (lax.axis_index(a) for a in ("dp", "seq", "mp"))
+
+    def place(self, i, step, mask):
+        rows = self.shards[i].shape[0]
+        block = flip(self.dp, mask) * self.nseq + self.z + step
+        return pl.ds(pl.multiple_of(block * rows, rows), rows)
+
+    def copy(self, i, step, mask, there, mask_there, target):
+        whole = self.wholes[i].at[self.place(i, step, mask)]
+        index = (i, there + self.nseq - 1, mask_there)
         return pltpu.make_async_remote_copy(
-            src_ref=shards[i] if step == 0 and mask == 0 and target is not None else wholes[i].at[at],
-            dst_ref=wholes[i].at[at],
-            send_sem=send.at[index],
-            recv_sem=recv.at[index],
-            device_id=(dp, z, mp) if target is None else target,
+            src_ref=self.shards[i] if step == 0 and mask == 0 and target is not None else whole,
+            dst_ref=whole,
+            send_sem=self.send.at[index],
+            recv_sem=self.recv.at[index],
+            device_id=(self.dp, self.z, self.mp) if target is None else target,
             device_id_type=MESH,
         )
 
-    def along(i, step, mask):
+    def along(self, i, step, mask):
         for way in (1, -1):
             if step * way > 0:
                 continue
-            near = z < nseq - 1 if way > 0 else z > 0
-            here = near if step == 0 else near & valid(step)
-            copies.start(
-                here,
-                functools.partial(copy, i, step, mask, step - way, mask, (dp, z + way, mp)),
-            )
-
-    def across(i, step, mask, bit):
-        copies.start(
-            valid(step),
-            functools.partial(copy, i, step, mask, step, mask | bit, (flip(dp, bit), z, mp)),
+            near = in_line(self.nseq, way)
+            here = near if step == 0 else near & in_line(self.nseq, step)
+            target = (self.dp, self.z + way, self.mp)
+            self.copies.start(here, functools.partial(self.copy, i, step, mask, step - way, mask, target))
+
+    def across(self, i, step, mask, bit):
+        target = (flip(self.dp, bit), self.z, self.mp)
+        self.copies.start(
+            in_line(self.nseq, step), functools.partial(self.copy, i, step, mask, step, mask | bit, target)
         )
 
-    def go_on(i, step, mask):
+    def go_on(self, i, step, mask):
         if mask & 1:
             return
-        lowest = mask & -mask if mask else ndp
-        if side_first[i]:
+        lower = [bit for bit in self.bits if mask == 0 or bit < mask & -mask]
+        if self.side_first[i]:
             if step == 0:
-                for bit in bits:
-                    if bit < lowest:
-                        across(i, step, mask, bit)
-            along(i, step, mask)
+                for bit in lower:
+                    self.across(i, step, mask, bit)
+            self.along(i, step, mask)
         else:
             if mask == 0:
-                along(i, step, mask)
-            for bit in bits:
-                if bit < lowest:
-                    across(i, step, mask, bit)
-        across(i, step, mask, 1)
-
-    def arrive(i, step, mask):
-        def wait():
-            copy(i, step, mask, step, mask, None).wait_recv()
-
-        if step == 0:
-            wait()
-        else:
-            pl.when(valid(step))(wait)
-        go_on(i, step, mask)
+                self.along(i, step, mask)
+            for bit in lower:
+                self.across(i, step, mask, bit)
+        self.across(i, step, mask, 1)
+
+    def arrive(self, i, step, mask):
+        under(in_line(self.nseq, step), lambda: self.copy(i, step, mask, step, mask, None).wait_recv())
+        self.go_on(i, step, mask)
+
+    def both(self, i, distance, mask):
+        for step in sorted({-distance, distance}):
+            self.arrive(i, step, mask)
+
+    def others(self, i):
+        for mask in self.masks:
+            for step in range(1 - self.nseq, self.nseq):
+                self.arrive(i, step, mask | 1)
+
+
+def gather_kernel(ndp, nseq, count, joined, tokens_ref, gain_ref, *refs):
+    shards, wide, refs = refs[:count], refs[count : count + 3], refs[count + 3 :]
+    wholes, refs = refs[:count], refs[count:]
+    pieces, refs = (refs[:1] * 2, refs[1:]) if joined else (refs[:2], refs[2:])
+    line, acts_ref, acts_t_ref, local_sem, send, recv, piece_send, piece_recv, line_send, line_recv = refs
+    dp, z, mp = (lax.axis_index(a) for a in ("dp", "seq", "mp"))
+    rows = shards[0].shape[0]
+    piece_cols = line.shape[2]
+    flow = Gather(ndp, nseq, [False] * count, shards, wholes, send, recv)
+
+    def piece_place(k, block):
+        if k == 2:
+            return line.at[block, pl.ds(pl.multiple_of(z * rows, rows), rows)]
+        at = pl.ds(pl.multiple_of(block * rows, rows), rows)
+        return pieces[k].at[at, pl.ds(k * piece_cols, piece_cols)] if joined else pieces[k].at[at]
 
     def piece_copy(k, mask):
         cols = pl.ds(pl.multiple_of(flip(dp, mask) * piece_cols, LANES), piece_cols)
-        src = wide[k].at[:, cols] if len(wide[k].shape) == 2 else wide[k].at[flip(dp, mask)]
-        dst = pieces[k].at[pl.ds(pl.multiple_of(dp * rows, rows), rows)]
+        src = wide[k].at[:, cols] if joined else wide[k].at[flip(dp, mask)]
         if mask == 0:
-            return pltpu.make_async_copy(src, dst, local_sem.at[count + k])
+            return pltpu.make_async_copy(src, piece_place(k, dp), local_sem.at[count + k])
         return pltpu.make_async_remote_copy(
-            src_ref=src, dst_ref=dst, send_sem=piece_send.at[k, mask], recv_sem=piece_recv.at[k, mask],
-            device_id=(flip(dp, mask), z, mp), device_id_type=MESH,
+            src_ref=src, dst_ref=piece_place(k, dp), send_sem=piece_send.at[k, mask],
+            recv_sem=piece_recv.at[k, mask], device_id=(flip(dp, mask), z, mp), device_id_type=MESH,
         )
 
-    def piece_arrived(k, mask):
-        at = pl.ds(pl.multiple_of(flip(dp, mask) * rows, rows), rows)
-        pltpu.make_async_remote_copy(
-            src_ref=pieces[k].at[at], dst_ref=pieces[k].at[at], send_sem=piece_send.at[k, mask],
-            recv_sem=piece_recv.at[k, mask], device_id=(dp, z, mp), device_id_type=MESH,
-        ).wait_recv()
-
-    neighbour_barrier(ndp, nseq)
-    for i in range(count):
-        here = pl.ds(pl.multiple_of((dp * nseq + z) * rows, rows), rows)
-        pltpu.make_async_copy(shards[i], wholes[i].at[here], local_sem.at[i]).start()
-    order = sorted(range(count), key=lambda i: not side_first[i])
-    for i in order:
-        go_on(i, 0, 0)
-    masks = [0]
-    for bit in bits:
-        masks += [m | bit for m in masks]
-    sides = masks[1:]
-    first, last = [i for i in order if side_first[i]], [i for i in order if not side_first[i]]
-    for i in first:
-        for mask in sides:
-            arrive(i, 0, mask)
-    pieces_left = list(range(split))
-    for step in range(1, nseq):
-        if pieces_left:
-            k = pieces_left.pop(0)
-            for mask in range(ndp):
-                piece_copy(k, mask).start()
-        for i in order:
-            arrive(i, -step, 0)
-            arrive(i, step, 0)
-        for i in last:
-            for mask in sides:
-                arrive(i, 1 - step, mask)
-                if step > 1:
-                    arrive(i, step - 1, mask)
-        for i in first:
-            for mask in sides:
-                arrive(i, -step, mask)
-                arrive(i, step, mask)
-    for k in pieces_left:
+    def send_pieces(k):
         for mask in range(ndp):
             piece_copy(k, mask).start()
-    for i in last:
-        for mask in sides:
-            arrive(i, 1 - nseq, mask)
-            arrive(i, nseq - 1, mask)
-    for i in range(count):
-        for mask in masks:
-            for step in range(1 - nseq, nseq):
-                arrive(i, step, mask | 1)
-    for k in range(split):
-        for mask in range(1, ndp):
-            piece_arrived(k, mask)
-    for i in range(count):
-        here = pl.ds(pl.multiple_of((dp * nseq + z) * rows, rows), rows)
-        pltpu.make_async_copy(shards[i], wholes[i].at[here], local_sem.at[i]).wait()
-    for k in range(split):
+
+    def pieces_here(k):
         piece_copy(k, 0).wait()
         for mask in range(1, ndp):
+            place = piece_place(k, flip(dp, mask))
+            pltpu.make_async_remote_copy(
+                src_ref=place, dst_ref=place, send_sem=piece_send.at[k, mask],
+                recv_sem=piece_recv.at[k, mask], device_id=(dp, z, mp), device_id_type=MESH,
+            ).wait_recv()
+
+    def line_copy(step, there, target):
+        place = line.at[:, pl.ds(pl.multiple_of((z + step) * rows, rows), rows)]
+        return pltpu.make_async_remote_copy(
+            src_ref=place, dst_ref=place, send_sem=line_send.at[there + nseq - 1],
+            recv_sem=line_recv.at[there + nseq - 1], device_id=target, device_id_type=MESH,
+        )
+
+    def line_on(step):
+        for way in (1, -1):
+            if step * way <= 0:
+                near = in_line(nseq, way)
+                here = near if step == 0 else near & in_line(nseq, step)
+                flow.copies.start(here, functools.partial(line_copy, step, step - way, (dp, z + way, mp)))
+
+    def line_both(distance):
+        for step in (-distance, distance):
+            under(in_line(nseq, step), lambda: line_copy(step, step, (dp, z, mp)).wait_recv())
+            line_on(step)
+
+    def own(i):
+        return pltpu.make_async_copy(shards[i], wholes[i].at[flow.place(i, 0, 0)], local_sem.at[i])
+
+    neighbour_barrier(ndp, nseq)
+    send_pieces(2)
+    for i in range(count):
+        flow.go_on(i, 0, 0)
+    for i in range(count):
+        own(i).start()
+
+    def norm(c, _):
+        at = pl.ds(pl.multiple_of(c * LANES, LANES), LANES)
+        values = tokens_ref[at, :].astype(f32)
+        scale = lax.rsqrt(jnp.mean(values * values, axis=-1, keepdims=True) + epsilon)
+        acts = values * scale * gain_ref[...]
+        acts_ref[at, :] = acts.astype(bf16)
+        acts_t_ref[:, at] = acts.T.astype(bf16)
+        return 0
+
+    lax.fori_loop(0, tokens_ref.shape[0] // LANES, norm, 0)
+    pieces_here(2)
+    line_on(0)
+    sides = flow.masks[1:]
+    for step in range(1, nseq):
+        if step < 3:
+            send_pieces(step - 1)
+        for i in range(count):
+            flow.both(i, step, 0)
+        line_both(step)
+        for i in range(count):
+            for mask in sides:
+                flow.both(i, step - 1, mask)
+    for i in range(count):
+        for mask in sides:
+            flow.both(i, nseq - 1, mask)
+    for i in range(count):
+        flow.others(i)
+    for k in (0, 1):
+        pieces_here(k)
+    for i in range(count):
+        own(i).wait()
+    for k in range(3):
+        for mask in range(1, ndp):
             piece_copy(k, mask).wait_send()
-    copies.finish()
-
-
-def gather_weights(ndp, nseq, shards, side_first, wide, number):
+    flow.copies.finish()
+
+
+def gather_weights(ndp, nseq, tokens, gain, shards, wide):
     rows = shards[0].shape[0]
-    count, split = len(shards), len(wide)
-    piece = wide[0].shape[1] // ndp if split else LANES
-    if piece % LANES:
+    count = len(shards)
+    piece = wide[0].shape[1] // ndp
+    joined = piece % LANES == 0
+    if not joined:
         wide = [jnp.swapaxes(w.reshape(rows, ndp, piece), 0, 1) for w in wide]
     dma = pltpu.SemaphoreType.DMA
-    anywhere = pl.BlockSpec(memory_space=pl.ANY)
-    return pl.pallas_call(
-        functools.partial(gather_kernel, ndp, nseq, side_first, split),
+    vmem, anywhere = pl.BlockSpec(memory_space=pltpu.VMEM), pl.BlockSpec(memory_space=pl.ANY)
+    pairs = [(ndp * rows, 2 * piece)] if joined else [(ndp * rows, piece)] * 2
+    *wholes, line, acts, acts_t = pl.pallas_call(
+        functools.partial(gather_kernel, ndp, nseq, count, joined),
         out_shape=[jax.ShapeDtypeStruct((ndp * nseq * rows, s.shape[1]), s.dtype) for s in shards]
-        + [jax.ShapeDtypeStruct((ndp * rows, piece), w.dtype) for w in wide],
-        in_specs=[anywhere] * (count + split),
-        out_specs=[anywhere] * (count + split),
+        + [jax.ShapeDtypeStruct(shape, bf16) for shape in pairs]
+        + [jax.ShapeDtypeStruct((ndp, nseq * rows, piece), bf16)]
+        + [jax.ShapeDtypeStruct(tokens.shape, bf16), jax.ShapeDtypeStruct(tokens.shape[::-1], bf16)],
+        in_specs=[vmem] * 2 + [anywhere] * (count + 3),
+        out_specs=[anywhere] * (count + len(pairs) + 1) + [vmem] * 2,
         scratch_shapes=[
-            dma((count + split,)), dma((count, 2 * nseq - 1, ndp)), dma((count, 2 * nseq - 1, ndp)),
-            dma((max(split, 1), ndp)), dma((max(split, 1), ndp)),
+            dma((count + 3,)), dma((count, 2 * nseq - 1, ndp)), dma((count, 2 * nseq - 1, ndp)),
+            dma((3, ndp)), dma((3, ndp)), dma((2 * nseq - 1,)), dma((2 * nseq - 1,)),
         ],
-        compiler_params=pltpu.CompilerParams(collective_id=number, has_side_effects=True),
+        compiler_params=pltpu.CompilerParams(
+            collective_id=3, has_side_effects=True, vmem_limit_bytes=VMEM_LIMIT
+        ),
+        cost_estimate=cost(3),
         name="gather_weights",
-    )(*shards, *wide)
-
-
-def reduce_kernel(ndp, nseq, kinds, *refs):
+    )(tokens, gain, *shards, *wide)
+    wholes, pairs = wholes[:count], wholes[count:]
+    return wholes, jnp.concatenate(pairs, axis=1), line.reshape(-1, piece), acts, acts_t
+
+
+class DpSum:
+    def __init__(self, ndp, nseq, product, keep, block, buffers, sems, copies):
+        self.ndp, self.nseq, self.copies = ndp, nseq, copies
+        self.product, self.keep, self.block = product, keep, block
+        self.core_out, self.core_in, self.side_out, self.side_in = buffers
+        self.core_sems, self.side_sems = sems
+        self.rows = self.core_out.shape[2]
+        self.evens = list(range(0, ndp, 2))
+        self.bits = doubling(ndp)[0]
+        self.dp, self.z, self.mp = (lax.axis_index(a) for a in ("dp", "seq", "mp"))
+
+    def remote(self, out, into, sems, at, bit):
+        return pltpu.make_async_remote_copy(
+            src_ref=out.at[at], dst_ref=into.at[at], send_sem=sems.at[(0, *at)], recv_sem=sems.at[(1, *at)],
+            device_id=(flip(self.dp, bit), self.z, self.mp), device_id_type=MESH,
+        )
+
+    def core(self, step, mask):
+        return self.remote(self.core_out, self.core_in, self.core_sems, (self.z + step, mask // 2), 1)
+
+    def side(self, step, mask, bit):
+        return self.remote(self.side_out, self.side_in, self.side_sems, (self.z + step, mask // 2 - 1), bit)
+
+    def begin(self):
+        for mask in self.evens:
+            total = self.product(mask | 1).astype(bf16)
+            for z in range(self.nseq):
+                self.core_out[z, mask // 2] = total[z * self.rows : (z + 1) * self.rows]
+        for step in far_first(self.nseq):
+            for mask in self.evens:
+                self.copies.start(in_line(self.nseq, step), functools.partial(self.core, step, mask))
+        if self.keep is not None:
+            for mask in self.evens:
+                total = self.product(mask)
+                for z in range(self.nseq):
+                    self.keep[z, mask // 2] = total[z * self.rows : (z + 1) * self.rows]
+
+    def with_core(self, step, mask):
+        self.core(step, mask).wait_recv()
+        at = (self.z + step, mask // 2)
+        total = self.keep[at] if self.keep is not None else self.block(step, mask)
+        total = total + self.core_in[at].astype(f32)
+        for more in self.bits:
+            if mask == 0 or more > mask:
+                self.side(step, mask | more, more).wait_recv()
+                total = total + self.side_in[self.z + step, (mask | more) // 2 - 1].astype(f32)
+        return total
+
+    def to_side(self):
+        for step in far_first(self.nseq):
+            for mask in self.evens[:0:-1]:
+                bit = 1 << (mask.bit_length() - 1)
+
+                def work():
+                    self.side_out[self.z + step, mask // 2 - 1] = self.with_core(step, mask).astype(bf16)
+
+                under(in_line(self.nseq, step), work)
+                self.copies.start(in_line(self.nseq, step), functools.partial(self.side, step, mask, bit))
+
+
+def dp_rows(ref, rows, mask):
+    return ref[pl.ds(pl.multiple_of(flip(lax.axis_index("dp"), mask) * rows, rows), rows), :]
+
+
+def far_first(nseq):
+    return [step for k in range(nseq - 1, 0, -1) for step in (k, -k)] + [0]
+
+
+def dp_sum_shapes(ndp, nseq, rows, width, keep):
+    dma, evens = pltpu.SemaphoreType.DMA, ndp // 2
+    kept = [pltpu.VMEM((nseq, evens, rows, width), f32)] if keep else []
+    return [
+        pltpu.VMEM((nseq, lead, rows, width), bf16) for lead in (evens, evens, evens - 1, evens - 1)
+    ] + kept, [dma((2, nseq, evens)), dma((2, nseq, evens - 1))]
+
+
+def reduce_kernel(ndp, nseq, kinds, moves, *refs):
     lefts = max(kind[0] for kind in kinds if kind[0] is not None) + 1
     left_refs, refs = refs[:lefts], refs[lefts:]
     count = len(kinds)
-    rights, outs = refs[:count], refs[count : 2 * count]
-    buffers, refs = refs[2 * count : 9 * count], refs[9 * count :]
-    core_out, core_in, side_out, side_in, flow_out, up_in, down_in = (
-        buffers[k * count : (k + 1) * count] for k in range(7)
-    )
-    acc, core_sems, side_sems, flow_sems, up_sems, down_sems = refs
+    summed = [i for i in range(count) if kinds[i][0] != -1]
+    rights, sources, refs = refs[:count], refs[count : count + moves], refs[count + moves :]
+    all_ref, outs, moved = refs[0], refs[1:count], refs[count : count + moves]
+    refs = refs[count + moves :]
+    parts = {}
+    copies = Copies()
     dp, z, mp = (lax.axis_index(a) for a in ("dp", "seq", "mp"))
-    evens = list(range(0, ndp, 2))
-    bits = [1 << k for k in range(1, ndp.bit_length() - 1)][::-1]
-    order = [s for k in range(nseq - 1, 0, -1) for s in (k, -k)] + [0]
-    copies = Copies()
-    me = (dp, z, mp)
-
-    def valid(step):
-        if step == 0:
-            return None
-        return z + step < nseq if step > 0 else z + step >= 0
-
-    def under(here, body):
-        if here is None:
-            body()
-        else:
-            pl.when(here)(body)
-
-    def remote(src, dst, send_sem, recv_sem, target):
-        return pltpu.make_async_remote_copy(
-            src_ref=src, dst_ref=dst, send_sem=send_sem, recv_sem=recv_sem,
-            device_id=target, device_id_type=MESH,
+    for i in summed:
+        left, _, rows = kinds[i]
+        buffers, refs = refs[:4], refs[4:]
+        keep = None
+        if left is not None:
+            keep, refs = refs[0], refs[1:]
+        sems, refs = refs[:2], refs[2:]
+
+        def product(i, mask):
+            left, _, rows = kinds[i]
+            taken = dp_rows(rights[i] if left is None else left_refs[left], rows * nseq, mask)
+            return taken if left is None else matmul(taken, rights[i][...])
+
+        def block(i, step, mask):
+            rows = kinds[i][2]
+            start = pl.multiple_of((flip(dp, mask) * nseq + z + step) * rows, rows)
+            return rights[i][pl.ds(start, rows), :]
+
+        parts[i] = DpSum(
+            ndp, nseq, functools.partial(product, i), keep, functools.partial(block, i), buffers, sems, copies
         )
-
-    def core(i, step, mask):
-        at = (z + step, mask // 2)
-        return remote(
-            core_out[i].at[at], core_in[i].at[at], core_sems.at[(0, i, *at)], core_sems.at[(1, i, *at)],
-            (flip(dp, 1), z, mp),
-        )
-
-    def side(i, step, mask, bit):
-        at = (z + step, mask // 2 - 1)
-        return remote(
-            side_out[i].at[at], side_in[i].at[at], side_sems.at[(0, i, *at)], side_sems.at[(1, i, *at)],
-            (flip(dp, bit), z, mp),
-        )
+    flow_out, up_in, down_in, refs = refs[:count], refs[count : 2 * count], refs[2 * count : 3 * count], refs[3 * count :]
+    held, refs = refs[:moves], refs[moves:]
+    acc, shard, flow_sems, up_sems, down_sems, send, recv, move_send, move_recv = refs
+    moving = Regroup(ndp, sources, held, moved, move_send, move_recv)
+    order = far_first(nseq)
 
     def flow(i, step, way):
         into, sems = (up_in, up_sems) if way > 0 else (down_in, down_sems)
-        return remote(
-            flow_out[i].at[z + step], into[i].at[z + step], flow_sems.at[i, z + step], sems.at[i, z + step],
-            (dp, z + way, mp),
+        return pltpu.make_async_remote_copy(
+            src_ref=flow_out[i].at[z + step], dst_ref=into[i].at[z + step],
+            send_sem=flow_sems.at[i, z + step], recv_sem=sems.at[i, z + step],
+            device_id=(dp, z + way, mp), device_id_type=MESH,
         )
 
-    def product(i, step, mask):
-        rows = kinds[i][2]
-        start = pl.multiple_of((flip(dp, mask) * nseq + z + step) * rows, rows)
-        left = kinds[i][0]
-        if left is None:
-            return rights[i][pl.ds(start, rows), :]
-        return jnp.dot(left_refs[left][pl.ds(start, rows), :], rights[i][...], preferred_element_type=f32)
-
-    def block(ref, i, step, *more):
-        return ref[i][(z + step, *more)].astype(f32)
-
-    def store(ref, value, i, step, *more):
-        ref[i][(z + step, *more)] = value.astype(bf16)
-
+    spread = Gather(ndp, nseq, [False], [shard], [all_ref], send, recv)
+    sides = spread.masks[1:]
+
+    def pass_on(i, step):
+        spot = (pl.ds(0, kinds[i][2]), pl.ds(0, kinds[i][1]))
+
+        def work():
+            acc[spot] = parts[i].with_core(step, 0) if i in parts else rights[i][z + step].astype(f32)
+
+            def add(into, way):
+                flow(i, step, way).wait_recv()
+                acc[spot] += into[i][z + step].astype(f32)
+
+            if step >= 0:
+                pl.when(z > 0)(lambda: add(up_in, 1))
+            if step <= 0:
+                pl.when(z < nseq - 1)(lambda: add(down_in, -1))
+            if step:
+                flow_out[i][z + step] = acc[spot].astype(bf16)
+            elif i:
+                outs[i - 1][...] = acc[spot]
+            else:
+                shard[...] = acc[spot].astype(bf16)
+                all_ref[spread.place(0, 0, 0), :] = shard[...]
+
+        under(in_line(nseq, step), work)
+        if step:
+            copies.start(in_line(nseq, step), functools.partial(flow, i, step, 1 if step > 0 else -1))
+
+    def along(items, distance):
+        for i in items:
+            for step in (distance, -distance):
+                pass_on(i, step)
+
+    ready = [i for i in range(1, count) if i not in parts]
+    products = [i for i in range(1, count) if i in parts]
     neighbour_barrier(ndp, nseq)
-    for i in range(count):
-        for step in order:
-
-            def to_core():
-                for mask in evens:
-                    store(core_out, product(i, step, mask | 1), i, step, mask // 2)
-
-            under(valid(step), to_core)
-            for mask in evens:
-                copies.start(valid(step), functools.partial(core, i, step, mask))
-    for i in range(count):
-        for step in order:
-            for mask in evens[:0:-1]:
-                bit = 1 << (mask.bit_length() - 1)
-
-                def to_side():
-                    core(i, step, mask).wait_recv()
-                    total = product(i, step, mask) + block(core_in, i, step, mask // 2)
-                    for more in bits:
-                        if more > bit:
-                            side(i, step, mask | more, more).wait_recv()
-                            total = total + block(side_in, i, step, (mask | more) // 2 - 1)
-                    store(side_out, total, i, step, mask // 2 - 1)
-
-                under(valid(step), to_side)
-                copies.start(valid(step), functools.partial(side, i, step, mask, bit))
-    for i in range(count):
-        spot = (pl.ds(0, kinds[i][2]), pl.ds(0, kinds[i][1]))
-        for step in order:
-
-            def to_flow():
-                core(i, step, 0).wait_recv()
-                acc[spot] = product(i, step, 0) + block(core_in, i, step, 0)
-                for more in bits:
-                    side(i, step, more, more).wait_recv()
-                    acc[spot] += block(side_in, i, step, more // 2 - 1)
-
-                def add(into, way):
-                    flow(i, step, way).wait_recv()
-                    acc[spot] += block(into, i, step)
-
-                if step >= 0:
-                    pl.when(z > 0)(lambda: add(up_in, 1))
-                if step <= 0:
-                    pl.when(z < nseq - 1)(lambda: add(down_in, -1))
-                if step:
-                    store(flow_out, acc[spot], i, step)
-                else:
-                    outs[i][...] = acc[spot]
-
-            under(valid(step), to_flow)
-            if step:
-                copies.start(valid(step), functools.partial(flow, i, step, 1 if step > 0 else -1))
+    along(ready, nseq - 1)
+    parts[0].begin()
+    for k, i in enumerate(products):
+        parts[i].begin()
+        if k == 0:
+            parts[0].to_side()
+        parts[i].to_side()
+        if nseq - 2 - k > 0:
+            along(ready, nseq - 2 - k)
+    for distance in range(nseq - 2 - len(products), 0, -1):
+        along(ready, distance)
+    moving.start()
+    for step in order:
+        pass_on(0, step)
+    spread.go_on(0, 0, 0)
+    for k, i in enumerate(products):
+        for distance in range(nseq - 1, 0, -1):
+            along([i], distance)
+        if k + 1 < nseq:
+            spread.both(0, k + 1, 0)
+    for i in ready + products:
+        pass_on(i, 0)
+    for distance in range(len(products) + 1, nseq):
+        spread.both(0, distance, 0)
+    for mask in sides:
+        for distance in range(nseq):
+            spread.both(0, distance, mask)
+    moving.finish()
+    spread.others(0)
+    spread.copies.finish()
     copies.finish()
 
 
-def reduce_weights(ndp, nseq, lefts, rights, number):
+def reduce_weights(ndp, nseq, lefts, rights, values):
     blocks = ndp * nseq
-    kinds = [(k, r.shape[1], (r if k is None else lefts[k].T).shape[0] // blocks) for k, r in rights]
-    count, evens = len(rights), ndp // 2
+    kinds = [
+        (k, r.shape[-1], r.shape[1] if k == -1 else (r if k is None else lefts[k]).shape[0] // blocks)
+        for k, r in rights
+    ]
+    count = len(rights)
     vmem = pl.BlockSpec(memory_space=pltpu.VMEM)
     dma = pltpu.SemaphoreType.DMA
-    low = functools.partial(pltpu.VMEM, dtype=bf16)
-
-    def buffers(*lead):
-        return [low((nseq, *lead, rows, width)) for _, width, rows in kinds]
-
+    first_rows, first_width = kinds[0][2], kinds[0][1]
+    scratch = []
+    for left, width, rows in kinds:
+        if left != -1:
+            scratch += sum(dp_sum_shapes(ndp, nseq, rows, width, left is not None), [])
+    for _ in range(3):
+        scratch += [pltpu.VMEM((nseq, rows, width), bf16) for _, width, rows in kinds]
+    moves = len(values)
+    scratch += [pltpu.VMEM(value.shape, value.dtype) for value in values]
     return pl.pallas_call(
-        functools.partial(reduce_kernel, ndp, nseq, kinds),
-        out_shape=[jax.ShapeDtypeStruct((rows, width), f32) for _, width, rows in kinds],
-        in_specs=[vmem] * (len(lefts) + count),
+        functools.partial(reduce_kernel, ndp, nseq, kinds, moves),
+        out_shape=[jax.ShapeDtypeStruct((first_rows * blocks, first_width), bf16)]
+        + [jax.ShapeDtypeStruct((rows, width), f32) for _, width, rows in kinds[1:]]
+        + [regrouped(value) for value in values],
+        in_specs=[vmem] * (len(lefts) + count + moves),
+        out_specs=[vmem] * (count + moves),
+        scratch_shapes=[
+            *scratch,
+            pltpu.VMEM((max(kind[2] for kind in kinds), max(kind[1] for kind in kinds)), f32),
+            pltpu.VMEM((first_rows, first_width), bf16),
+            dma((count, nseq)), dma((count, nseq)), dma((count, nseq)),
+            dma((1, 2 * nseq - 1, ndp)), dma((1, 2 * nseq - 1, ndp)),
+            dma((max(moves, 1), ndp)), dma((max(moves, 1), ndp)),
+        ],
+        compiler_params=pltpu.CompilerParams(
+            collective_id=4, has_side_effects=True, vmem_limit_bytes=VMEM_LIMIT
+        ),
+        cost_estimate=cost(3),
+        name="reduce_weights",
+    )(*lefts, *[r for _, r in rights], *values)
+
+
+class Regroup:
+    def __init__(self, ndp, sources, held, outs, send, recv):
+        self.ndp, self.sources, self.held, self.outs, self.send, self.recv = ndp, sources, held, outs, send, recv
+        self.dp, self.z, self.mp = (lax.axis_index(a) for a in ("dp", "seq", "mp"))
+        self.all = [(k, mask) for k in range(len(sources)) for mask in range(1, ndp)]
+
+    def copy(self, k, mask):
+        return pltpu.make_async_remote_copy(
+            src_ref=self.sources[k].at[flip(self.dp, mask)], dst_ref=self.held[k].at[mask],
+            send_sem=self.send.at[k, mask], recv_sem=self.recv.at[k, mask],
+            device_id=(flip(self.dp, mask), self.z, self.mp), device_id_type=MESH,
+        )
+
+    def place(self, k, mask, value):
+        width = value.shape[1]
+        cols = pl.ds(pl.multiple_of(flip(self.dp, mask) * width, LANES), width)
+        self.outs[k][:, cols] = value.astype(f32)
+
+    def start(self):
+        for item in self.all:
+            self.copy(*item).start()
+
+    def finish(self):
+        for k, source in enumerate(self.sources):
+            self.place(k, 0, source[self.dp])
+        for k, mask in self.all:
+            self.copy(k, mask).wait_recv()
+            self.place(k, mask, self.held[k][mask])
+        for item in self.all:
+            self.copy(*item).wait_send()
+
+
+def regroup_kernel(ndp, count, *refs):
+    barrier = pltpu.get_barrier_semaphore()
+    dp, z, mp = (lax.axis_index(a) for a in ("dp", "seq", "mp"))
+    for mask in range(1, ndp):
+        pl.semaphore_signal(barrier, inc=1, device_id=(flip(dp, mask), z, mp), device_id_type=MESH)
+    pl.semaphore_wait(barrier, ndp - 1)
+    moving = Regroup(ndp, refs[:count], refs[2 * count : 3 * count], refs[count : 2 * count], *refs[3 * count :])
+    moving.start()
+    moving.finish()
+
+
+def regroup_plain(value):
+    return lax.all_to_all(value, "dp", 0, 2, tiled=True)[0].astype(f32)
+
+
+def regrouped(value):
+    ndp, rows, width = value.shape
+    return jax.ShapeDtypeStruct((rows, ndp * width), f32)
+
+
+def regroup(ndp, values):
+    if any(value.shape[2] % LANES for value in values):
+        return [regroup_plain(value) for value in values]
+    count = len(values)
+    vmem = pl.BlockSpec(memory_space=pltpu.VMEM)
+    dma = pltpu.SemaphoreType.DMA
+    return pl.pallas_call(
+        functools.partial(regroup_kernel, ndp, count),
+        out_shape=[regrouped(value) for value in values],
+        in_specs=[vmem] * count,
         out_specs=[vmem] * count,
         scratch_shapes=[
-            *buffers(evens), *buffers(evens), *buffers(evens - 1), *buffers(evens - 1),
-            *buffers(), *buffers(), *buffers(),
-            pltpu.VMEM((max(kind[2] for kind in kinds), max(kind[1] for kind in kinds)), f32),
-            dma((2, count, nseq, evens)), dma((2, count, nseq, evens)),
-            dma((count, nseq)), dma((count, nseq)), dma((count, nseq)),
+            *[pltpu.VMEM(v.shape, v.dtype) for v in values], dma((count, ndp)), dma((count, ndp)),
         ],
         compiler_params=pltpu.CompilerParams(
-            collective_id=number, has_side_effects=True, vmem_limit_bytes=VMEM_LIMIT
+            collective_id=8, has_side_effects=True, vmem_limit_bytes=VMEM_LIMIT
         ),
-        cost_estimate=cost(100),
-        name="reduce_weights",
-    )(*[left.T for left in lefts], *[r for _, r in rights])
+        cost_estimate=cost(3),
+        name="regroup",
+    )(*values)
 
 
 PART = 64
@@ -1005,18 +1227,22 @@
         compiler_params=pltpu.CompilerParams(
             collective_id=6, has_side_effects=True, vmem_limit_bytes=VMEM_LIMIT
         ),
-        cost_estimate=cost(65),
+        cost_estimate=cost(3),
         name="enter_mlp",
     )(mixed, all_out, tokens, gain, *cots)
 
 
 def leave_kernel(
     ndp, cots_ref, to_gate_ref, to_up_ref, mixed_ref, gate_up_ref, down_ref, middle_ref, gain_ref,
-    grads_ref, out_ref, grad_ref, low_ref, gain_out_ref,
+    grad_gate_ref, grad_up_ref, *refs,
+):
+    out_refs, refs = refs[: ndp // 2], refs[ndp // 2 :]
+    (
+        grad_ref, low_ref, gain_out_ref,
     cot_s, to_gate_s, to_up_s, mixed_s, grads_s, out_s, grad_s, load_sem, grads_sem, out_sem, grad_sem,
     keep, core_out, core_in, side_out, side_in, mine, theirs, out_keep, out_core, out_core_in,
     core_sems, side_sems, mp_sems, out_sems,
-):
+    ) = refs
     rows, features = middle_ref.shape
     piece = down_ref.shape[1]
     parts = rows // PART
@@ -1037,11 +1263,16 @@
 
     def store_grads(c):
         slot = lax.rem(c, 2)
-        return pltpu.make_async_copy(grads_s.at[slot], grads_ref.at[:, at(c)], grads_sem.at[slot])
-
-    def store_out(c):
+        return [
+            pltpu.make_async_copy(
+                grads_s.at[slot, :, :, pl.ds(k * piece, piece)], ref.at[:, at(c)], grads_sem.at[slot, k]
+            )
+            for k, ref in enumerate((grad_gate_ref, grad_up_ref))
+        ]
+
+    def store_out(c, k):
         slot = lax.rem(c, 2)
-        return pltpu.make_async_copy(out_s.at[slot], out_ref.at[:, at(c)], out_sem.at[slot])
+        return pltpu.make_async_copy(out_s.at[slot, k], out_refs[k].at[at(c)], out_sem.at[slot, k])
 
     def store_grad(c):
         slot = lax.rem(c, 2)
@@ -1083,7 +1314,8 @@
 
         @pl.when(c >= 2)
         def _():
-            store_grads(c - 2).wait()
+            for copy in store_grads(c - 2):
+                copy.wait()
             to_core(c - 2).wait_send()
             out_to_core(c - 2).wait_send()
 
@@ -1091,7 +1323,8 @@
         grad_mixed = matmul(cot_s[slot].reshape(ndp * PART, features), down_ref[...]).reshape(ndp, PART, piece)
         grads_s[slot, :, :, :piece] = (grad_mixed * to_gate_s[slot].astype(f32)).astype(bf16)
         grads_s[slot, :, :, piece:] = (grad_mixed * to_up_s[slot].astype(f32)).astype(bf16)
-        store_grads(c).start()
+        for copy in store_grads(c):
+            copy.start()
         total = contract(grads_s[slot].reshape(ndp * PART, 2 * piece), gate_up_ref[...])
         total = total.reshape(ndp, PART, features)
         for mask in range(0, ndp, 2):
@@ -1121,13 +1354,14 @@
 
         @pl.when(c >= 2)
         def _():
-            store_out(c - 2).wait()
+            for k in range(ndp // 2):
+                store_out(c - 2, k).wait()
 
         slot = lax.rem(c, 2)
         out_to_core(c).wait_recv()
         for k in range(ndp // 2):
             out_s[slot, k] = (out_keep[slot, k] + out_core_in[c, k].astype(f32)).astype(bf16)
-        store_out(c).start()
+            store_out(c, k).start()
 
     def after_side(c):
         total = keep[lax.rem(c, 4), 0]
@@ -1164,8 +1398,10 @@
 
     lax.fori_loop(0, parts + 4, turn, 0)
     for c in (parts - 2, parts - 1):
-        store_grads(c).wait()
-        store_out(c).wait()
+        for copy in store_grads(c):
+            copy.wait()
+        for k in range(ndp // 2):
+            store_out(c, k).wait()
         store_grad(c).wait()
         to_core(c).wait_send()
         out_to_core(c).wait_send()
@@ -1190,14 +1426,14 @@
     return pl.pallas_call(
         functools.partial(leave_kernel, ndp),
         out_shape=(
-            jax.ShapeDtypeStruct((ndp, rows, 2 * piece), bf16),
-            jax.ShapeDtypeStruct((evens, rows, features), bf16),
+            *[jax.ShapeDtypeStruct((ndp, rows, piece), bf16)] * 2,
+            *[jax.ShapeDtypeStruct((rows, features), bf16)] * evens,
             jax.ShapeDtypeStruct((rows, features), f32),
             jax.ShapeDtypeStruct((rows, features), bf16),
             jax.ShapeDtypeStruct((8, features), f32),
         ),
         in_specs=[anywhere] * 4 + [vmem] * 4,
-        out_specs=(anywhere, anywhere, anywhere, vmem, vmem),
+        out_specs=(*[anywhere] * (3 + evens), vmem, vmem),
         scratch_shapes=[
             low((2, ndp, PART, features)),
             pltpu.VMEM((2, ndp, PART, piece), to_gate.dtype),
@@ -1206,7 +1442,7 @@
             low((2, ndp, PART, 2 * piece)),
             low((2, evens, PART, features)),
             pltpu.VMEM((2, PART, features), f32),
-            dma((4, 2)), dma((2,)), dma((2,)), dma((2,)),
+            dma((4, 2)), dma((2, 2)), dma((2, evens)), dma((2,)),
             pltpu.VMEM((4, evens, PART, features), f32),
             low((2, evens, PART, features)), low((parts, evens, PART, features)),
             low((parts, evens - 1, PART, features)), low((parts, evens - 1, PART, features)),
@@ -1218,7 +1454,7 @@
         compiler_params=pltpu.CompilerParams(
             collective_id=7, has_side_effects=True, vmem_limit_bytes=VMEM_LIMIT
         ),
-        cost_estimate=cost(75),
+        cost_estimate=cost(3),
         name="leave_mlp",
     )(cots, to_gate, to_up, mixed, gate_up, down, middle, gain)
 
@@ -1232,17 +1468,19 @@
 
 
 def side_sum(ndp, value):
-    return (value[0::2].astype(f32) + xor_permute(value[1::2], "dp", 1).astype(f32)).astype(bf16)
-
-
-def halving(ndp, value, after=None):
+    return list((value[0::2].astype(f32) + xor_permute(value[1::2], "dp", 1).astype(f32)).astype(bf16))
+
+
+def halving(ndp, values, after=None):
     for bit in doubling(ndp)[0]:
-        half = value.shape[0] // 2
-        other = xor_permute(value[half:], "dp", bit)
+        half = len(values) // 2
+        others = [xor_permute(value, "dp", bit) for value in values[half:]]
         if after is not None:
-            other, _ = lax.optimization_barrier((other, after))
-        value = (value[:half].astype(f32) + other.astype(f32)).astype(bf16)
-    return value[0]
+            others, _ = lax.optimization_barrier((others, after))
+        values = [
+            (value.astype(f32) + other.astype(f32)).astype(bf16) for value, other in zip(values[:half], others)
+        ]
+    return values[0]
 
 
 def enter_mlp_plain(ndp, mixed, all_out, tokens, gain, cots):
@@ -1269,7 +1507,7 @@
     )
     out = contract(mixed.reshape(-1, piece), down).astype(bf16).reshape(ndp, rows, features)
     gain_out = jnp.sum((grad * normed).reshape(rows // 8, 8, features), axis=0)
-    return grads, side_sum(ndp, out), grad_middle, grad_middle.astype(bf16), gain_out
+    return grads[..., :piece], grads[..., piece:], *side_sum(ndp, out), grad_middle, grad_middle.astype(bf16), gain_out
 
 
 def on_device(
@@ -1293,15 +1531,11 @@
     def flat(value):
         return value.reshape(-1, value.shape[-1])
 
-    def gather_mlp(value):
-        value = value.reshape(ndp, rows_here, -1)
-        return lax.all_gather(value, "seq", axis=1, tiled=True).reshape(features, -1)
-
-    all_y, all_x, all_out, gate_rows, up_rows, down_rows = gather_weights(
-        ndp, nseq, [w_y, w_x, w_out], [False, True, False], [w_gate, w_up, w_down], 3
+    (all_y, all_x, all_out), gate_up_rows, all_down, acts_one, acts_one_t = gather_weights(
+        ndp, nseq, tokens, norm_gain[None], [w_y, w_x, w_out], [w_gate, w_up, w_down]
     )
-    gate_up = gather_mlp(jnp.concatenate([gate_rows, up_rows], axis=1))
-    all_down = gather_mlp(down_rows)
+    gate_up = lax.all_gather(gate_up_rows.reshape(ndp, rows_here, -1), "seq", axis=1, tiled=True)
+    gate_up = gate_up.reshape(features, -1)
 
     position = lax.axis_index("seq") * local_len + jnp.arange(local_len + PAD, dtype=jnp.int32)
     lengths_row = doc_lengths[0]
@@ -1316,9 +1550,6 @@
         [conv_w, conv_b[None], bias_a[None], bias_i[None], jax.nn.softplus(-decay_param)[None]], axis=0
     )
 
-    resid = tokens.astype(f32)
-    scale_one = norm_scale(resid)
-    acts_one = (resid * scale_one * norm_gain).astype(bf16)
     cots_ready, _ = lax.optimization_barrier((cotangent, all_y))
     mixed_rec, states, pxe, pre_y, rate, ig, conv_out = rec_forward(
         nseq, acts_one, all_x, all_y, marks, gate_a, gate_i, vectors
@@ -1342,20 +1573,28 @@
     def reduce_mlp(total):
         return lax.psum_scatter(total, "seq", scatter_dimension=1, tiled=True)
 
-    sum_down = reduce_mlp(rows_total(cots_flat, mixed))
-    grads, out_sides, grad_middle, grad_middle_low, gain_two = (leave_mlp if small_group else leave_mlp_plain)(
+    total_down, mixed = lax.optimization_barrier((rows_total(cots_flat, mixed), mixed))
+    sum_down = reduce_mlp(total_down)
+    grad_gate, grad_up, *out_sides, grad_middle, grad_middle_low, gain_two = (leave_mlp if small_group else leave_mlp_plain)(
         ndp, cots, to_gate, to_up, mixed.reshape(ndp, local_len, piece), gate_up, all_down, middle, mlp_gain[None]
     )
-    total_gate_up, grad_middle_low = lax.optimization_barrier((rows_total(acts_flat, flat(grads)), grad_middle_low))
-    sum_gate_up = reduce_mlp(total_gate_up)
-
-    grad_pre_y, grad_pre_x, grad_gate_a, grad_gate_i, sums = rec_backward(
-        nseq, grad_middle_low, all_out, marks, gate_a, gate_i, vectors, (pre_y, states, rate, pxe, ig, conv_out)
+    total_gate = rows_total(acts_flat, flat(grad_gate))
+    total_up = rows_total(acts_flat, flat(grad_up))
+    total_gate, total_up, grad_middle_low, sum_down = lax.optimization_barrier(
+        (total_gate, total_up, grad_middle_low, sum_down)
+    )
+    sum_gate, sum_up = reduce_mlp(total_gate), reduce_mlp(total_up)
+
+    grad_pre_y, grad_pre_x, grad_gate_a, grad_gate_i, sums, grad_w_out = rec_backward(
+        ndp, nseq, grad_middle_low, mixed_rec, all_out, marks, gate_a, gate_i, vectors,
+        (pre_y, states, rate, pxe, ig, conv_out),
     )
     part = (contract(grad_pre_y, all_y) + contract(grad_pre_x, all_x)).astype(bf16)
     other = xor_permute(part, "mp", 1)
     out_part = halving(ndp, out_sides, grad_pre_y)
     other_out = xor_permute(out_part, "mp", 1)
+    resid = tokens.astype(f32)
+    scale_one = norm_scale(resid)
     normed = resid * scale_one
     small = [
         grad_gate_a, grad_gate_i, sums, jnp.sum(part.astype(f32) * normed, axis=0), jnp.sum(gain_two, axis=0),
@@ -1365,12 +1604,11 @@
     small_rows = jnp.concatenate(
         [value.reshape(-1, block) for value in small] + [jnp.zeros((total_rows - sum(sizes), block), f32)], axis=0
     )
-    small_sum, grad_w_y, grad_w_x, grad_w_out = reduce_weights(
-        ndp, nseq, [acts_one, grad_middle_low],
-        [(None, small_rows), (0, grad_pre_y), (0, grad_pre_x), (1, mixed_rec)], 4,
+    moved = [] if piece % LANES else [sum_gate, sum_down]
+    small_all, grad_w_y, grad_w_x, grad_w_out, *moved = reduce_weights(
+        ndp, nseq, [acts_one_t], [(None, small_rows), (0, grad_pre_y), (0, grad_pre_x), (-1, grad_w_out)], moved
     )
-    small_sum, sum_gate_up, other, other_out = lax.optimization_barrier((small_sum, sum_gate_up, other, other_out))
-    (small_all,) = gather_weights(ndp, nseq, [small_sum.astype(bf16)], [False], [], 5)
+    small_all, sum_up, other, other_out = lax.optimization_barrier((small_all, sum_up, other, other_out))
     totals, begin = [], 0
     for value, size in zip(small, sizes):
         totals.append(small_all[begin : begin + size].astype(f32).reshape(value.shape))
@@ -1386,11 +1624,8 @@
 
     output = (middle + (out_part.astype(f32) + other_out.astype(f32))).astype(bf16)
 
-    def regroup(value):
-        return lax.all_to_all(value, "dp", 0, 2, tiled=True)[0].astype(f32)
-
-    grad_w_down = regroup(sum_down)
-    grad_w_gate, grad_w_up = regroup(sum_gate_up[:, :, :piece]), regroup(sum_gate_up[:, :, piece:])
+    grad_w_gate, grad_w_down = moved or [regroup_plain(sum_gate), regroup_plain(sum_down)]
+    (grad_w_up,) = regroup(ndp, [sum_up])
     return (
         output,
         input_grad,

time: 670 us -> 657 us (0.981)
  Pallas kernels: 453 us -> 511 us
  local copies, waits for them, and re-layouts: 48.1 us -> 23.4 us
  waiting for transfers between devices: 33.5 us -> 10.9 us
  starting transfers between devices: 16.9 us -> 6.13 us
    pallas_call x5, Pallas kernels: 351 us -> 410 us  [the longest x1 129 us: gather_weights(): pl.pallas_call(functools.partial(gather_kernel, ndp, nseq, count, joined)...]
    all_gather x2 -> x1, waiting for transfers between devices: 33.2 us -> 0.22 us  [on_device(): lax.all_gather(gate_up_rows.reshape(ndp, rows_here, -1), 'seq', axis=1, t...]
    ppermute x5, waiting for transfers between devices: 0.01 us -> 10.6 us  [xor_permute(): lax.ppermute(value, axis, [(source, source ^ bit) for source in range(cou...]
    all_to_all x3 -> x0, starting transfers between devices: 10.5 us -> none  [regroup(): return lax.all_to_all(value, 'dp', 0, 2, tiled=True)[0].astype(f32)]
    dot_general x2, matrix products: 16.7 us -> 9.1 us  [contract(): lax.dot_general(left, right, (((1,), (1,)), ((), ())), preferred_element_...]
    convert_element_type x4 -> x0, local copies, waits for them, and re-layouts: 7.12 us -> none  [the longest x1 4.07 us: on_device(): acts_one = (resid * scale_one * norm_gain).astype(bf16)]
    unnamed x67 -> x59, local copies, waits for them, and re-layouts: 21.1 us -> 16.9 us
    dot_general x2 -> x3, matrix products: 27.7 us -> 30.5 us  [contract_rows(): lax.dot_general(left, right, (((0,), (0,)), ((), ())), preferred_element_...]
  transfers between devices with their start and end apart: 12 -> 9, of which waited for: 2 -> 2; matrix products, arithmetic and copies ran while one was open for 20% -> 10% of each run, Pallas kernels for 51% -> 58%
where the time goes in v3:
time: 657 us; the launch traced here: 653 us
  Pallas kernels  511 us (78%)
  matrix products  57 us (9%)
  other arithmetic  30.3 us (5%)
  local copies, waits for them, and re-layouts  23.4 us (4%)
  between operations  14.4 us (2%)
  waiting for transfers between devices  10.9 us (2%)
    pallas_call x1, Pallas kernels, gather_weights(): pl.pallas_call(functools.partial(gather_kernel, ndp, nseq, count, joined)...  129 us
    pallas_call x1, Pallas kernels, reduce_weights(): pl.pallas_call(functools.partial(reduce_kernel, ndp, nseq, kinds, moves),...  115 us
    pallas_call x1, Pallas kernels, leave_mlp(): pl.pallas_call(functools.partial(leave_kernel, ndp), out_shape=(*[jax.Sha...  77 us
    pallas_call x1, Pallas kernels, rec_backward(): pl.pallas_call(functools.partial(rec_backward_kernel, ndp, nseq, heads, b...  76.1 us
    pallas_call x1, Pallas kernels, enter_mlp(): pl.pallas_call(functools.partial(enter_kernel, ndp), out_shape=(jax.Shape...  66.8 us
    pallas_call x1, Pallas kernels, rec_forward(): pl.pallas_call(functools.partial(rec_forward_kernel, nseq, heads, block),...  34 us
    dot_general x3, matrix products, contract_rows(): lax.dot_general(left, right, (((0,), (0,)), ((), ())), preferred_element_...  30.5 us
    dot_general x1, matrix products, matmul(): return jnp.dot(left, right, preferred_element_type=f32)  17.4 us
  transfers between devices with their start and end apart: 9, of which 2 were waited for; matrix products, arithmetic and copies ran while one was open for 10% of the time, Pallas kernels for 58%

profile of v3, /device:TPU:0, one launch (start us, length us, event | category | flops | bytes accessed | tf_op | source)
XLA Modules:
  0.0 653.3 jit_solution(5988437478413980484)
XLA Ops:
  7.3 129.2 %gather_weights.1 = (bf16[2048,1280]{1,0:T(8,128)(2,1)}, bf16[2048,1280]{1,0:T(8,128)(2,1)}, bf16[2048,1280]{1,0:T(8,128)(2,1)}, bf16[512,1536]{1,0:T(8,128)(2,1...) custom-call(bf16[512,2048]{1,0:T(8,128)(2,1)} %tokens_ref.3, ...), custom_call_target="tpu_custom_call" | custom-call | flops 3000000000 | bytes 300000 | tf_op jit(solution)/shard_map/gather_weights/pallas_call | solution.py:763
  140.2 34.0 %rec_forward.1 = (bf16[512,1280]{1,0:T(8,128)(2,1)}, f32[520,1280]{1,0:T(8,128)}, f32[520,1280]{1,0:T(8,128)}, f32[512,1280]{1,0:T(8,128)}, f32[512,1280]{1,0:T(...) custom-call(bf16[512,2048]{1,0:T(8,128)(2,1)} %get-tuple-element.65.acts_ref, ...), custom_call_target="tpu_custom_call" | custom-call | flops 3000000000 | bytes 300000 | tf_op jit(solution)/shard_map/rec_forward/pallas_call | solution.py:250
  174.2 10.6 %collective-permute-done.refs_1_ = bf16[512,2048]{1,0:T(8,128)(2,1)} collective-permute-done((bf16[512,2048]{1,0:T(8,128)(2,1)S(1)}, bf16[512,2048]{1,0:T(8,128)(2,1)}, u32[]{:S(2)}, u32[]{:S(2)}) %collective-permute-start) | collective-permute-done | bytes 2097184 | tf_op jit(solution)/shard_map/ppermute | solution.py:22
  184.8 66.8 %enter_mlp.1 = (f32[512,2048]{1,0:T(8,128)}, bf16[4,512,2048]{2,1,0:T(8,128)(2,1)}, bf16[4,512,2048]{2,1,0:T(8,128)(2,1)}) custom-call(bf16[512,1280]{1,0:T(8,128)(2,1)} %get-tuple-element.68.mixed_ref, bf16[2048,1280]{1,0:T(8,128)(2,1)} %get-tuple-element.69.out_ref, bf16[512,2048]{1,0:T(8,128)(2,1)} %tokens_ref.3, f32[1,2048]{1,0:T(1,128)} %bitcast.63, ...), custom_call_target="tpu_custom_call" | custom-call | flops 3000000000 | bytes 300000 | tf_op jit(solution)/shard_map/enter_mlp/pallas_call | solution.py:1218
  251.8 17.4 %fusion.20 = f32[2048,1536]{1,0:T(8,128)S(1)} fusion(bf16[2048,2048]{1,0:T(8,128)(2,1)} %bitcast.66, bf16[2048,1536]{1,0:T(8,128)(2,1)} %bitcast.47), kind=kOutput, calls=%fused_computation.56 | convolution fusion | flops 12884901888 | bytes 27262976 | tf_op jit(solution)/shard_map/dot_general | solution.py:26
  269.2 7.3 %multiply_convert_fusion = (bf16[2048,768]{1,0:T(8,128)(2,1)S(1)}, f32[2048,768]{1,0:T(8,128)}, f32[2048,768]{1,0:T(8,128)}) fusion(f32[2048,1536]{1,0:T(8,128)S(1)} %fusion.20), kind=kLoop, calls=%fused_computation.11 | loop fusion | flops 33030144 | bytes 28311552 | tf_op jit(solution)/shard_map/convert_element_type | solution.py:1567
  276.5 8.5 %convolution_convert_fusion = bf16[2048,768]{1,0:T(8,128)(2,1)} fusion(bf16[2048,2048]{1,0:T(8,128)(2,1)S(1)} %bitcast.46, bf16[2048,768]{1,0:T(8,128)(2,1)S(1)} %get-tuple-element.75), kind=kOutput, calls=%fused_computation.30 | convolution fusion | flops 6444023808 | bytes 14680064 | tf_op jit(solution)/shard_map/dot_general | solution.py:34
  285.2 77.0 %leave_mlp.1 = (bf16[4,512,768]{2,1,0:T(8,128)(2,1)}, bf16[4,512,768]{2,1,0:T(8,128)(2,1)}, bf16[512,2048]{1,0:T(8,128)(2,1)}, bf16[512,2048]{1,0:T(8,128)(2,1)}...) custom-call(bf16[4,512,2048]{2,1,0:T(8,128)(2,1)} %get-tuple-element.72.cots_ref, ...), custom_call_target="tpu_custom_call" | custom-call | flops 3000000000 | bytes 300000 | tf_op jit(solution)/shard_map/leave_mlp/pallas_call | solution.py:1426
  362.2 11.5 %bitcast_convert_fusion = bf16[2048,768]{1,0:T(8,128)(2,1)} fusion(bf16[4,512,2048]{2,1,0:T(8,128)(2,1)} %get-tuple-element.73, bf16[4,512,768]{2,1,0:T(8,128)(2,1)} %get-tuple-element.80), kind=kOutput, calls=%fused_computation.9 | convolution fusion | flops 6444023808 | bytes 14680064 | tf_op jit(solution)/shard_map/dot_general | solution.py:34
  373.8 10.5 %bitcast_convert_fusion.1 = bf16[2048,768]{1,0:T(8,128)(2,1)} fusion(bf16[4,512,2048]{2,1,0:T(8,128)(2,1)} %get-tuple-element.73, bf16[4,512,768]{2,1,0:T(8,128)(2,1)S(1)} %copy-done.17), kind=kOutput, calls=%fused_computation.10 | convolution fusion | flops 6444023808 | bytes 14680064 | tf_op jit(solution)/shard_map/dot_general | solution.py:34
  387.2 76.1 %rec_backward.1 = (bf16[512,1280]{1,0:T(8,128)(2,1)}, bf16[512,1280]{1,0:T(8,128)(2,1)}, f32[5,256,256]{2,1,0:T(8,128)}, f32[5,256,256]{2,1,0:T(8,128)}, f32[8,1...) custom-call(bf16[512,2048]{1,0:T(8,128)(2,1)} %get-tuple-element.83.low_ref, bf16[512,1280]{1,0:T(8,128)(2,1)} %get-tuple-element.68.mixed_ref, ...), custom_call_target="tpu_custom_call" | custom-call | flops 20000000000 | bytes 2000000 | tf_op jit(solution)/shard_map/rec_backward/pallas_call | solution.py:488
  463.4 4.6 add_convert_fusion.2
  469.0 4.9 fusion.21
  474.0 4.2 fusion.12
  479.3 2.5 constant_dynamic-update-slice_fusion.4
  485.4 114.7 %reduce_weights.1 = (bf16[2816,256]{1,0:T(8,128)(2,1)}, f32[128,1280]{1,0:T(8,128)}, f32[128,1280]{1,0:T(8,128)}, f32[128,1280]{1,0:T(8,128)}, f32[128,3072]{1,0:T(8,128)}, /*index=5*/f32[128,3072]{1,0:T(8,128)}) custom-call(bf16[2048,512]{1,0:T(8,128)(2,1)} %get-tuple-element.92.refs_0_, f32[2816,256]{1,0:T(8,128)} %broadcast_dynamic-update-slice_fusion.refs_1_, ...), custom_call_target="tpu_custom_call" | custom-call | flops 3000000000 | bytes 300000 | tf_op jit(solution)/shard_map/reduce_weights/pallas_call | solution.py:995
  600.8 1.4 fusion.18
  602.9 1.7 collective-permute-start.4
  604.6 3.4 fusion.13
  608.0 13.4 %regroup.1 = f32[128,3072]{1,0:T(8,128)} custom-call(bf16[4,128,768]{2,1,0:T(8,128)(2,1)} %reduce-scatter.8.cloned.1.call-done.refs_0_), custom_call_target="tpu_custom_call" | custom-call | flops 3000000000 | bytes 300000 | tf_op jit(solution)/shard_map/regroup/pallas_call | solution.py:1076
  621.5 9.0 %fusion.16 = (f32[512,2048]{1,0:T(8,128)}, bf16[512,2048]{1,0:T(8,128)(2,1)}) fusion(f32[512,2048]{1,0:T(8,128)} %get-tuple-element.104, bf16[512,2048]{1,0:T(8,128)(2,1)S(1)} %copy-done, bf16[512,2048]{1,0:T(8,128)(2,1)} %collective-permute-done.2, bf16[512,2048]{1,0:T(8,128)(2,1)} %get-tuple-element.128, f32[512]{0:T(512)S(1)} %broadcast_multiply_fusion, ...), kind=kLoop, calls=%fused_computation.25 | loop fusion | flops 15728640 | bytes 25178112 | tf_op jit(solution)/shard_map/add | solution.py:1621
  637.1 2.0 copy.54
  639.1 2.1 copy.55
  641.2 2.0 copy.56
  (113 shorter events, 24.3 us)
Async XLA Ops:
  7.2 244.6 %all-gather.2.cloned.1.call-start = ((), (), s32[]{:S(2)}) async-start(), calls=%async_computation.3 | async-start | bytes 7864320 | tf_op jit(solution)/shard_map/all_gather | solution.py:1537
  7.2 129.4 %copy-start.3 = (bf16[512,2048]{1,0:T(8,128)(2,1)S(1)}, bf16[512,2048]{1,0:T(8,128)(2,1)}, u32[]{:S(2)}) copy-start(bf16[512,2048]{1,0:T(8,128)(2,1)} %refs_0_.2) | copy-start | bytes 6291460
  7.3 130.4 %copy-start.18 = (s32[1,4]{1,0:T(1,128)S(1)}, s32[1,4]{1,0:T(1,128)}, u32[]{:S(2)}) copy-start(s32[1,4]{1,0:T(1,128)} %param.19) | copy-start | bytes 52
  7.3 130.7 %copy-start.11 = (f32[1280]{0:T(1024)S(1)}, f32[1280]{0:T(1024)}, u32[]{:S(2)}) copy-start(f32[1280]{0:T(1024)} %param.29) | copy-start | bytes 15364
  7.3 130.7 %copy-start.14 = (f32[1280]{0:T(1024)S(1)}, f32[1280]{0:T(1024)}, u32[]{:S(2)}) copy-start(f32[1280]{0:T(1024)} %param.28) | copy-start | bytes 15364
  7.3 130.8 %copy-start.15 = (f32[1280]{0:T(1024)S(1)}, f32[1280]{0:T(1024)}, u32[]{:S(2)}) copy-start(f32[1280]{0:T(1024)} %param.25) | copy-start | bytes 15364
  7.3 130.8 %copy-start.16 = (f32[1280]{0:T(1024)S(1)}, f32[1280]{0:T(1024)}, u32[]{:S(2)}) copy-start(f32[1280]{0:T(1024)} %param.26) | copy-start | bytes 15364
  7.3 130.8 %copy-start.13 = (f32[4,1280]{1,0:T(4,128)S(1)}, f32[4,1280]{1,0:T(4,128)}, u32[]{:S(2)}) copy-start(f32[4,1280]{1,0:T(4,128)} %param.27) | copy-start | bytes 61444
  136.6 247.7 %reduce-scatter.4.cloned.1.call-start = ((), (), s32[]{:S(2)}) async-start(), calls=%async_computation.4 | async-start | bytes 3932160 | tf_op jit(solution)/shard_map/reduce_scatter | solution.py:1574
  136.6 48.2 %collective-permute-start = (bf16[512,2048]{1,0:T(8,128)(2,1)S(1)}, bf16[512,2048]{1,0:T(8,128)(2,1)}, u32[]{:S(2)}, u32[]{:S(2)}) collective-permute-start(bf16[512,2048]{1,0:T(8,128)(2,1)S(1)} %copy-done.3), channel_id=1, source_target_pairs={{0,16},{8,24},{16,0},{24,8},{1,17},{9,25},{17,1},{25,9},{2,18},{10... | collective-permute-start | bytes 6291464 | tf_op jit(solution)/shard_map/ppermute | solution.py:22
  276.5 8.5 %copy-start.1 = (bf16[2048,768]{1,0:T(8,128)(2,1)}, bf16[2048,768]{1,0:T(8,128)(2,1)S(1)}, u32[]{:S(2)}) copy-start(bf16[2048,768]{1,0:T(8,128)(2,1)S(1)} %get-tuple-element.75) | copy-start | bytes 9437188
  285.0 200.4 %reduce-scatter.6.cloned.1.call-start = ((), (), s32[]{:S(2)}) async-start(), calls=%async_computation.5 | async-start | bytes 3932160 | tf_op jit(solution)/shard_map/reduce_scatter | solution.py:1574
  362.2 11.5 %copy-start.17 = (bf16[4,512,768]{2,1,0:T(8,128)(2,1)S(1)}, bf16[4,512,768]{2,1,0:T(8,128)(2,1)}, u32[]{:S(2)}) copy-start(bf16[4,512,768]{2,1,0:T(8,128)(2,1)} %get-tuple-element.79) | copy-start | bytes 9437188
  384.3 215.9 %reduce-scatter.8.cloned.1.call-start = ((), (), s32[]{:S(2)}) async-start(), calls=%async_computation.6 | async-start | bytes 3932160 | tf_op jit(solution)/shard_map/reduce_scatter | solution.py:1574
  386.3 77.0 %collective-permute-start.1 = (bf16[512,2048]{1,0:T(8,128)(2,1)}, bf16[512,2048]{1,0:T(8,128)(2,1)}, u32[]{:S(2)}, u32[]{:S(2)}) collective-permute-start(bf16[512,2048]{1,0:T(8,128)(2,1)} %get-tuple-element.78), channel_id=1, source_target_pairs={{0,16},{8,24},{16,0},{24,8},{1,17},{9,25},{17,1},{25,9},{2,18},{10... | collective-permute-start | bytes 6291464 | tf_op jit(solution)/shard_map/ppermute | solution.py:22
  463.3 10.6 %slice-start = ((s8[5242880]{0:T(1024)(128)(4,1)}), s8[4194304]{0:T(1024)(128)(4,1)S(1)}, s32[]{:S(2)}) async-start(s8[5242880]{0:T(1024)(128)(4,1)} %bitcast.49), calls=%async_computation.7 | async-start | bytes 8388608
  468.0 132.1 %collective-permute-start.3 = (bf16[512,2048]{1,0:T(8,128)(2,1)}, bf16[512,2048]{1,0:T(8,128)(2,1)}, u32[]{:S(2)}, u32[]{:S(2)}) collective-permute-start(bf16[512,2048]{1,0:T(8,128)(2,1)} %add_convert_fusion.2), channel_id=1, source_target_pairs={{0,1},{1,0},{2,3},{3,2},{4,5},{5,4},{6,7},{7,6},{8,9},{9,8},{10,11... | collective-permute-start | bytes 6291464 | tf_op jit(solution)/shard_map/ppermute | solution.py:22
  474.0 7.7 %copy-start.7 = (f32[5,256,256]{2,1,0:T(8,128)S(1)}, f32[5,256,256]{2,1,0:T(8,128)}, u32[]{:S(2)}) copy-start(f32[5,256,256]{2,1,0:T(8,128)} %get-tuple-element.94) | copy-start | bytes 3932164
  478.2 121.9 %collective-permute-start.2 = (bf16[512,2048]{1,0:T(8,128)(2,1)}, bf16[512,2048]{1,0:T(8,128)(2,1)}, u32[]{:S(2)}, u32[]{:S(2)}) collective-permute-start(bf16[512,2048]{1,0:T(8,128)(2,1)} %get-tuple-element.128), channel_id=1, source_target_pairs={{0,1},{1,0},{2,3},{3,2},{4,5},{5,4},{6,7},{7,6},{8,9},{9,8},{10,11... | collective-permute-start | bytes 6291464 | tf_op jit(solution)/shard_map/ppermute | solution.py:22
  485.4 119.2 %copy-start.10 = (f32[2048]{0:T(1024)S(1)}, f32[2048]{0:T(1024)}, u32[]{:S(2)}) copy-start(f32[2048]{0:T(1024)} %param.20) | copy-start | bytes 24580
  602.9 33.5 %collective-permute-start.4 = (f32[2048]{0:T(1024)S(1)}, f32[2048]{0:T(1024)S(1)}, u32[]{:S(2)}, u32[]{:S(2)}) collective-permute-start(f32[2048]{0:T(1024)S(1)} %bitcast.61), channel_id=1, source_target_pairs={{0,1},{1,0},{2,3},{3,2},{4,5},{5,4},{6,7},{7,6},{8,9},{9,8},{10,11... | collective-permute-start | bytes 24584 | tf_op jit(solution)/shard_map/ppermute | solution.py:22
  621.5 9.0 %copy-start.12 = (f32[1280]{0:T(1024)S(1)}, f32[1280]{0:T(1024)}, u32[]{:S(2)}) copy-start(f32[1280]{0:T(1024)} %param.29) | copy-start | bytes 15364
  630.5 12.6 %copy-start.5 = (f32[128,3072]{1,0:T(8,128)S(1)}, f32[128,3072]{1,0:T(8,128)}, u32[]{:S(2)}) copy-start(f32[128,3072]{1,0:T(8,128)} %get-tuple-element.162) | copy-start | bytes 4718596
  633.5 10.8 %copy-start.6 = (f32[128,3072]{1,0:T(8,128)S(1)}, f32[128,3072]{1,0:T(8,128)}, u32[]{:S(2)}) copy-start(f32[128,3072]{1,0:T(8,128)} %regroup.1) | copy-start | bytes 4718596
  (8 other events, 43.3 us)
Sparse Core Ops, SparseCore 0:
  136.7 115.0 all-gather.1
  285.1 62.5 reduce-scatter.3
  384.4 64.9 reduce-scatter.5
  451.5 74.2 reduce-scatter.7
